TPU v7x, 32 devices: a whole 2x2x4 slice. The times are simulated.
32 devices in a mesh: seq: 4 (over z), dp: 8 (over y, x, core).
Axes of the slice: x: 2, y: 2, z: 4, core: 2. Of those that a mesh axis runs over, the one named last changes fastest.
Arguments:
- tokens: bfloat16 [8, 1536, 1024], P('dp', 'seq'), may hold values from -6 to 6
- enc_states: bfloat16 [8, 512, 1024], P('dp', 'seq'), may hold values from -6 to 6
- order: int32 [8, 1536], P('dp'), may hold values from 0 to 1535, each once within a row
- lengths: int32 [8, 3], P('dp'), may hold values from 256 to 832, as said below
- enc_lengths: int32 [8, 3], P('dp'), may hold values from 64 to 304, as said below
- attn_in: bfloat16 [1024, 3072], P(None, 'dp'), may hold values from -0.1875 to 0.1875
- attn_out: bfloat16 [1024, 1024], P(None, 'dp'), may hold values from -1.5 to 1.5
- cross_q: bfloat16 [1024, 1024], P(None, 'dp'), may hold values from -0.1875 to 0.1875
- cross_kv: bfloat16 [1024, 2048], P(None, 'dp'), may hold values from -0.1875 to 0.1875
- cross_out: bfloat16 [1024, 1024], P(None, 'dp'), may hold values from -1.5 to 1.5
- ffn_in: bfloat16 [1024, 4096], P(None, 'dp'), may hold values from -0.1875 to 0.1875
- ffn_out: bfloat16 [4096, 1024], P(None, 'dp'), may hold values from -0.09375 to 0.09375
- proj_bias: bfloat16 [7, 1024], P(None, 'dp'), may hold values from -1.5 to 1.5
- gains: bfloat16 [4, 1024], P(None, 'dp'), may hold values from 0.099609375 to 1.8984375
- ln_bias: bfloat16 [4, 1024], P(None, 'dp'), may hold values from -1.5 to 1.5
- ffn_bias: bfloat16 [1, 4096], P(None, 'dp'), may hold values from -1.5 to 1.5
- cotangent: bfloat16 [8, 1536, 1024], P('dp', 'seq'), may hold values from -6 to 6
Outputs:
- output: bfloat16 [8, 1536, 1024], P('dp', 'seq')
- tokens_grad: float32 [8, 1536, 1024], P('dp', 'seq')
- enc_grad: float32 [8, 512, 1024], P('dp', 'seq')
- attn_in_grad: float32 [1024, 3072], P(None, 'dp')
- attn_out_grad: float32 [1024, 1024], P(None, 'dp')
- cross_q_grad: float32 [1024, 1024], P(None, 'dp')
- cross_kv_grad: float32 [1024, 2048], P(None, 'dp')
- cross_out_grad: float32 [1024, 1024], P(None, 'dp')
- ffn_in_grad: float32 [1024, 4096], P(None, 'dp')
- ffn_out_grad: float32 [4096, 1024], P(None, 'dp')
- proj_bias_grad: float32 [7, 1024], P(None, 'dp')
- gains_grad: float32 [4, 1024], P(None, 'dp')
- ln_bias_grad: float32 [4, 1024], P(None, 'dp')
- ffn_bias_grad: float32 [1, 4096], P(None, 'dp')
Inputs may be any that keep to these rules, and one draw needn't show every extreme that they name: Each row is a permutation; row r of a group's 1536 rows of tokens and cotangent is the token at place order[r] when the group's sequences stand end to end in order. lengths of a group's 3 sequences in the order in which they stand end to end; they sum to 1536, and exactly one of them is 832. `enc_lengths`: encoder states of a group's sequences, in the same order, laid end to end in its 512 rows; they sum to 512, and exactly one of them is 304.
All inputs are finite; a program needn't handle non-finite values.
Results may differ from a plain program's by a relative error of at most 0.022.
Values may be sent and summed in bfloat16 or wider, within the bound.
No kernel may reach another device: no remote copies, remote signals or barrier semaphores. Data moves between devices by JAX's collectives and lax.ppermute only.
A program may use at most 192 MiB of HBM per device.

v0:
```python
import jax
import jax.numpy as jnp
from jax import lax
from jax.sharding import PartitionSpec as P

HEADS = 16


EPSILON = 1e-05


def apply_layer_norm(input_tokens, gain, shift):
    center = input_tokens - jnp.mean(input_tokens, axis=-1, keepdims=True)
    inv_dev = lax.rsqrt(jnp.mean(center * center, axis=-1, keepdims=True) + EPSILON)
    normed = center * inv_dev
    return (normed * gain + shift, normed, inv_dev)


def norm_backward_pass(normed, inv_dev, gain, incoming_gradient):
    scaled = incoming_gradient * gain
    back_val = inv_dev * (
        scaled
        - jnp.mean(scaled, axis=-1, keepdims=True)
        - normed * jnp.mean(scaled * normed, axis=-1, keepdims=True)
    )
    return (
        back_val,
        jnp.sum(incoming_gradient * normed, axis=0),
        jnp.sum(incoming_gradient, axis=0),
    )


def smooth_gate(values):
    return jax.nn.gelu(values, approximate=True)


def dense(left, right):
    return jnp.dot(left, right, preferred_element_type=jnp.float32)


def dense_left(left, right):
    return lax.dot_general(
        left, right, (((0,), (0,)), ((), ())), preferred_element_type=jnp.float32
    )


def dense_product_right(left, right):
    return lax.dot_general(
        left, right, (((1,), (1,)), ((), ())), preferred_element_type=jnp.float32
    )


def segment_ids(positions, seq_lengths):
    ends = jnp.cumsum(seq_lengths)
    return jnp.sum((positions[:, None] >= ends[None, :]).astype(jnp.int32), axis=1)


def masked_scores(query_blk, keys_all, mask_blk):
    scale_val = query_blk.shape[-1] ** (-0.5)
    scores = (
        jnp.einsum("qhd,khd->hqk", query_blk, keys_all, preferred_element_type=jnp.float32)
        * scale_val
    )
    return jnp.where(mask_blk[None], scores, -1e30)


def attend_forward(queries, keys_all, values_all, positions, segments, mask_fn):
    row_total = queries.shape[0]
    block_rows = min(512, row_total)
    block_count = row_total // block_rows

    def per_block(pieces):
        query_blk, pos_blk, seg_blk = pieces
        scores = masked_scores(query_blk, keys_all, mask_fn(pos_blk, seg_blk))
        row_peak = jnp.max(scores, axis=-1, keepdims=True)
        row_exp = jnp.exp(scores - row_peak)
        row_sum = jnp.sum(row_exp, axis=-1, keepdims=True)
        probs_low = (row_exp / row_sum).astype(jnp.bfloat16)
        result = jnp.einsum(
            "hqk,khd->qhd", probs_low, values_all, preferred_element_type=jnp.float32
        )
        return (result.astype(jnp.bfloat16), (row_peak + jnp.log(row_sum))[:, :, 0])

    results, log_sums = lax.map(
        per_block,
        (
            queries.reshape((block_count, block_rows) + queries.shape[1:]),
            positions.reshape(block_count, block_rows),
            segments.reshape(block_count, block_rows),
        ),
    )
    return (results.reshape(queries.shape), log_sums)


def attend_backward(
    queries, keys_all, values_all, positions, segments, mask_fn, log_sums, grad_out
):
    row_total = queries.shape[0]
    block_rows = min(512, row_total)
    block_count = row_total // block_rows
    scale_val = queries.shape[-1] ** (-0.5)

    def per_block(carry, pieces):
        key_acc, value_acc = carry
        query_blk, pos_blk, seg_blk, lse_blk, grad_blk = pieces
        scores = masked_scores(query_blk, keys_all, mask_fn(pos_blk, seg_blk))
        probs_full = jnp.exp(scores - lse_blk[:, :, None])
        grad_probs = jnp.einsum(
            "qhd,khd->hqk", grad_blk, values_all, preferred_element_type=jnp.float32
        )
        grad_scores = (
            probs_full * (grad_probs - jnp.sum(probs_full * grad_probs, axis=-1, keepdims=True))
        ).astype(jnp.bfloat16)
        grad_query = (
            jnp.einsum("hqk,khd->qhd", grad_scores, keys_all, preferred_element_type=jnp.float32)
            * scale_val
        ).astype(jnp.bfloat16)
        key_acc = (
            key_acc
            + jnp.einsum("hqk,qhd->khd", grad_scores, query_blk, preferred_element_type=jnp.float32)
            * scale_val
        )
        value_acc = value_acc + jnp.einsum(
            "hqk,qhd->khd",
            probs_full.astype(jnp.bfloat16),
            grad_blk,
            preferred_element_type=jnp.float32,
        )
        return ((key_acc, value_acc), grad_query)

    zero_keys = jnp.zeros(keys_all.shape, jnp.float32)
    carried, grad_blocks = lax.scan(
        per_block,
        (zero_keys, zero_keys),
        (
            queries.reshape((block_count, block_rows) + queries.shape[1:]),
            positions.reshape(block_count, block_rows),
            segments.reshape(block_count, block_rows),
            log_sums,
            grad_out.reshape((block_count, block_rows) + grad_out.shape[1:]),
        ),
    )
    return (
        grad_blocks.reshape(queries.shape),
        carried[0].astype(jnp.bfloat16),
        carried[1].astype(jnp.bfloat16),
    )


def local(
    tokens,
    enc_states,
    order,
    lengths,
    enc_lengths,
    attn_in,
    attn_out,
    cross_q,
    cross_kv,
    cross_out,
    ffn_in,
    ffn_out,
    proj_bias,
    gains,
    ln_bias,
    ffn_bias,
    cotangent,
):
    gathered = (
        lax.all_gather(attn_in, "dp", axis=1, tiled=True),
        lax.all_gather(attn_out, "dp", axis=1, tiled=True),
        lax.all_gather(cross_q, "dp", axis=1, tiled=True),
        lax.all_gather(cross_kv, "dp", axis=1, tiled=True),
        lax.all_gather(cross_out, "dp", axis=1, tiled=True),
        lax.all_gather(ffn_in, "dp", axis=1, tiled=True),
        lax.all_gather(ffn_out, "dp", axis=1, tiled=True),
        lax.all_gather(proj_bias, "dp", axis=1, tiled=True),
        lax.all_gather(gains, "dp", axis=1, tiled=True),
        lax.all_gather(ln_bias, "dp", axis=1, tiled=True),
        lax.all_gather(ffn_bias, "dp", axis=1, tiled=True),
    )
    (
        joint_projection_weight,
        w_out,
        cross_query_weight,
        w_cross_kv,
        w_cross_out,
        up_weight,
        w_down,
        bias_all,
        gain_all,
        shift_all,
        up_bias,
    ) = gathered
    bias_vals = bias_all.astype(jnp.float32)
    gain_entries = gain_all.astype(jnp.float32)
    shift_entries = shift_all.astype(jnp.float32)
    up_bias_vals = up_bias.astype(jnp.float32)
    seq_count = lax.axis_size("seq")
    model_width = w_out.shape[0]
    part_width = model_width // seq_count
    heads_here = HEADS // seq_count
    head_size = model_width // HEADS
    input_tokens = tokens[0].astype(jnp.float32)
    local_rows = input_tokens.shape[0]
    group_rows = local_rows * seq_count
    states = enc_states[0]
    enc_local = states.shape[0]
    enc_rows = enc_local * seq_count
    positions = order[0]
    seg_query = segment_ids(positions, lengths[0])
    seg_enc = segment_ids(jnp.arange(enc_rows, dtype=jnp.int32), enc_lengths[0])
    zero_row = jnp.zeros((model_width,), jnp.float32)

    def self_mask(pos_blk, seg_blk):
        return (seg_blk[:, None] == seg_query[None, :]) & (positions[None, :] <= pos_blk[:, None])

    def cross_mask(pos_blk, seg_blk):
        return seg_blk[:, None] == seg_enc[None, :]

    first_normalized, first_centered_scaled, first_inverse_deviation = apply_layer_norm(
        input_tokens, gain_entries[0], shift_entries[0]
    )
    act_one = first_normalized.astype(jnp.bfloat16)
    qkv_tok = (
        (
            dense(act_one, joint_projection_weight)
            + jnp.concatenate([bias_vals[0], zero_row, bias_vals[1]])
        )
        .astype(jnp.bfloat16)
        .reshape(local_rows, 3, seq_count, part_width)
    )
    kv_tok = (
        (dense(states, w_cross_kv) + jnp.concatenate([zero_row, bias_vals[4]]))
        .astype(jnp.bfloat16)
        .reshape(enc_local, 2, seq_count, part_width)
    )
    qkv_heads, kv_heads = (
        lax.all_to_all(qkv_tok, "seq", split_axis=2, concat_axis=0, tiled=True),
        lax.all_to_all(kv_tok, "seq", split_axis=2, concat_axis=0, tiled=True),
    )
    queries = qkv_heads[:, 0, 0].reshape(group_rows, heads_here, head_size)
    keys_self = qkv_heads[:, 1, 0].reshape(group_rows, heads_here, head_size)
    values_self = qkv_heads[:, 2, 0].reshape(group_rows, heads_here, head_size)
    enc_keys = kv_heads[:, 0, 0].reshape(enc_rows, heads_here, head_size)
    enc_values = kv_heads[:, 1, 0].reshape(enc_rows, heads_here, head_size)
    self_heads, self_lse = attend_forward(
        queries, keys_self, values_self, positions, seg_query, self_mask
    )
    self_tok = lax.all_to_all(
        self_heads.reshape(group_rows, 1, 1, part_width),
        "seq",
        split_axis=0,
        concat_axis=2,
        tiled=True,
    ).reshape(local_rows, model_width)
    first_residual_state = input_tokens + dense(self_tok, w_out) + bias_vals[2]
    second_normalized, second_centered_scaled, second_inverse_deviation = apply_layer_norm(
        first_residual_state, gain_entries[1], shift_entries[1]
    )
    act_two = second_normalized.astype(jnp.bfloat16)
    cross_tok = (
        (dense(act_two, cross_query_weight) + bias_vals[3])
        .astype(jnp.bfloat16)
        .reshape(local_rows, 1, seq_count, part_width)
    )
    cross_queries = lax.all_to_all(
        cross_tok, "seq", split_axis=2, concat_axis=0, tiled=True
    ).reshape(group_rows, heads_here, head_size)
    cross_heads, cross_lse = attend_forward(
        cross_queries, enc_keys, enc_values, positions, seg_query, cross_mask
    )
    cross_res = lax.all_to_all(
        cross_heads.reshape(group_rows, 1, 1, part_width),
        "seq",
        split_axis=0,
        concat_axis=2,
        tiled=True,
    ).reshape(local_rows, model_width)
    second_residual_state = first_residual_state + dense(cross_res, w_cross_out) + bias_vals[5]
    third_normalized, third_centered_scaled, third_inverse_deviation = apply_layer_norm(
        second_residual_state, gain_entries[2], shift_entries[2]
    )
    act_three = third_normalized.astype(jnp.bfloat16)
    up_proj = dense(act_three, up_weight) + up_bias_vals[0]
    gate_value, gate_pullback = jax.vjp(smooth_gate, up_proj)
    gelu_out = gate_value.astype(jnp.bfloat16)
    third_residual_state = second_residual_state + dense(gelu_out, w_down) + bias_vals[6]
    closing_norm, fourth_centered_scaled, fourth_inverse_deviation = apply_layer_norm(
        third_residual_state, gain_entries[3], shift_entries[3]
    )
    output = closing_norm.astype(jnp.bfloat16)[None]
    incoming_gradient = cotangent[0].astype(jnp.float32)
    third_residual_gradient, final_gain, final_shift = norm_backward_pass(
        fourth_centered_scaled, fourth_inverse_deviation, gain_entries[3], incoming_gradient
    )
    grad_down_in = third_residual_gradient.astype(jnp.bfloat16)
    grad_w_down = dense_left(gelu_out, grad_down_in)
    grad_gate = dense_product_right(grad_down_in, w_down)
    up_projection_gradient = gate_pullback(grad_gate)[0].astype(jnp.bfloat16)
    grad_up_bias = jnp.sum(up_projection_gradient, axis=0, dtype=jnp.float32)
    grad_w_up = dense_left(act_three, up_projection_gradient)
    back_three, gain_third, shift_third = norm_backward_pass(
        third_centered_scaled,
        third_inverse_deviation,
        gain_entries[2],
        dense_product_right(up_projection_gradient, up_weight),
    )
    grad_two = third_residual_gradient + back_three
    grad_cross_in = grad_two.astype(jnp.bfloat16)
    grad_w_cross_out = dense_left(cross_res, grad_cross_in)
    grad_cross_tok = (
        dense_product_right(grad_cross_in, w_cross_out)
        .astype(jnp.bfloat16)
        .reshape(local_rows, 1, seq_count, part_width)
    )
    grad_cross_heads = lax.all_to_all(
        grad_cross_tok, "seq", split_axis=2, concat_axis=0, tiled=True
    ).reshape(group_rows, heads_here, head_size)
    grad_cq, grad_ek, grad_ev = attend_backward(
        cross_queries,
        enc_keys,
        enc_values,
        positions,
        seg_query,
        cross_mask,
        cross_lse,
        grad_cross_heads,
    )
    grad_cq_tok, grad_kv_tok = (
        lax.all_to_all(
            grad_cq.reshape(group_rows, 1, 1, part_width),
            "seq",
            split_axis=0,
            concat_axis=2,
            tiled=True,
        ),
        lax.all_to_all(
            jnp.stack([grad_ek, grad_ev], axis=1).reshape(enc_rows, 2, 1, part_width),
            "seq",
            split_axis=0,
            concat_axis=2,
            tiled=True,
        ),
    )
    cross_query_gradient_rows = grad_cq_tok.reshape(local_rows, model_width)
    grad_kv_flat = grad_kv_tok.reshape(enc_local, 2 * model_width)
    grad_w_cross_q = dense_left(act_two, cross_query_gradient_rows)
    grad_w_cross_kv = dense_left(states, grad_kv_flat)
    enc_grad = dense_product_right(grad_kv_flat, w_cross_kv)
    back_two, gain_second, shift_second = norm_backward_pass(
        second_centered_scaled,
        second_inverse_deviation,
        gain_entries[1],
        dense_product_right(cross_query_gradient_rows, cross_query_weight),
    )
    grad_one = grad_two + back_two
    grad_self_in = grad_one.astype(jnp.bfloat16)
    grad_w_out = dense_left(self_tok, grad_self_in)
    grad_self_tok = (
        dense_product_right(grad_self_in, w_out)
        .astype(jnp.bfloat16)
        .reshape(local_rows, 1, seq_count, part_width)
    )
    grad_self_heads = lax.all_to_all(
        grad_self_tok, "seq", split_axis=2, concat_axis=0, tiled=True
    ).reshape(group_rows, heads_here, head_size)
    grad_query, grad_key, grad_value = attend_backward(
        queries, keys_self, values_self, positions, seg_query, self_mask, self_lse, grad_self_heads
    )
    grad_qkv_tok = lax.all_to_all(
        jnp.stack([grad_query, grad_key, grad_value], axis=1).reshape(group_rows, 3, 1, part_width),
        "seq",
        split_axis=0,
        concat_axis=2,
        tiled=True,
    )
    joint_projection_gradient = grad_qkv_tok.reshape(local_rows, 3 * model_width)
    grad_w_qkv = dense_left(act_one, joint_projection_gradient)
    back_one, gain_first, shift_first = norm_backward_pass(
        first_centered_scaled,
        first_inverse_deviation,
        gain_entries[0],
        dense_product_right(joint_projection_gradient, joint_projection_weight),
    )
    tokens_grad = grad_one + back_one
    grad_bias = jnp.stack(
        [
            jnp.sum(joint_projection_gradient[:, :model_width], axis=0, dtype=jnp.float32),
            jnp.sum(joint_projection_gradient[:, 2 * model_width :], axis=0, dtype=jnp.float32),
            jnp.sum(grad_one, axis=0),
            jnp.sum(cross_query_gradient_rows, axis=0, dtype=jnp.float32),
            jnp.sum(grad_kv_flat[:, model_width:], axis=0, dtype=jnp.float32),
            jnp.sum(grad_two, axis=0),
            jnp.sum(third_residual_gradient, axis=0),
        ]
    )
    grad_gain = jnp.stack([gain_first, gain_second, gain_third, final_gain])
    grad_shift = jnp.stack([shift_first, shift_second, shift_third, final_shift])
    all_grads = (
        grad_w_qkv,
        grad_w_out,
        grad_w_cross_q,
        grad_w_cross_kv,
        grad_w_cross_out,
        grad_w_up,
        grad_w_down,
        grad_bias,
        grad_gain,
        grad_shift,
        grad_up_bias[None],
    )
    shares = (
        lax.psum_scatter(all_grads[0], "dp", scatter_dimension=1, tiled=True),
        lax.psum_scatter(all_grads[1], "dp", scatter_dimension=1, tiled=True),
        lax.psum_scatter(all_grads[2], "dp", scatter_dimension=1, tiled=True),
        lax.psum_scatter(all_grads[3], "dp", scatter_dimension=1, tiled=True),
        lax.psum_scatter(all_grads[4], "dp", scatter_dimension=1, tiled=True),
        lax.psum_scatter(all_grads[5], "dp", scatter_dimension=1, tiled=True),
        lax.psum_scatter(all_grads[6], "dp", scatter_dimension=1, tiled=True),
        lax.psum_scatter(all_grads[7], "dp", scatter_dimension=1, tiled=True),
        lax.psum_scatter(all_grads[8], "dp", scatter_dimension=1, tiled=True),
        lax.psum_scatter(all_grads[9], "dp", scatter_dimension=1, tiled=True),
        lax.psum_scatter(all_grads[10], "dp", scatter_dimension=1, tiled=True),
    )
    totals = (
        lax.psum(shares[0].astype(jnp.bfloat16), "seq").astype(jnp.float32),
        lax.psum(shares[1].astype(jnp.bfloat16), "seq").astype(jnp.float32),
        lax.psum(shares[2].astype(jnp.bfloat16), "seq").astype(jnp.float32),
        lax.psum(shares[3].astype(jnp.bfloat16), "seq").astype(jnp.float32),
        lax.psum(shares[4].astype(jnp.bfloat16), "seq").astype(jnp.float32),
        lax.psum(shares[5].astype(jnp.bfloat16), "seq").astype(jnp.float32),
        lax.psum(shares[6].astype(jnp.bfloat16), "seq").astype(jnp.float32),
        lax.psum(shares[7].astype(jnp.bfloat16), "seq").astype(jnp.float32),
        lax.psum(shares[8].astype(jnp.bfloat16), "seq").astype(jnp.float32),
        lax.psum(shares[9].astype(jnp.bfloat16), "seq").astype(jnp.float32),
        lax.psum(shares[10].astype(jnp.bfloat16), "seq").astype(jnp.float32),
    )
    return (
        output,
        tokens_grad[None],
        enc_grad[None],
        totals[0],
        totals[1],
        totals[2],
        totals[3],
        totals[4],
        totals[5],
        totals[6],
        totals[7],
        totals[8],
        totals[9],
        totals[10],
    )


def solution(mesh):
    in_specs = (
        P("dp", "seq", None),
        P("dp", "seq", None),
        P("dp", None),
        P("dp", None),
        P("dp", None),
        P(None, "dp"),
        P(None, "dp"),
        P(None, "dp"),
        P(None, "dp"),
        P(None, "dp"),
        P(None, "dp"),
        P(None, "dp"),
        P(None, "dp"),
        P(None, "dp"),
        P(None, "dp"),
        P(None, "dp"),
        P("dp", "seq", None),
    )
    out_specs = (
        P("dp", "seq", None),
        P("dp", "seq", None),
        P("dp", "seq", None),
        P(None, "dp"),
        P(None, "dp"),
        P(None, "dp"),
        P(None, "dp"),
        P(None, "dp"),
        P(None, "dp"),
        P(None, "dp"),
        P(None, "dp"),
        P(None, "dp"),
        P(None, "dp"),
        P(None, "dp"),
    )
    return jax.shard_map(local, mesh=mesh, in_specs=in_specs, out_specs=out_specs, check_vma=False)
```

profile of v0, /device:TPU:0, one launch (start us, length us, event | category | flops | bytes accessed | tf_op | source)
XLA Modules:
  0.0 1348.8 jit_solution(12867101386150693535)
XLA Ops:
  40.8 18.6 %all-gather.8.cloned.1.call-done = bf16[1024,3072]{1,0:T(8,128)(2,1)} async-done(((bf16[1024,384]{1,0:T(8,128)(2,1)}), bf16[1024,3072]{1,0:T(8,128)(2,1)}) %all-gather.8.cloned.1.call-update) | async-done | bytes 6291472 | tf_op jit(solution)/shard_map/all_gather | solution.py:170
  78.4 53.2 %all-to-all-done = bf16[384,3,4,256]{3,0,1,2:T(8,128)(2,1)S(1)} async-done(((bf16[384,3,4,256]{3,0,1,2:T(8,128)(2,1)}), bf16[384,3,4,256]{3,0,1,2:T(8,128)(2,1)S(1)}, u32[]{:S(2)}, u32[]{:S(2)}) %all-to-all-start) | async-done | bytes 2359328 | tf_op jit(solution)/shard_map/all_to_all | solution.py:239
  140.4 35.9 %while.54 = (s32[]{:T(128)}, bf16[3,512,4,64]{1,3,2,0:T(8,128)(2,1)}, f32[3,4,512]{2,1,0:T(4,128)S(1)}, s32[3,512]{1,0:T(4,128)S(1)}, s32[1536]{0:T(1024)S(1)}, ...) while((s32[]{:T(128)}, ...), condition=%wide.region_7.8_spmd, body=%wide.region_4.0_spmd.sunk | while | flops 845543424 | bytes 43094160 | solution.py:84
  207.3 13.7 %all-to-all-done.1 = bf16[4,2,49152]{2,1,0:T(2,128)(2,1)S(1)} async-done(((bf16[4,2,49152]{2,1,0:T(2,128)(2,1)}), bf16[4,2,49152]{2,1,0:T(2,128)(2,1)S(1)}, u32[]{:S(2)}, u32[]{:S(2)}) %all-to-all-start.1) | async-done | bytes 786464 | tf_op jit(solution)/shard_map/all_to_all | solution.py:250
  245.4 17.7 %all-to-all-done.2 = bf16[384,1,4,256]{0,3,1,2:T(8,128)(2,1)S(1)} async-done(((bf16[384,1,4,256]{0,3,1,2:T(8,128)(2,1)}), bf16[384,1,4,256]{0,3,1,2:T(8,128)(2,1)S(1)}, u32[]{:S(2)}, u32[]{:S(2)}) %all-to-all-start.2) | async-done | bytes 786464 | tf_op jit(solution)/shard_map/all_to_all | solution.py:267
  269.4 12.5 while.55
  366.6 10.8 convert_reduce_fusion
  401.7 14.6 %all-to-all-done.5 = bf16[384,1,4,256]{0,3,1,2:T(8,128)(2,1)} async-done(((bf16[384,1,4,256]{0,3,1,2:T(8,128)(2,1)}), bf16[384,1,4,256]{0,3,1,2:T(8,128)(2,1)}, u32[]{:S(2)}, u32[]{:S(2)}) %all-to-all-start.5) | async-done | bytes 786464 | tf_op jit(solution)/shard_map/all_to_all | solution.py:317
  426.0 22.8 %while.56 = (s32[]{:T(128)}, f32[512,4,64]{0,2,1:T(8,128)S(1)}, f32[512,4,64]{0,2,1:T(8,128)}, bf16[3,512,4,64]{1,3,2,0:T(8,128)(2,1)}, bf16[3,512,4,64]{1,3,2,0...) while((s32[]{:T(128)}, f32[512,4,64]{0,2,1:T(8,128)S(1)}, ...), condition=%wide.region_26.27_spmd.clone, body=%wide.region_24.26_spmd.clone.sunk | while | flops 687994880 | bytes 45154584 | solution.py:132
  468.9 23.1 %all_to_all.156 = bf16[4,2,49152]{2,1,0:T(2,128)(2,1)S(1)} all-to-all(bf16[4,2,49152]{2,1,0:T(2,128)(2,1)} %reshape.518), channel_id=1, replica_groups=mesh['seq'=4,'dp'=8] {'seq'}, dimensions={0} | all-to-all | bytes 1572864 | tf_op jit(solution)/shard_map/all_to_all | solution.py:331
  513.7 16.5 %all_to_all.157 = bf16[512,2,1,256]{3,1,2,0:T(2,128)(2,1)S(1)} all-to-all(bf16[512,2,1,256]{3,1,2,0:T(2,128)(2,1)S(1)} %copy.303), channel_id=1, replica_groups=mesh['seq'=4,'dp'=8] {'seq'}, dimensions={0} | all-to-all | bytes 1048576 | tf_op jit(solution)/shard_map/all_to_all | solution.py:338
  536.5 11.7 fusion.139
  569.3 18.6 %all-to-all-done.7 = bf16[384,1,4,256]{0,3,1,2:T(8,128)(2,1)S(1)} async-done(((bf16[384,1,4,256]{0,3,1,2:T(8,128)(2,1)}), bf16[384,1,4,256]{0,3,1,2:T(8,128)(2,1)S(1)}, u32[]{:S(2)}, u32[]{:S(2)}) %all-to-all-start.7) | async-done | bytes 786464 | tf_op jit(solution)/shard_map/all_to_all | solution.py:365
  594.1 73.2 %while.57 = (s32[]{:T(128)}, f32[1536,4,64]{0,2,1:T(8,128)}, f32[1536,4,64]{0,2,1:T(8,128)}, bf16[3,512,4,64]{1,3,2,0:T(8,128)(2,1)}, bf16[3,512,4,64]{1,3,2,0:T...) while((s32[]{:T(128)}, f32[1536,4,64]{0,2,1:T(8,128)}, ...), condition=%wide.region_31.32_spmd.clone, body=%wide.region_29.31_spmd.clone.sunk | while | flops 2046162944 | bytes 134295824 | solution.py:132
  679.2 73.1 %all_to_all.158 = bf16[1536,3,1,256]{3,1,2,0:T(4,128)(2,1)S(1)} all-to-all(bf16[1536,3,1,256]{3,1,2,0:T(4,128)(2,1)S(1)} %copy.300), channel_id=1, replica_groups=mesh['seq'=4,'dp'=8] {'seq'}, dimensions={0} | all-to-all | bytes 4718592 | tf_op jit(solution)/shard_map/all_to_all | solution.py:371
  787.6 13.1 reduce-scatter.30.cloned.1.call-done
  803.3 116.9 %reduce-scatter.28.cloned.1.call-done = f32[1024,512]{1,0:T(8,128)} async-done(((f32[1024,4096]{1,0:T(8,128)}), f32[1024,512]{1,0:T(8,128)}) %reduce-scatter.28.cloned.1.call-update) | async-done | bytes 2097168 | tf_op jit(solution)/shard_map/reduce_scatter | solution.py:419
  922.9 93.1 %reduce-scatter.18.cloned.1.call-done = f32[1024,384]{1,0:T(8,128)} async-done(((f32[1024,3072]{1,0:T(8,128)}), f32[1024,384]{1,0:T(8,128)}) %reduce-scatter.18.cloned.1.call-update) | async-done | bytes 1572880 | tf_op jit(solution)/shard_map/reduce_scatter | solution.py:414
  1018.4 42.5 %reduce-scatter.38.cloned.1.call-done = f32[512,1]{1,0:T(8,128)} async-done(((f32[4096,1]{1,0:T(8,128)}), f32[512,1]{1,0:T(8,128)}) %reduce-scatter.38.cloned.1.call-update) | async-done | bytes 2064
  1068.4 29.9 %reduce-scatter.36.cloned.1.call-done = f32[128,4]{1,0:T(8,128)} async-done(((f32[1024,4]{1,0:T(8,128)}), f32[128,4]{1,0:T(8,128)}) %reduce-scatter.36.cloned.1.call-update) | async-done | bytes 2064
  1099.2 36.8 %reduce-scatter.34.cloned.1.call-done = f32[128,4]{1,0:T(8,128)} async-done(((f32[1024,4]{1,0:T(8,128)}), f32[128,4]{1,0:T(8,128)}) %reduce-scatter.34.cloned.1.call-update) | async-done | bytes 2064
  1136.9 33.5 %reduce-scatter.32.cloned.1.call-done = f32[7,128]{1,0:T(8,128)} async-done(((f32[7,1024]{1,0:T(8,128)}), f32[7,128]{1,0:T(8,128)}) %reduce-scatter.32.cloned.1.call-update) | async-done | bytes 3600 | tf_op jit(solution)/shard_map/reduce_scatter | solution.py:421
  1171.1 11.8 all-reduce.1
  1185.3 146.5 %all-reduce.5.cloned.1.call-done = (bf16[1024,256]{0,1:T(8,128)(2,1)}, bf16[1024,384]{1,0:T(8,128)(2,1)}, bf16[1024,128]{1,0:T(8,128)(2,1)}, bf16[1024,128]{1,0:...) async-done(((bf16[1024,256]{0,1:T(8,128)(2,1)}, bf16[1024,384]{1,0:T(8,128)(2,1)}, bf16[1024,128]{1,0:T(8,128)(2,1)}, ...) | async-done | bytes 4194320 | tf_op jit(solution)/shard_map/psum | solution.py:430
  (523 shorter events, 537.0 us)
Async XLA Ops:
  7.2 52.1 %all-gather.8.cloned.1.call-start = ((), (), s32[]{:S(2)}) async-start(), calls=%async_computation.21 | async-start | bytes 7077888 | tf_op jit(solution)/shard_map/all_gather | solution.py:170
  8.0 193.3 %all-gather.14.cloned.1.call-start = ((), (), s32[]{:S(2)}) async-start(), calls=%async_computation.24 | async-start | bytes 4718592 | tf_op jit(solution)/shard_map/all_gather | solution.py:173
  8.7 221.0 %all-gather.10.cloned.1.call-start = ((), (), s32[]{:S(2)}) async-start(), calls=%async_computation.22 | async-start | bytes 2359296 | tf_op jit(solution)/shard_map/all_gather | solution.py:171
  9.5 223.6 %all-gather.12.cloned.1.call-start = ((), (), s32[]{:S(2)}) async-start(), calls=%async_computation.23 | async-start | bytes 2359296 | tf_op jit(solution)/shard_map/all_gather | solution.py:172
  10.0 326.5 %all-gather.16.cloned.1.call-start = ((), (), s32[]{:S(2)}) async-start(), calls=%async_computation.25 | async-start | bytes 2359296 | tf_op jit(solution)/shard_map/all_gather | solution.py:174
  10.6 331.7 %all-gather.18.cloned.1.call-start = ((), (), s32[]{:S(2)}) async-start(), calls=%async_computation.26 | async-start | bytes 9437184 | tf_op jit(solution)/shard_map/all_gather | solution.py:175
  72.6 59.0 %all-to-all-start = ((bf16[384,3,4,256]{3,0,1,2:T(8,128)(2,1)}), bf16[384,3,4,256]{3,0,1,2:T(8,128)(2,1)S(1)}, u32[]{:S(2)}, u32[]{:S(2)}) async-start(bf16[384,3,4,256]{3,0,1,2:T(8,128)(2,1)} %copy.269), calls=%async_computation | async-start | bytes 4718592 | tf_op jit(solution)/shard_map/all_to_all | solution.py:239
  77.3 275.1 %all-gather.20.cloned.1.call-start = ((), (), s32[]{:S(2)}) async-start(), calls=%async_computation.27 | async-start | bytes 9437184 | tf_op jit(solution)/shard_map/all_gather | solution.py:176
  197.3 23.7 %all-to-all-start.1 = ((bf16[4,2,49152]{2,1,0:T(2,128)(2,1)}), bf16[4,2,49152]{2,1,0:T(2,128)(2,1)S(1)}, u32[]{:S(2)}, u32[]{:S(2)}) async-start(bf16[4,2,49152]{2,1,0:T(2,128)(2,1)} %reshape.514), calls=%async_computation.1 | async-start | bytes 1572864 | tf_op jit(solution)/shard_map/all_to_all | solution.py:250
  240.1 23.1 %all-to-all-start.2 = ((bf16[384,1,4,256]{0,3,1,2:T(8,128)(2,1)}), bf16[384,1,4,256]{0,3,1,2:T(8,128)(2,1)S(1)}, u32[]{:S(2)}, u32[]{:S(2)}) async-start(bf16[384,1,4,256]{0,3,1,2:T(8,128)(2,1)} %bitcast.33), calls=%async_computation.2 | async-start | bytes 1572864 | tf_op jit(solution)/shard_map/all_to_all | solution.py:267
  304.1 24.1 %all-to-all-start.4 = ((bf16[4,2,49152]{2,1,0:T(2,128)(2,1)}), bf16[4,2,49152]{2,1,0:T(2,128)(2,1)}, u32[]{:S(2)}, u32[]{:S(2)}) async-start(bf16[4,2,49152]{2,1,0:T(2,128)(2,1)} %reshape.516), calls=%async_computation.4 | async-start | bytes 1572864 | tf_op jit(solution)/shard_map/all_to_all | solution.py:273
  392.5 23.8 %all-to-all-start.5 = ((bf16[384,1,4,256]{0,3,1,2:T(8,128)(2,1)}), bf16[384,1,4,256]{0,3,1,2:T(8,128)(2,1)}, u32[]{:S(2)}, u32[]{:S(2)}) async-start(bf16[384,1,4,256]{0,3,1,2:T(8,128)(2,1)} %bitcast.416), calls=%async_computation.5 | async-start | bytes 1572864 | tf_op jit(solution)/shard_map/all_to_all | solution.py:317
  396.7 383.4 %reduce-scatter.26.cloned.1.call-start = ((), (), s32[]{:S(2)}) async-start(), calls=%async_computation.32 | async-start | bytes 4718592 | tf_op jit(solution)/shard_map/reduce_scatter | solution.py:418
  401.6 380.2 %reduce-scatter.22.cloned.1.call-start = ((), (), s32[]{:S(2)}) async-start(), calls=%async_computation.30 | async-start | bytes 4718592 | tf_op jit(solution)/shard_map/reduce_scatter | solution.py:416
  501.6 282.1 %reduce-scatter.20.cloned.1.call-start = ((), (), s32[]{:S(2)}) async-start(), calls=%async_computation.29 | async-start | bytes 4718592 | tf_op jit(solution)/shard_map/reduce_scatter | solution.py:415
  512.1 273.4 %reduce-scatter.24.cloned.1.call-start = ((), (), s32[]{:S(2)}) async-start(), calls=%async_computation.31 | async-start | bytes 9437184 | tf_op jit(solution)/shard_map/reduce_scatter | solution.py:417
  535.1 265.5 %reduce-scatter.30.cloned.1.call-start = ((), (), s32[]{:S(2)}) async-start(), calls=%async_computation.34 | async-start | bytes 18874368 | tf_op jit(solution)/shard_map/reduce_scatter | solution.py:420
  548.3 371.9 %reduce-scatter.28.cloned.1.call-start = ((), (), s32[]{:S(2)}) async-start(), calls=%async_computation.33 | async-start | bytes 18874368 | tf_op jit(solution)/shard_map/reduce_scatter | solution.py:419
  569.0 447.0 %reduce-scatter.18.cloned.1.call-start = ((), (), s32[]{:S(2)}) async-start(), calls=%async_computation.28 | async-start | bytes 14155776 | tf_op jit(solution)/shard_map/reduce_scatter | solution.py:414
  763.9 297.1 %reduce-scatter.38.cloned.1.call-start = ((), (), s32[]{:S(2)}) async-start(), calls=%async_computation.38 | async-start | bytes 2359296
  767.2 331.1 %reduce-scatter.36.cloned.1.call-start = ((), (), s32[]{:S(2)}) async-start(), calls=%async_computation.37 | async-start | bytes 589824
  777.7 358.3 %reduce-scatter.34.cloned.1.call-start = ((), (), s32[]{:S(2)}) async-start(), calls=%async_computation.36 | async-start | bytes 589824
  778.9 391.6 %reduce-scatter.32.cloned.1.call-start = ((), (), s32[]{:S(2)}) async-start(), calls=%async_computation.35 | async-start | bytes 36864 | tf_op jit(solution)/shard_map/reduce_scatter | solution.py:421
  780.0 551.8 %all-reduce.5.cloned.1.call-start = ((), (), s32[]{:S(2)}) async-start(), calls=%async_computation.39 | async-start | bytes 8388608 | tf_op jit(solution)/shard_map/psum | solution.py:430
  (103 other events, 847.6 us)
Sparse Core Ops, SparseCore 0:
  9.9 49.3 all-gather.7
  61.2 37.4 all-gather.13
  100.6 28.1 all-gather.9
  130.5 28.1 all-gather.11
  160.5 28.2 all-gather.15
  190.5 55.9 all-gather.17
  248.4 55.9 all-gather.19
  401.8 51.6 reduce-scatter.25
  501.7 49.7 reduce-scatter.21
  554.7 51.3 reduce-scatter.19
  609.9 71.2 reduce-scatter.23
  684.6 115.9 reduce-scatter.29
  804.2 115.9 reduce-scatter.27
  923.5 92.3 reduce-scatter.17
  1019.7 41.2 reduce-scatter.37
  1064.2 34.0 reduce-scatter.35
  1101.8 34.1 reduce-scatter.33
  1139.1 31.2 reduce-scatter.31
  1174.5 157.2 all-reduce.4
where the time goes:
time: 1360 us; the launch traced here: 1350 us
  waiting for transfers between devices  667 us (49%)
  matrix products  227 us (17%)
  blocking collectives  161 us (12%)
  local copies, waits for them, and re-layouts  139 us (10%)
  other arithmetic  109 us (8%)
  starting transfers between devices  29.5 us (2%)
  between operations  15.5 us (1%)
    psum x1, waiting for transfers between devices, local(): lax.psum(shares[3].astype(jnp.bfloat16), 'seq').astype(jnp.float32)  146 us
    reduce_scatter x1, waiting for transfers between devices, local(): lax.psum_scatter(all_grads[5], 'dp', scatter_dimension=1, tiled=True)  117 us
    unnamed x22, waiting for transfers between devices  114 us
    reduce_scatter x1, waiting for transfers between devices, local(): lax.psum_scatter(all_grads[0], 'dp', scatter_dimension=1, tiled=True)  93.1 us
    all_to_all x1, blocking collectives, local(): lax.all_to_all(jnp.stack([grad_query, grad_key, grad_value], axis=1).resh...  73.1 us
    all_to_all x1, waiting for transfers between devices, local(): lax.all_to_all(qkv_tok, 'seq', split_axis=2, concat_axis=0, tiled=True)  53.2 us
    dot_general x7, matrix products, dense_left(): lax.dot_general(left, right, (((0,), (0,)), ((), ())), preferred_element_...  45.7 us
    unnamed x185, local copies, waits for them, and re-layouts  40.4 us
  transfers between devices with their start and end apart: 26, of which 16 were waited for; matrix products, arithmetic and copies ran while one was open for 31% of the time, Pallas kernels for 0%

commit v1 on v0

v1 whole, which is shorter than its diff:
```python
import functools

import jax
import jax.numpy as jnp
from jax import lax
from jax.experimental import pallas as pl
from jax.experimental.pallas import tpu as pltpu
from jax.sharding import PartitionSpec as P

HEADS = 16
EPSILON = 1e-05
BF = jnp.bfloat16
F32 = jnp.float32
NEG = -1e30
VMEM_LIMIT = 56 * 1024 * 1024


def params(**kw):
    return pltpu.CompilerParams(vmem_limit_bytes=VMEM_LIMIT, **kw)


def layer_norm(v, gain, shift):
    center = v - jnp.mean(v, axis=-1, keepdims=True)
    inv = lax.rsqrt(jnp.mean(center * center, axis=-1, keepdims=True) + EPSILON)
    normed = center * inv
    return normed * gain + shift, normed, inv


def norm_input_grad(normed, inv, gain, c):
    e = c * gain
    return inv * (
        e
        - jnp.mean(e, axis=-1, keepdims=True)
        - normed * jnp.mean(e * normed, axis=-1, keepdims=True)
    )


def norm_sums(normed, c):
    return jnp.sum(c * normed, axis=0), jnp.sum(c, axis=0)


def dense(a, b):
    return jnp.dot(a, b, preferred_element_type=F32)


def dense_t(a, b):
    return lax.dot_general(a, b, (((1,), (1,)), ((), ())), preferred_element_type=F32)


def dense_left(a, b):
    return lax.dot_general(a, b, (((0,), (0,)), ((), ())), preferred_element_type=F32)


def segment_ids(positions, lengths):
    ends = jnp.cumsum(lengths)
    return jnp.sum((positions[:, None] >= ends[None, :]).astype(jnp.int32), axis=1)


def split_heads(block, scale):
    head = block.shape[1] // 2
    lane = lax.broadcasted_iota(jnp.int32, block.shape, 1)
    zero = jnp.zeros_like(block)
    both = jnp.concatenate(
        [jnp.where(lane < head, block, zero), jnp.where(lane >= head, block, zero)], axis=0
    )
    return both if scale is None else both * jnp.asarray(scale, both.dtype)


def join_heads(acc):
    head, rows = acc.shape[0] // 2, acc.shape[1] // 2
    return jnp.concatenate([acc[:head, :rows], acc[head:, rows:]], axis=0)


def nt(a, b):
    return lax.dot_general(a, b, (((1,), (1,)), ((), ())), preferred_element_type=F32)


def tn(a, b):
    return lax.dot_general(a, b, (((0,), (0,)), ((), ())), preferred_element_type=F32)


def attn_fwd_kernel(scale, chunk, q_ref, k_ref, v_ref, bias_ref, o_ref, lse_ref, acc_ref, m_ref, l_ref):
    both = split_heads(q_ref[...], scale)
    acc_ref[...] = jnp.zeros_like(acc_ref)
    m_ref[...] = jnp.full_like(m_ref, NEG)
    l_ref[...] = jnp.zeros_like(l_ref)

    @pl.loop(0, k_ref.shape[0] // chunk)
    def _(c):
        rows = pl.ds(pl.multiple_of(c * chunk, chunk), chunk)
        b = bias_ref[rows, :]
        s = nt(k_ref[rows, :], both) + jnp.concatenate([b, b], axis=1)
        m_old = m_ref[...]
        m_new = jnp.maximum(m_old, jnp.max(s, axis=0, keepdims=True))
        alpha = jnp.exp(m_old - m_new)
        p = jnp.exp(s - m_new)
        m_ref[...] = m_new
        l_ref[...] = l_ref[...] * alpha + jnp.sum(p, axis=0, keepdims=True)
        acc_ref[...] = acc_ref[...] * alpha + tn(v_ref[rows, :], p.astype(BF))

    total = l_ref[...]
    o_ref[...] = jnp.transpose(join_heads(acc_ref[...] / total)).astype(BF)
    lse_ref[0] = m_ref[...] + jnp.log(total)


def attn_fwd(q, kv, bias):
    nq, width = q.shape
    nk = kv.shape[0]
    head = width // HEADS
    pairs, pw = HEADS // 2, 2 * head
    chunk = 256
    return pl.pallas_call(
        functools.partial(attn_fwd_kernel, head**-0.5, chunk),
        grid=(pairs,),
        in_specs=[
            pl.BlockSpec((nq, pw), lambda i: (0, i)),
            pl.BlockSpec((nk, pw), lambda i: (0, i)),
            pl.BlockSpec((nk, pw), lambda i: (0, pairs + i)),
            pl.BlockSpec((nk, nq), lambda i: (0, 0)),
        ],
        out_specs=[
            pl.BlockSpec((nq, pw), lambda i: (0, i)),
            pl.BlockSpec((1, 1, 2 * nq), lambda i: (i, 0, 0)),
        ],
        out_shape=[
            jax.ShapeDtypeStruct((nq, width), BF),
            jax.ShapeDtypeStruct((pairs, 1, 2 * nq), F32),
        ],
        scratch_shapes=[
            pltpu.VMEM((pw, 2 * nq), F32),
            pltpu.VMEM((1, 2 * nq), F32),
            pltpu.VMEM((1, 2 * nq), F32),
        ],
        compiler_params=params(),
        cost_estimate=pl.CostEstimate(
            flops=8 * HEADS * nq * nk * head,
            bytes_accessed=4 * nk * width + 4 * nq * width + 4 * nk * nq,
            transcendentals=HEADS * nq * nk,
        ),
    )(q, kv, kv, bias)


def attn_bwd_kernel(
    scale, chunk, q_ref, k_ref, v_ref, do_ref, bias_ref, lse_ref, delta_ref, dq_ref, dk_ref, dv_ref, acc_ref
):
    both = split_heads(q_ref[...], scale)
    dboth = split_heads(do_ref[...], None)
    acc_ref[...] = jnp.zeros_like(acc_ref)
    lse = lse_ref[0]
    delta = delta_ref[0]

    @pl.loop(0, k_ref.shape[0] // chunk)
    def _(c):
        rows = pl.ds(pl.multiple_of(c * chunk, chunk), chunk)
        b = bias_ref[rows, :]
        k = k_ref[rows, :]
        p = jnp.exp(nt(k, both) + jnp.concatenate([b, b], axis=1) - lse)
        ds = (p * (nt(v_ref[rows, :], dboth) - delta)).astype(BF)
        dk_ref[rows, :] = dense(ds, both).astype(BF)
        dv_ref[rows, :] = dense(p.astype(BF), dboth).astype(BF)
        acc_ref[...] += tn(k, ds)

    dq_ref[...] = jnp.transpose(join_heads(acc_ref[...]) * scale).astype(BF)


def attn_bwd(q, kv, bias, lse, out, dout):
    nq, width = q.shape
    nk = kv.shape[0]
    head = width // HEADS
    pairs, pw = HEADS // 2, 2 * head
    chunk = 256
    delta = jnp.sum((dout.astype(F32) * out.astype(F32)).reshape(nq, HEADS, head), axis=-1)
    delta = delta.T.reshape(pairs, 1, 2 * nq)
    row_spec = pl.BlockSpec((nq, pw), lambda i: (0, i))
    key_spec = pl.BlockSpec((nk, pw), lambda i: (0, i))
    vec_spec = pl.BlockSpec((1, 1, 2 * nq), lambda i: (i, 0, 0))
    return pl.pallas_call(
        functools.partial(attn_bwd_kernel, head**-0.5, chunk),
        grid=(pairs,),
        in_specs=[
            row_spec,
            key_spec,
            pl.BlockSpec((nk, pw), lambda i: (0, pairs + i)),
            row_spec,
            pl.BlockSpec((nk, nq), lambda i: (0, 0)),
            vec_spec,
            vec_spec,
        ],
        out_specs=[row_spec, key_spec, key_spec],
        out_shape=[
            jax.ShapeDtypeStruct((nq, width), BF),
            jax.ShapeDtypeStruct((nk, width), BF),
            jax.ShapeDtypeStruct((nk, width), BF),
        ],
        scratch_shapes=[pltpu.VMEM((pw, 2 * nq), F32)],
        compiler_params=params(),
        cost_estimate=pl.CostEstimate(
            flops=20 * HEADS * nq * nk * head,
            bytes_accessed=8 * nk * width + 6 * nq * width + 4 * nk * nq,
            transcendentals=HEADS * nq * nk,
        ),
    )(q, kv, kv, dout, bias, lse, delta)


def swap(v, bit):
    return lax.ppermute(v, "dp", [(i, i ^ bit) for i in range(8)])


def assemble_kernel(me_ref, mine_ref, other_ref, out_ref, sems):
    n = mine_ref.shape[2]
    copies = []
    for i in range(4):
        for t, ref in enumerate((mine_ref, other_ref)):
            d = jnp.bitwise_xor(me_ref[0], 2 * i + t)
            dst = out_ref.at[:, pl.ds(pl.multiple_of(d * n, 128), n)]
            copies.append(pltpu.make_async_copy(ref.at[i], dst, sems.at[2 * i + t]))
    for c in copies:
        c.start()
    for c in copies:
        c.wait()


def assemble(me, mine, other):
    _, rows, n = mine.shape
    return pl.pallas_call(
        assemble_kernel,
        in_specs=[
            pl.BlockSpec(memory_space=pltpu.SMEM),
            pl.BlockSpec(memory_space=pl.ANY),
            pl.BlockSpec(memory_space=pl.ANY),
        ],
        out_specs=pl.BlockSpec(memory_space=pl.ANY),
        out_shape=jax.ShapeDtypeStruct((rows, 8 * n), mine.dtype),
        scratch_shapes=[pltpu.SemaphoreType.DMA((8,))],
        compiler_params=params(),
        cost_estimate=pl.CostEstimate(flops=0, bytes_accessed=32 * rows * n, transcendentals=0),
    )(me, mine, other)


def gather_columns(w, me):
    half = w.shape[0] // 2
    top, low = w[:half], w[half:]
    x_top, y_low = swap(top, 2), swap(low, 4)
    y_top, x_low = swap(top, 4), swap(low, 2)
    xy_top, xy_low = swap(x_top, 4), swap(y_low, 2)
    mine = jnp.concatenate([top, low, x_top, x_low, y_top, y_low, xy_top, xy_low], axis=0)
    mine = mine.reshape((4,) + w.shape)
    return assemble(me, mine, swap(mine, 1))


def wgrad_kernel(me_ref, x_ref, keep_in, send_in, keep_ref, send_ref, xt_ref):
    @pl.when((pl.program_id(0) == 0) & (pl.program_id(1) == 0))
    def _():
        xt_ref[...] = jnp.transpose(x_ref[...])

    n = keep_in.shape[1]
    res = dense(xt_ref[...], jnp.concatenate([keep_in[...], send_in[...]], axis=1))
    keep_ref[0] = res[:, :n].astype(BF)
    send_ref[0] = res[:, n:].astype(BF)


def wgrad(me, x, dy):
    tok, rows = x.shape
    n = dy.shape[1] // 8
    block = 128
    nb = n // block
    col = lambda t: lambda i, j, me_ref: (0, jnp.bitwise_xor(me_ref[0], 2 * i + t) * nb + j)
    out_spec = pl.BlockSpec((1, rows, block), lambda i, j, me_ref: (i, 0, j))
    return pl.pallas_call(
        wgrad_kernel,
        grid_spec=pltpu.PrefetchScalarGridSpec(
            num_scalar_prefetch=1,
            grid=(4, nb),
            in_specs=[
                pl.BlockSpec((tok, rows), lambda i, j, me_ref: (0, 0)),
                pl.BlockSpec((tok, block), col(0)),
                pl.BlockSpec((tok, block), col(1)),
            ],
            out_specs=[out_spec, out_spec],
            scratch_shapes=[pltpu.VMEM((rows, tok), BF)],
        ),
        out_shape=[jax.ShapeDtypeStruct((4, rows, n), BF)] * 2,
        compiler_params=params(),
        cost_estimate=pl.CostEstimate(
            flops=2 * tok * rows * 8 * n,
            bytes_accessed=2 * (tok * rows + tok * 8 * n + rows * 8 * n),
            transcendentals=0,
        ),
    )(me, x, dy, dy)


def add(*terms):
    total = terms[0].astype(F32)
    for t in terms[1:]:
        total = total + t.astype(F32)
    return total.astype(BF)


def scatter_columns(keep, send):
    got = swap(send, 1)
    half = keep.shape[1] // 2
    ka, kb, ga, gb = keep[:, :half], keep[:, half:], got[:, :half], got[:, half:]
    pick = lambda a, i: jnp.stack([a[i], a[3]])
    xa = swap(add(pick(ka, 1), pick(ga, 1)), 2)
    yb = swap(add(pick(kb, 2), pick(gb, 2)), 4)
    ya = swap(add(ka[2], ga[2], xa[1]), 4)
    xb = swap(add(kb[1], gb[1], yb[1]), 2)
    return jnp.concatenate([add(ka[0], ga[0], xa[0], ya), add(kb[0], gb[0], yb[0], xb)], axis=0)


def shift(v, n, step, pairs):
    return lax.ppermute(v, "seq", [(a, a + step) for a in pairs if 0 <= a + step < n])


def gather_rows(v, z, n):
    right, left = [v], [v]
    for s in range(n - 1):
        right.append(shift(right[-1], n, 1, range(s, n)))
        left.append(shift(left[-1], n, -1, range(0, n - s)))
    out = []
    for k in range(n):
        val = v
        for d in range(1, n):
            if k + d < n:
                val = jnp.where(z == k + d, right[d], val)
            if k - d >= 0:
                val = jnp.where(z == k - d, left[d], val)
        out.append(val)
    return jnp.concatenate(out, axis=0)


def scatter_rows(v, z, n):
    part = lambda t: lax.dynamic_index_in_dim(v, jnp.clip(t, 0, n - 1), 0, keepdims=False)
    r = l = None
    for p in range(1, n):
        rv, lv = part(n - p + z), part(p - n + z)
        if r is not None:
            rv, lv = rv + r.astype(F32), lv + l.astype(F32)
        r = shift(rv.astype(BF), n, 1, range(0, p))
        l = shift(lv.astype(BF), n, -1, range(n - p, n))
    return part(z) + r.astype(F32) + l.astype(F32)


def local(
    tokens, enc_states, order, lengths, enc_lengths, attn_in, attn_out, cross_q, cross_kv,
    cross_out, ffn_in, ffn_out, proj_bias, gains, ln_bias, ffn_bias, cotangent,
):
    n_dp, n_seq = lax.axis_size("dp"), lax.axis_size("seq")
    z = lax.axis_index("seq")
    dp = lax.axis_index("dp")
    me = dp.astype(jnp.int32).reshape(1)
    fast = n_dp == 8 and attn_out.shape[1] % 128 == 0
    x = tokens[0]
    rows, width = x.shape
    enc_rows = enc_states.shape[1] * n_seq
    group_rows = rows * n_seq
    shard = attn_out.shape[1]

    x_full = gather_rows(x, z, n_seq)
    states = gather_rows(enc_states[0], z, n_seq)
    small = jnp.concatenate([proj_bias, gains, ln_bias, ffn_bias.reshape(-1, shard)], axis=0)
    count = small.shape[0]
    if fast:
        pad_rows = 32
        w = attn_in.shape[1]
        flat = jnp.concatenate([small.reshape(-1), jnp.zeros((pad_rows * w - small.size,), BF)])
        first = gather_columns(jnp.concatenate([attn_in, flat.reshape(pad_rows, w)], axis=0), me)
        w_in = first[:width]
        small_all = first[width:].reshape(pad_rows, n_dp, w).transpose(1, 0, 2).reshape(n_dp, -1)
        small_all = small_all[:, : small.size].reshape(n_dp, count, shard)
        gather = lambda v: gather_columns(v, me)
    else:
        gather = lambda v: lax.all_gather(v, "dp", axis=1, tiled=True)
        w_in = gather(attn_in)
        small_all = lax.all_gather(small, "dp", axis=0, tiled=False)
    w_ckv = gather(cross_kv)
    w_out = gather(attn_out)
    w_cq = gather(cross_q)
    w_cout = gather(cross_out)
    w_up = gather(ffn_in)
    w_down = gather(ffn_out)
    n_bias, n_norm = proj_bias.shape[0], gains.shape[0]
    rows_all = small_all[:, : n_bias + 2 * n_norm].transpose(1, 0, 2).reshape(-1, width).astype(F32)
    bias = rows_all[:n_bias]
    gain = rows_all[n_bias : n_bias + n_norm]
    shift_v = rows_all[n_bias + n_norm :]
    up_bias = small_all[:, n_bias + 2 * n_norm :].reshape(-1).astype(F32)

    place = order[0]
    seg = segment_ids(place, lengths[0])
    seg_enc = segment_ids(jnp.arange(enc_rows, dtype=jnp.int32), enc_lengths[0])
    my_place = lax.dynamic_slice_in_dim(place, z * rows, rows)
    my_seg = lax.dynamic_slice_in_dim(seg, z * rows, rows)
    self_keep = (seg[:, None] == my_seg[None, :]) & (place[:, None] <= my_place[None, :])
    self_bias = jnp.where(self_keep, 0.0, NEG).astype(F32)
    cross_bias = jnp.where(seg_enc[:, None] == my_seg[None, :], 0.0, NEG).astype(F32)
    zero_row = jnp.zeros((width,), F32)

    xf = x_full.astype(F32)
    v1, _, _ = layer_norm(xf, gain[0], shift_v[0])
    a1_full = v1.astype(BF)
    x32 = x.astype(F32)
    v1_own, xh1, rs1 = layer_norm(x32, gain[0], shift_v[0])
    a1 = v1_own.astype(BF)
    q = (dense(a1, w_in[:, :width]) + bias[0]).astype(BF)
    kv = (dense(a1_full, w_in[:, width:]) + jnp.concatenate([zero_row, bias[1]])).astype(BF)
    ekv = (dense(states, w_ckv) + jnp.concatenate([zero_row, bias[4]])).astype(BF)
    attn, lse = attn_fwd(q, kv, self_bias)
    h1 = x32 + dense(attn, w_out) + bias[2]
    v2, xh2, rs2 = layer_norm(h1, gain[1], shift_v[1])
    a2 = v2.astype(BF)
    cq = (dense(a2, w_cq) + bias[3]).astype(BF)
    cattn, clse = attn_fwd(cq, ekv, cross_bias)
    h2 = h1 + dense(cattn, w_cout) + bias[5]
    v3, xh3, rs3 = layer_norm(h2, gain[2], shift_v[2])
    a3 = v3.astype(BF)
    up = dense(a3, w_up) + up_bias
    gelu, gelu_back = jax.vjp(lambda u: jax.nn.gelu(u, approximate=True), up)
    gelu_h = gelu.astype(BF)
    h3 = h2 + dense(gelu_h, w_down) + bias[6]
    out, xh4, rs4 = layer_norm(h3, gain[3], shift_v[3])

    def reduce_dp(a, b):
        if fast:
            return scatter_columns(*wgrad(me, a, b))
        return lax.psum_scatter(dense_left(a, b), "dp", scatter_dimension=1, tiled=True).astype(BF)

    def reduce_seq(v):
        return lax.psum(v, "seq").astype(F32)

    ct = cotangent[0].astype(F32)
    g3, s3 = norm_sums(xh4, ct)
    dh3 = norm_input_grad(xh4, rs4, gain[3], ct)
    dz = dh3.astype(BF)
    g_down = reduce_dp(gelu_h, dz)
    du = gelu_back(dense_t(dz, w_down))[0].astype(BF)
    g_up = reduce_dp(a3, du)
    c3 = dense_t(du, w_up)
    g2, s2 = norm_sums(xh3, c3)
    dh2 = dh3 + norm_input_grad(xh3, rs3, gain[2], c3)
    dc = dh2.astype(BF)
    g_cout = reduce_dp(cattn, dc)
    dcattn = dense_t(dc, w_cout).astype(BF)
    dcq, dke, dve = attn_bwd(cq, ekv, cross_bias, clse, cattn, dcattn)
    dekv = jnp.concatenate([dke, dve], axis=1)
    g_cq = reduce_dp(a2, dcq)
    g_ckv = reduce_dp(states, dekv)
    enc_part = dense_t(dekv, w_ckv)
    enc_grad = scatter_rows(enc_part.reshape(n_seq, -1, width), z, n_seq)
    c2 = dense_t(dcq, w_cq)
    g1, s1 = norm_sums(xh2, c2)
    dh1 = dh2 + norm_input_grad(xh2, rs2, gain[1], c2)
    da = dh1.astype(BF)
    g_out = reduce_dp(attn, da)
    dattn = dense_t(da, w_out).astype(BF)
    dq, dk, dv = attn_bwd(q, kv, self_bias, lse, attn, dattn)
    dq_rows = lax.dynamic_update_slice(jnp.zeros((group_rows, width), BF), dq, (z * rows, 0))
    c1_part = dense_t(dk, w_in[:, width : 2 * width]) + dense_t(dv, w_in[:, 2 * width :])
    c1_q = dense_t(dq, w_in[:, :width])
    c1 = scatter_rows(c1_part.reshape(n_seq, rows, width), z, n_seq) + c1_q
    g_in = reduce_dp(a1_full, jnp.concatenate([dq_rows, dk, dv], axis=1))
    tokens_grad = dh1 + norm_input_grad(xh1, rs1, gain[0], c1)
    _, xh1_full, _ = layer_norm(xf, gain[0], shift_v[0])
    g0, s0 = (a + b for a, b in zip(norm_sums(xh1_full, c1_part), norm_sums(xh1, c1_q)))

    total = lambda v: jnp.sum(v, axis=0, dtype=F32)
    bias_rows = [total(dq), total(dv), total(dh1), total(dcq), total(dve), total(dh2), total(dh3)]
    small_rows = jnp.stack(bias_rows + [g0, g1, g2, g3, s0, s1, s2, s3])
    small_rows = small_rows.reshape(-1, n_dp, shard).transpose(1, 0, 2)
    small_rows = jnp.concatenate([small_rows, total(du).reshape(n_dp, -1, shard)], axis=1)
    small_own = lax.psum_scatter(small_rows, "dp", scatter_dimension=0, tiled=False)
    small_own = lax.psum(small_own, "seq")
    return (
        out.astype(BF)[None],
        tokens_grad[None],
        enc_grad[None],
        reduce_seq(g_in),
        reduce_seq(g_out),
        reduce_seq(g_cq),
        reduce_seq(g_ckv),
        reduce_seq(g_cout),
        reduce_seq(g_up),
        reduce_seq(g_down),
        small_own[:n_bias],
        small_own[n_bias : n_bias + n_norm],
        small_own[n_bias + n_norm : n_bias + 2 * n_norm],
        small_own[n_bias + 2 * n_norm :].reshape(1, -1),
    )


def solution(mesh):
    rows, cols, per_dp = P("dp", "seq", None), P(None, "dp"), P("dp", None)
    in_specs = (rows, rows, per_dp, per_dp, per_dp) + (cols,) * 11 + (rows,)
    out_specs = (rows,) * 3 + (cols,) * 11
    return jax.shard_map(local, mesh=mesh, in_specs=in_specs, out_specs=out_specs, check_vma=False)
```

time: 1360 us -> 1930 us (1.42)
  Pallas kernels: 0 us -> 1200 us
  waiting for transfers between devices: 667 us -> 298 us
  blocking collectives: 161 us -> 19 us
  matrix products: 227 us -> 89.9 us
  starting transfers between devices: 29.5 us -> 136 us
  local copies, waits for them, and re-layouts: 139 us -> 78 us
  other arithmetic: 109 us -> 81.9 us
    pallas_call x0 -> x18, Pallas kernels: none -> 1200 us  [the longest x7 1030 us: assemble(): pl.pallas_call(assemble_kernel, in_specs=[pl.BlockSpec(memory_space=pltpu...]
    reduce_scatter x8 -> x0, waiting for transfers between devices: 257 us -> none  [the longest x1 117 us: local(): lax.psum_scatter(all_grads[5], 'dp', scatter_dimension=1, tiled=True)]
    ppermute x0 -> x108, waiting for transfers between devices: none -> 228 us  [the longest x84 142 us: swap(): return lax.ppermute(v, 'dp', [(i, i ^ bit) for i in range(8)])]
    dot_general x63 -> x17, matrix products: 227 us -> 89.9 us  [the longest x9 51.4 us: dense_t(): lax.dot_general(a, b, (((1,), (1,)), ((), ())), preferred_element_type=F32)]
    ppermute x0 -> x108, starting transfers between devices: none -> 136 us  [the longest x84 76.8 us: swap(): return lax.ppermute(v, 'dp', [(i, i ^ bit) for i in range(8)])]
    all_to_all x7 -> x0, waiting for transfers between devices: 132 us -> none  [the longest x1 53.2 us: local(): lax.all_to_all(qkv_tok, 'seq', split_axis=2, concat_axis=0, tiled=True)]
    unnamed x22 -> x3, waiting for transfers between devices: 114 us -> 0.03 us
    all_to_all x3 -> x0, blocking collectives: 113 us -> none  [the longest x1 73.1 us: local(): lax.all_to_all(jnp.stack([grad_query, grad_key, grad_value], axis=1).resh...]
  transfers between devices with their start and end apart: 26 -> 110, of which waited for: 16 -> 41; matrix products, arithmetic and copies ran while one was open for 31% -> 9% of each run, Pallas kernels for 0% -> 44%
where the time goes in v1:
time: 1930 us; the launch traced here: 1920 us
  Pallas kernels  1200 us (62%)
  waiting for transfers between devices  298 us (15%)
  starting transfers between devices  136 us (7%)
  matrix products  89.9 us (5%)
  other arithmetic  81.9 us (4%)
  local copies, waits for them, and re-layouts  78 us (4%)
    pallas_call x7, Pallas kernels, assemble(): pl.pallas_call(assemble_kernel, in_specs=[pl.BlockSpec(memory_space=pltpu...  1030 us
    ppermute x84, waiting for transfers between devices, swap(): return lax.ppermute(v, 'dp', [(i, i ^ bit) for i in range(8)])  142 us
    ppermute x24, waiting for transfers between devices, shift(): lax.ppermute(v, 'seq', [(a, a + step) for a in pairs if 0 <= a + step < n])  86.5 us
    ppermute x84, starting transfers between devices, swap(): return lax.ppermute(v, 'dp', [(i, i ^ bit) for i in range(8)])  76.8 us
    psum x1, waiting for transfers between devices, reduce_seq(): return lax.psum(v, 'seq').astype(F32)  70.1 us
    pallas_call x7, Pallas kernels, wgrad(): pl.pallas_call(wgrad_kernel, grid_spec=pltpu.PrefetchScalarGridSpec(num_s...  65.3 us
    ppermute x24, starting transfers between devices, shift(): lax.ppermute(v, 'seq', [(a, a + step) for a in pairs if 0 <= a + step < n])  59.3 us
    pallas_call x2, Pallas kernels, attn_bwd(): pl.pallas_call(functools.partial(attn_bwd_kernel, head ** (-0.5), chunk),...  51.9 us
  transfers between devices with their start and end apart: 110, of which 41 were waited for; matrix products, arithmetic and copies ran while one was open for 9% of the time, Pallas kernels for 44%

profile of v1, /device:TPU:0, one launch (start us, length us, event | category | flops | bytes accessed | tf_op | source)
XLA Modules:
  0.0 1919.7 jit_solution(17394648515923701241)
XLA Ops:
  82.5 11.3 collective-permute-done.45
  109.4 14.2 collective-permute-done.38
  197.3 64.7 %shard_map.274 = bf16[1024,1024]{1,0:T(8,128)(2,1)} custom-call(s32[1]{0:T(128)} %bitcast.1.me_ref, bf16[4,1024,128]{2,1,0:T(8,128)(2,1)} %bitcast.316, bf16[4,1024,128]{2,1,0:T(8,128)(2,1)} %copy-done.50), custom_call_target="tpu_custom_call" | custom-call | bytes 4194304 | tf_op jit(solution)/shard_map/pallas_call | solution.py:225
  262.0 64.7 %shard_map.275 = bf16[1024,1024]{1,0:T(8,128)(2,1)} custom-call(s32[1]{0:T(128)} %bitcast.1.me_ref, bf16[4,1024,128]{2,1,0:T(8,128)(2,1)} %bitcast.318, bf16[4,1024,128]{2,1,0:T(8,128)(2,1)} %copy-done.51), custom_call_target="tpu_custom_call" | custom-call | bytes 4194304 | tf_op jit(solution)/shard_map/pallas_call | solution.py:225
  327.7 64.7 %shard_map.278 = bf16[1024,1024]{1,0:T(8,128)(2,1)} custom-call(s32[1]{0:T(128)} %bitcast.1.me_ref, bf16[4,1024,128]{2,1,0:T(8,128)(2,1)} %bitcast.314, bf16[4,1024,128]{2,1,0:T(8,128)(2,1)} %copy-done.52), custom_call_target="tpu_custom_call" | custom-call | bytes 4194304 | tf_op jit(solution)/shard_map/pallas_call | solution.py:225
  399.0 128.2 %shard_map.276 = bf16[1024,2048]{1,0:T(8,128)(2,1)} custom-call(s32[1]{0:T(128)} %bitcast.1.me_ref, bf16[4,1024,256]{2,1,0:T(8,128)(2,1)} %bitcast.21.mine_ref, bf16[4,1024,256]{2,1,0:T(8,128)(2,1)} %collective-permute-done.39.other_ref), custom_call_target="tpu_custom_call" | custom-call | bytes 8388608 | tf_op jit(solution)/shard_map/pallas_call | solution.py:225
  527.2 197.7 %shard_map.272 = bf16[1056,3072]{1,0:T(8,128)(2,1)} custom-call(s32[1]{0:T(128)} %bitcast.1.me_ref, bf16[4,1056,384]{2,1,0:T(8,128)(2,1)} %bitcast.3.mine_ref, bf16[4,1056,384]{2,1,0:T(8,128)(2,1)} %collective-permute-done.6.other_ref), custom_call_target="tpu_custom_call" | custom-call | bytes 12976128 | tf_op jit(solution)/shard_map/pallas_call | solution.py:225
  740.9 36.0 %shard_map.273 = (bf16[384,1024]{1,0:T(8,128)(2,1)}, f32[8,1,768]{2,1,0:T(1,128)}) custom-call(bf16[384,1024]{1,0:T(8,128)(2,1)} %add_convert_fusion.12.q_ref, bf16[1536,2048]{1,0:T(8,128)(2,1)} %add_convert_fusion.k_ref.v_ref, bf16[1536,2048]{1,0:T(8,128)(2,1)} %add_convert_fusion.k_ref.v_ref, f32[1536,384]{1,0:T(8,128)} %and_select_fusion.bias_ref), custom_call_target="tpu_custom_call" | custom-call | flops 4831838208 | bytes 10223616 | tf_op jit(solution)/shard_map/pallas_call | solution.py:112
  787.0 14.7 shard_map.277
  804.5 255.3 %shard_map.279 = bf16[1024,4096]{1,0:T(8,128)(2,1)} custom-call(s32[1]{0:T(128)} %bitcast.1.me_ref, bf16[4,1024,512]{2,1,0:T(8,128)(2,1)} %bitcast.29.mine_ref, bf16[4,1024,512]{2,1,0:T(8,128)(2,1)} %collective-permute-done.53.other_ref), custom_call_target="tpu_custom_call" | custom-call | bytes 16777216 | tf_op jit(solution)/shard_map/pallas_call | solution.py:225
  1059.8 10.8 multiply_convert_fusion
  1070.7 255.3 %shard_map.280 = bf16[4096,1024]{1,0:T(8,128)(2,1)} custom-call(s32[1]{0:T(128)} %bitcast.1.me_ref, bf16[4,4096,128]{2,1,0:T(8,128)(2,1)} %bitcast.31.mine_ref, bf16[4,4096,128]{2,1,0:T(8,128)(2,1)} %collective-permute-done.60.other_ref), custom_call_target="tpu_custom_call" | custom-call | bytes 16777216 | tf_op jit(solution)/shard_map/pallas_call | solution.py:225
  1335.6 10.7 convert_reduce_fusion.1
  1358.2 14.8 shard_map.281
  1383.0 37.1 %shard_map.282 = (bf16[384,1024]{1,0:T(8,128)(2,1)}, bf16[1536,1024]{1,0:T(8,128)(2,1)}, bf16[1536,1024]{1,0:T(8,128)(2,1)}) custom-call(bf16[384,1024]{1,0:T(8,128)(2,1)} %add_convert_fusion.12.q_ref, bf16[1536,2048]{1,0:T(8,128)(2,1)} %add_convert_fusion.k_ref.v_ref, bf16[1536,2048]{1,0:T(8,128)(2,1)} %add_convert_fusion.k_ref.v_ref, ...), custom_call_target="tpu_custom_call" | custom-call | flops 12079595520 | bytes 17301504 | tf_op jit(solution)/shard_map/pallas_call | solution.py:177
  1438.9 14.7 shard_map.288
  1468.7 11.1 fusion.103
  1512.6 17.7 shard_map.283
  1661.1 12.5 collective-permute-done.106
  1680.2 24.4 %collective-permute-done.75 = bf16[512,384]{1,0:T(8,128)(2,1)S(1)} collective-permute-done((bf16[512,384]{1,0:T(8,128)(2,1)S(1)}, bf16[512,384]{1,0:T(8,128)(2,1)S(1)}, u32[]{:S(2)}, u32[]{:S(2)}) %collective-permute-start.75) | collective-permute-done | bytes 393248 | tf_op jit(solution)/shard_map/ppermute | solution.py:206
  1753.9 10.3 collective-permute-done.68
  1783.5 26.5 %collective-permute-done.72 = bf16[128,1024]{1,0:T(8,128)(2,1)S(1)} collective-permute-done((bf16[128,1024]{1,0:T(8,128)(2,1)S(1)}, bf16[128,1024]{1,0:T(8,128)(2,1)S(1)}, u32[]{:S(2)}, u32[]{:S(2)}) %collective-permute-start.72) | collective-permute-done | bytes 262176 | tf_op jit(solution)/shard_map/ppermute | solution.py:312
  1812.6 19.0 psum.63
  1832.8 70.1 %all-reduce.7.cloned.1.call-done = (bf16[1024,384]{1,0:T(8,128)(2,1)}, bf16[1024,128]{1,0:T(8,128)(2,1)}, bf16[1024,128]{1,0:T(8,128)(2,1)}, bf16[1024,256]{1,0:...) async-done(((bf16[1024,384]{1,0:T(8,128)(2,1)}, bf16[1024,128]{1,0:T(8,128)(2,1)}, bf16[1024,128]{1,0:T(8,128)(2,1)}, ...) | async-done | bytes 4194320 | tf_op jit(solution)/shard_map/psum | solution.py:429
  (643 shorter events, 515.6 us)
Async XLA Ops:
  8.0 1804.6 %reduce-scatter.4.cloned.1.call-start = ((), (), s32[]{:S(2)}) async-start(), calls=%async_computation.1 | async-start | bytes 110592
  94.6 30.5 %collective-permute-start.47 = (bf16[512,512]{1,0:T(8,128)(2,1)S(1)}, bf16[512,512]{1,0:T(8,128)(2,1)S(1)}, u32[]{:S(2)}, u32[]{:S(2)}) collective-permute-start(bf16[512,512]{1,0:T(8,128)(2,1)S(1)} %copy-done.76), channel_id=1, source_target_pairs={{0,2},{1,3},{2,0},{3,1},{4,6},{5,7},{6,4},{7,5},{8,10},{9,11},{10,... | collective-permute-start | bytes 1572872 | tf_op jit(solution)/shard_map/ppermute | solution.py:206
  181.4 345.8 %collective-permute-start.6 = (bf16[4,1056,384]{2,1,0:T(8,128)(2,1)}, bf16[4,1056,384]{2,1,0:T(8,128)(2,1)}, u32[]{:S(2)}, u32[]{:S(2)}) collective-permute-start(bf16[4,1056,384]{2,1,0:T(8,128)(2,1)} %bitcast.3.mine_ref), channel_id=1, source_target_pairs={{0,1},{1,0},{2,3},{3,2},{4,5},{5,4},{6,7},{7,6},{8,9},{9,8},{10,11... | collective-permute-start | bytes 9732104 | tf_op jit(solution)/shard_map/ppermute | solution.py:206
  183.5 143.2 %collective-permute-start.46 = (bf16[4,1024,128]{2,1,0:T(8,128)(2,1)S(1)}, bf16[4,1024,128]{2,1,0:T(8,128)(2,1)S(1)}, u32[]{:S(2)}, u32[]{:S(2)}) collective-permute-start(bf16[4,1024,128]{2,1,0:T(8,128)(2,1)S(1)} %bitcast.313), channel_id=1, source_target_pairs={{0,1},{1,0},{2,3},{3,2},{4,5},{5,4},{6,7},{7,6},{8,9},{9,8},{10,11... | collective-permute-start | bytes 3145736 | tf_op jit(solution)/shard_map/ppermute | solution.py:206
  189.8 202.6 %collective-permute-start.12 = (bf16[384,1024]{1,0:T(8,128)(2,1)}, bf16[384,1024]{1,0:T(8,128)(2,1)}, u32[]{:S(2)}, u32[]{:S(2)}) collective-permute-start(bf16[384,1024]{1,0:T(8,128)(2,1)} %collective-permute-done.11), channel_id=1, source_target_pairs={{8,0},{9,1},{10,2},{11,3},{12,4},{13,5},{14,6},{15,7}} | collective-permute-start | bytes 2359304 | tf_op jit(solution)/shard_map/ppermute | solution.py:312
  191.1 201.8 %collective-permute-start.9 = (bf16[384,1024]{1,0:T(8,128)(2,1)}, bf16[384,1024]{1,0:T(8,128)(2,1)}, u32[]{:S(2)}, u32[]{:S(2)}) collective-permute-start(bf16[384,1024]{1,0:T(8,128)(2,1)} %collective-permute-done.8), channel_id=1, source_target_pairs={{16,24},{17,25},{18,26},{19,27},{20,28},{21,29},{22,30},{23,31}} | collective-permute-start | bytes 2359304 | tf_op jit(solution)/shard_map/ppermute | solution.py:312
  195.4 203.6 %collective-permute-start.39 = (bf16[4,1024,256]{2,1,0:T(8,128)(2,1)}, bf16[4,1024,256]{2,1,0:T(8,128)(2,1)}, u32[]{:S(2)}, u32[]{:S(2)}) collective-permute-start(bf16[4,1024,256]{2,1,0:T(8,128)(2,1)} %bitcast.21.mine_ref), channel_id=1, source_target_pairs={{0,1},{1,0},{2,3},{3,2},{4,5},{5,4},{6,7},{7,6},{8,9},{9,8},{10,11... | collective-permute-start | bytes 6291464 | tf_op jit(solution)/shard_map/ppermute | solution.py:206
  326.7 477.8 %collective-permute-start.53 = (bf16[4,1024,512]{2,1,0:T(8,128)(2,1)}, bf16[4,1024,512]{2,1,0:T(8,128)(2,1)}, u32[]{:S(2)}, u32[]{:S(2)}) collective-permute-start(bf16[4,1024,512]{2,1,0:T(8,128)(2,1)} %bitcast.29.mine_ref), channel_id=1, source_target_pairs={{0,1},{1,0},{2,3},{3,2},{4,5},{5,4},{6,7},{7,6},{8,9},{9,8},{10,11... | collective-permute-start | bytes 12582920 | tf_op jit(solution)/shard_map/ppermute | solution.py:206
  392.4 678.3 %collective-permute-start.60 = (bf16[4,4096,128]{2,1,0:T(8,128)(2,1)}, bf16[4,4096,128]{2,1,0:T(8,128)(2,1)}, u32[]{:S(2)}, u32[]{:S(2)}) collective-permute-start(bf16[4,4096,128]{2,1,0:T(8,128)(2,1)} %bitcast.31.mine_ref), channel_id=1, source_target_pairs={{0,1},{1,0},{2,3},{3,2},{4,5},{5,4},{6,7},{7,6},{8,9},{9,8},{10,11... | collective-permute-start | bytes 12582920 | tf_op jit(solution)/shard_map/ppermute | solution.py:206
  1483.9 70.9 %collective-permute-start.61 = (bf16[384,1024]{1,0:T(8,128)(2,1)}, bf16[384,1024]{1,0:T(8,128)(2,1)}, u32[]{:S(2)}, u32[]{:S(2)}) collective-permute-start(bf16[384,1024]{1,0:T(8,128)(2,1)} %get-tuple-element.111), channel_id=1, source_target_pairs={{0,8},{1,9},{2,10},{3,11},{4,12},{5,13},{6,14},{7,15}} | collective-permute-start | bytes 2359304 | tf_op jit(solution)/shard_map/ppermute | solution.py:312
  1492.6 41.7 %collective-permute-start.93 = (bf16[4,1024,128]{2,1,0:T(8,128)(2,1)}, bf16[4,1024,128]{2,1,0:T(8,128)(2,1)}, u32[]{:S(2)}, u32[]{:S(2)}) collective-permute-start(bf16[4,1024,128]{2,1,0:T(8,128)(2,1)} %get-tuple-element.57), channel_id=1, source_target_pairs={{0,1},{1,0},{2,3},{3,2},{4,5},{5,4},{6,7},{7,6},{8,9},{9,8},{10,11... | collective-permute-start | bytes 3145736 | tf_op jit(solution)/shard_map/ppermute | solution.py:206
  1504.1 64.0 %collective-permute-start.88 = (bf16[4,1024,256]{2,1,0:T(8,128)(2,1)}, bf16[4,1024,256]{2,1,0:T(8,128)(2,1)}, u32[]{:S(2)}, u32[]{:S(2)}) collective-permute-start(bf16[4,1024,256]{2,1,0:T(8,128)(2,1)} %get-tuple-element.55), channel_id=1, source_target_pairs={{0,1},{1,0},{2,3},{3,2},{4,5},{5,4},{6,7},{7,6},{8,9},{9,8},{10,11... | collective-permute-start | bytes 6291464 | tf_op jit(solution)/shard_map/ppermute | solution.py:206
  1505.7 32.4 %collective-permute-start.83 = (bf16[4,1024,128]{2,1,0:T(8,128)(2,1)}, bf16[4,1024,128]{2,1,0:T(8,128)(2,1)}, u32[]{:S(2)}, u32[]{:S(2)}) collective-permute-start(bf16[4,1024,128]{2,1,0:T(8,128)(2,1)} %get-tuple-element.53), channel_id=1, source_target_pairs={{0,1},{1,0},{2,3},{3,2},{4,5},{5,4},{6,7},{7,6},{8,9},{9,8},{10,11... | collective-permute-start | bytes 3145736 | tf_op jit(solution)/shard_map/ppermute | solution.py:206
  1505.8 34.0 %collective-permute-start.78 = (bf16[4,1024,128]{2,1,0:T(8,128)(2,1)}, bf16[4,1024,128]{2,1,0:T(8,128)(2,1)S(1)}, u32[]{:S(2)}, u32[]{:S(2)}) collective-permute-start(bf16[4,1024,128]{2,1,0:T(8,128)(2,1)} %get-tuple-element.51), channel_id=1, source_target_pairs={{0,1},{1,0},{2,3},{3,2},{4,5},{5,4},{6,7},{7,6},{8,9},{9,8},{10,11... | collective-permute-start | bytes 3145736 | tf_op jit(solution)/shard_map/ppermute | solution.py:206
  1562.3 81.8 %collective-permute-start.103 = (bf16[4,4096,128]{2,1,0:T(8,128)(2,1)}, bf16[4,4096,128]{2,1,0:T(8,128)(2,1)}, u32[]{:S(2)}, u32[]{:S(2)}) collective-permute-start(bf16[4,4096,128]{2,1,0:T(8,128)(2,1)} %get-tuple-element.61), channel_id=1, source_target_pairs={{0,1},{1,0},{2,3},{3,2},{4,5},{5,4},{6,7},{7,6},{8,9},{9,8},{10,11... | collective-permute-start | bytes 12582920 | tf_op jit(solution)/shard_map/ppermute | solution.py:206
  1562.4 62.4 %collective-permute-start.73 = (bf16[4,1024,384]{2,1,0:T(8,128)(2,1)S(1)}, bf16[4,1024,384]{2,1,0:T(8,128)(2,1)S(1)}, u32[]{:S(2)}, u32[]{:S(2)}) collective-permute-start(bf16[4,1024,384]{2,1,0:T(8,128)(2,1)S(1)} %copy-done.94), channel_id=1, source_target_pairs={{0,1},{1,0},{2,3},{3,2},{4,5},{5,4},{6,7},{7,6},{8,9},{9,8},{10,11... | collective-permute-start | bytes 9437192 | tf_op jit(solution)/shard_map/ppermute | solution.py:206
  1585.3 66.9 %collective-permute-start.98 = (bf16[4,1024,512]{2,1,0:T(8,128)(2,1)}, bf16[4,1024,512]{2,1,0:T(8,128)(2,1)}, u32[]{:S(2)}, u32[]{:S(2)}) collective-permute-start(bf16[4,1024,512]{2,1,0:T(8,128)(2,1)} %get-tuple-element.59), channel_id=1, source_target_pairs={{0,1},{1,0},{2,3},{3,2},{4,5},{5,4},{6,7},{7,6},{8,9},{9,8},{10,11... | collective-permute-start | bytes 12582920 | tf_op jit(solution)/shard_map/ppermute | solution.py:206
  1652.0 250.9 %all-reduce.7.cloned.1.call-start = ((), (), s32[]{:S(2)}) async-start(), calls=%async_computation.2 | async-start | bytes 8388608 | tf_op jit(solution)/shard_map/psum | solution.py:429
  1654.2 56.6 %collective-permute-start.101 = (bf16[2,512,512]{2,1,0:T(8,128)(2,1)S(1)}, bf16[2,512,512]{2,1,0:T(8,128)(2,1)S(1)}, u32[]{:S(2)}, u32[]{:S(2)}) collective-permute-start(bf16[2,512,512]{2,1,0:T(8,128)(2,1)S(1)} %add_convert_fusion.4), channel_id=1, source_target_pairs={{0,4},{1,5},{2,6},{3,7},{4,0},{5,1},{6,2},{7,3},{8,12},{9,13},{10,... | collective-permute-start | bytes 3145736 | tf_op jit(solution)/shard_map/ppermute | solution.py:206
  1656.9 54.0 %collective-permute-start.99 = (bf16[2,512,512]{2,1,0:T(8,128)(2,1)S(1)}, bf16[2,512,512]{2,1,0:T(8,128)(2,1)S(1)}, u32[]{:S(2)}, u32[]{:S(2)}) collective-permute-start(bf16[2,512,512]{2,1,0:T(8,128)(2,1)S(1)} %add_convert_fusion.5), channel_id=1, source_target_pairs={{0,2},{1,3},{2,0},{3,1},{4,6},{5,7},{6,4},{7,5},{8,10},{9,11},{10,... | collective-permute-start | bytes 3145736 | tf_op jit(solution)/shard_map/ppermute | solution.py:206
  1659.8 44.7 %collective-permute-start.75 = (bf16[512,384]{1,0:T(8,128)(2,1)S(1)}, bf16[512,384]{1,0:T(8,128)(2,1)S(1)}, u32[]{:S(2)}, u32[]{:S(2)}) collective-permute-start(bf16[512,384]{1,0:T(8,128)(2,1)S(1)} %get-tuple-element.107), channel_id=1, source_target_pairs={{0,4},{1,5},{2,6},{3,7},{4,0},{5,1},{6,2},{7,3},{8,12},{9,13},{10,... | collective-permute-start | bytes 1179656 | tf_op jit(solution)/shard_map/ppermute | solution.py:206
  1673.6 34.7 %collective-permute-start.77 = (bf16[512,384]{1,0:T(8,128)(2,1)S(1)}, bf16[512,384]{1,0:T(8,128)(2,1)S(1)}, u32[]{:S(2)}, u32[]{:S(2)}) collective-permute-start(bf16[512,384]{1,0:T(8,128)(2,1)S(1)} %get-tuple-element.108), channel_id=1, source_target_pairs={{0,2},{1,3},{2,0},{3,1},{4,6},{5,7},{6,4},{7,5},{8,10},{9,11},{10,... | collective-permute-start | bytes 1179656 | tf_op jit(solution)/shard_map/ppermute | solution.py:206
  1679.3 35.4 %collective-permute-start.105 = (bf16[2048,128]{1,0:T(8,128)(2,1)S(1)}, bf16[2048,128]{1,0:T(8,128)(2,1)S(1)}, u32[]{:S(2)}, u32[]{:S(2)}) collective-permute-start(bf16[2048,128]{1,0:T(8,128)(2,1)S(1)} %get-tuple-element.99), channel_id=1, source_target_pairs={{0,4},{1,5},{2,6},{3,7},{4,0},{5,1},{6,2},{7,3},{8,12},{9,13},{10,... | collective-permute-start | bytes 1572872 | tf_op jit(solution)/shard_map/ppermute | solution.py:206
  1774.0 36.0 %collective-permute-start.72 = (bf16[128,1024]{1,0:T(8,128)(2,1)S(1)}, bf16[128,1024]{1,0:T(8,128)(2,1)S(1)}, u32[]{:S(2)}, u32[]{:S(2)}) collective-permute-start(bf16[128,1024]{1,0:T(8,128)(2,1)S(1)} %fusion.78), channel_id=1, source_target_pairs={{8,0},{16,8},{24,16},{9,1},{17,9},{25,17},{10,2},{18,10},{26,18},{... | collective-permute-start | bytes 786440 | tf_op jit(solution)/shard_map/ppermute | solution.py:312
  (188 other events, 5693.2 us)
Sparse Core Ops, SparseCore 0:
  1652.0 31.1 reduce-scatter.3
Sparse Core Ops, SparseCore 1:
  1729.1 173.7 all-reduce.6

commit v2 on v1

v2 whole, which is shorter than its diff:
```python
import functools

import jax
import jax.numpy as jnp
from jax import lax
from jax.experimental import pallas as pl
from jax.experimental.pallas import tpu as pltpu
from jax.sharding import PartitionSpec as P

HEADS = 16
EPSILON = 1e-05
BF = jnp.bfloat16
F32 = jnp.float32
NEG = -1e30
VMEM_LIMIT = 56 * 1024 * 1024


def params(**kw):
    return pltpu.CompilerParams(vmem_limit_bytes=VMEM_LIMIT, **kw)


def layer_norm(v, gain, shift):
    center = v - jnp.mean(v, axis=-1, keepdims=True)
    inv = lax.rsqrt(jnp.mean(center * center, axis=-1, keepdims=True) + EPSILON)
    normed = center * inv
    return normed * gain + shift, normed, inv


def norm_input_grad(normed, inv, gain, c):
    e = c * gain
    return inv * (
        e
        - jnp.mean(e, axis=-1, keepdims=True)
        - normed * jnp.mean(e * normed, axis=-1, keepdims=True)
    )


def norm_sums(normed, c):
    return jnp.sum(c * normed, axis=0), jnp.sum(c, axis=0)


def dense(a, b):
    return jnp.dot(a, b, preferred_element_type=F32)


def dense_t(a, b):
    return lax.dot_general(a, b, (((1,), (1,)), ((), ())), preferred_element_type=F32)


def dense_left(a, b):
    return lax.dot_general(a, b, (((0,), (0,)), ((), ())), preferred_element_type=F32)


def segment_ids(positions, lengths):
    ends = jnp.cumsum(lengths)
    return jnp.sum((positions[:, None] >= ends[None, :]).astype(jnp.int32), axis=1)


def split_heads(block, scale):
    head = block.shape[1] // 2
    lane = lax.broadcasted_iota(jnp.int32, block.shape, 1)
    zero = jnp.zeros_like(block)
    both = jnp.concatenate(
        [jnp.where(lane < head, block, zero), jnp.where(lane >= head, block, zero)], axis=0
    )
    return both if scale is None else both * jnp.asarray(scale, both.dtype)


def join_heads(acc):
    head, rows = acc.shape[0] // 2, acc.shape[1] // 2
    return jnp.concatenate([acc[:head, :rows], acc[head:, rows:]], axis=0)


def nt(a, b):
    return lax.dot_general(a, b, (((1,), (1,)), ((), ())), preferred_element_type=F32)


def tn(a, b):
    return lax.dot_general(a, b, (((0,), (0,)), ((), ())), preferred_element_type=F32)


def attn_fwd_kernel(scale, chunk, q_ref, k_ref, v_ref, bias_ref, o_ref, lse_ref, acc_ref, m_ref, l_ref):
    both = split_heads(q_ref[...], scale)
    acc_ref[...] = jnp.zeros_like(acc_ref)
    m_ref[...] = jnp.full_like(m_ref, NEG)
    l_ref[...] = jnp.zeros_like(l_ref)

    @pl.loop(0, k_ref.shape[0] // chunk)
    def _(c):
        rows = pl.ds(pl.multiple_of(c * chunk, chunk), chunk)
        b = bias_ref[rows, :]
        s = nt(k_ref[rows, :], both) + jnp.concatenate([b, b], axis=1)
        m_old = m_ref[...]
        m_new = jnp.maximum(m_old, jnp.max(s, axis=0, keepdims=True))
        alpha = jnp.exp(m_old - m_new)
        p = jnp.exp(s - m_new)
        m_ref[...] = m_new
        l_ref[...] = l_ref[...] * alpha + jnp.sum(p, axis=0, keepdims=True)
        acc_ref[...] = acc_ref[...] * alpha + tn(v_ref[rows, :], p.astype(BF))

    total = l_ref[...]
    o_ref[...] = jnp.transpose(join_heads(acc_ref[...] / total)).astype(BF)
    lse_ref[0] = m_ref[...] + jnp.log(total)


def attn_fwd(q, kv, bias, first=0, count=HEADS // 2):
    nq, width = q.shape
    nk = kv.shape[0]
    head = width // HEADS
    pairs, pw = HEADS // 2, 2 * head
    chunk = 256
    return pl.pallas_call(
        functools.partial(attn_fwd_kernel, head**-0.5, chunk),
        grid=(count,),
        in_specs=[
            pl.BlockSpec((nq, pw), lambda i: (0, first + i)),
            pl.BlockSpec((nk, pw), lambda i: (0, first + i)),
            pl.BlockSpec((nk, pw), lambda i: (0, pairs + first + i)),
            pl.BlockSpec((nk, nq), lambda i: (0, 0)),
        ],
        out_specs=[
            pl.BlockSpec((nq, pw), lambda i: (0, i)),
            pl.BlockSpec((1, 1, 2 * nq), lambda i: (i, 0, 0)),
        ],
        out_shape=[
            jax.ShapeDtypeStruct((nq, count * pw), BF),
            jax.ShapeDtypeStruct((count, 1, 2 * nq), F32),
        ],
        scratch_shapes=[
            pltpu.VMEM((pw, 2 * nq), F32),
            pltpu.VMEM((1, 2 * nq), F32),
            pltpu.VMEM((1, 2 * nq), F32),
        ],
        compiler_params=params(),
        cost_estimate=pl.CostEstimate(
            flops=16 * count * nq * nk * head,
            bytes_accessed=4 * nk * count * pw + 4 * nq * count * pw + 4 * nk * nq,
            transcendentals=2 * count * nq * nk,
        ),
    )(q, kv, kv, bias)


def attn_bwd_kernel(
    scale, chunk, q_ref, k_ref, v_ref, do_ref, bias_ref, lse_ref, delta_ref, dq_ref, dk_ref, dv_ref, acc_ref
):
    both = split_heads(q_ref[...], scale)
    dboth = split_heads(do_ref[...], None)
    acc_ref[...] = jnp.zeros_like(acc_ref)
    lse = lse_ref[0]
    delta = delta_ref[0]

    @pl.loop(0, k_ref.shape[0] // chunk)
    def _(c):
        rows = pl.ds(pl.multiple_of(c * chunk, chunk), chunk)
        b = bias_ref[rows, :]
        k = k_ref[rows, :]
        p = jnp.exp(nt(k, both) + jnp.concatenate([b, b], axis=1) - lse)
        ds = (p * (nt(v_ref[rows, :], dboth) - delta)).astype(BF)
        dk_ref[rows, :] = dense(ds, both).astype(BF)
        dv_ref[rows, :] = dense(p.astype(BF), dboth).astype(BF)
        acc_ref[...] += tn(k, ds)

    dq_ref[...] = jnp.transpose(join_heads(acc_ref[...]) * scale).astype(BF)


def attn_delta(out, dout):
    nq, width = out.shape
    delta = jnp.sum((dout.astype(F32) * out.astype(F32)).reshape(nq, HEADS, width // HEADS), axis=-1)
    return delta.T.reshape(HEADS // 2, 1, 2 * nq)


def attn_bwd(q, kv, bias, lse, delta, dout, first=0, count=HEADS // 2):
    nq, width = q.shape
    nk = kv.shape[0]
    head = width // HEADS
    pairs, pw = HEADS // 2, 2 * head
    chunk = 256
    row_spec = pl.BlockSpec((nq, pw), lambda i: (0, first + i))
    key_spec = pl.BlockSpec((nk, pw), lambda i: (0, first + i))
    vec_spec = pl.BlockSpec((1, 1, 2 * nq), lambda i: (first + i, 0, 0))
    new_spec = lambda n: pl.BlockSpec((n, pw), lambda i: (0, i))
    return pl.pallas_call(
        functools.partial(attn_bwd_kernel, head**-0.5, chunk),
        grid=(count,),
        in_specs=[
            row_spec,
            key_spec,
            pl.BlockSpec((nk, pw), lambda i: (0, pairs + first + i)),
            row_spec,
            pl.BlockSpec((nk, nq), lambda i: (0, 0)),
            vec_spec,
            vec_spec,
        ],
        out_specs=[new_spec(nq), new_spec(nk), new_spec(nk)],
        out_shape=[
            jax.ShapeDtypeStruct((nq, count * pw), BF),
            jax.ShapeDtypeStruct((nk, count * pw), BF),
            jax.ShapeDtypeStruct((nk, count * pw), BF),
        ],
        scratch_shapes=[pltpu.VMEM((pw, 2 * nq), F32)],
        compiler_params=params(),
        cost_estimate=pl.CostEstimate(
            flops=40 * count * nq * nk * head,
            bytes_accessed=8 * nk * count * pw + 6 * nq * count * pw + 4 * nk * nq,
            transcendentals=2 * count * nq * nk,
        ),
    )(q, kv, kv, dout, bias, lse, delta)


def swap(v, bit):
    return lax.ppermute(v, "dp", [(i, i ^ bit) for i in range(8)])


def assemble_kernel(widths, me_ref, *refs):
    ins, out_refs = refs[:10], refs[10:]
    upper = pl.program_id(0) < pl.num_programs(0) // 2
    start = 0
    for n, out_ref in zip(widths, out_refs):
        cols = slice(start, start + n)
        start += n

        def put(t, i, value):
            d = jnp.bitwise_xor(me_ref[0], 2 * i + t)
            out_ref[:, pl.ds(pl.multiple_of(d * n, 128), n)] = value

        for t in (0, 1):
            for i in range(3):
                put(t, i, ins[5 * t + i][:, cols])

            @pl.when(upper)
            def _():
                put(t, 3, ins[5 * t + 3][:, cols])

            @pl.when(jnp.logical_not(upper))
            def _():
                put(t, 3, ins[5 * t + 4][:, cols])


def assemble(me, mine, other, widths):
    rows, total = mine[0].shape
    block = next(b for b in (512, 256, 176, 128, 96, 64, 32, 16) if rows // 2 % b == 0)
    last = rows // 2 // block - 1
    every = pl.BlockSpec((block, total), lambda i, me_ref: (i, 0))
    upper = pl.BlockSpec((block, total), lambda i, me_ref: (jnp.minimum(i, last), 0))
    lower = pl.BlockSpec((block, total), lambda i, me_ref: (jnp.maximum(i - last - 1, 0), 0))
    return pl.pallas_call(
        functools.partial(assemble_kernel, widths),
        grid_spec=pltpu.PrefetchScalarGridSpec(
            num_scalar_prefetch=1,
            grid=(rows // block,),
            in_specs=[every, every, every, upper, lower] * 2,
            out_specs=[pl.BlockSpec((block, 8 * n), lambda i, me_ref: (i, 0)) for n in widths],
        ),
        out_shape=[jax.ShapeDtypeStruct((rows, 8 * n), BF) for n in widths],
        compiler_params=params(),
        cost_estimate=pl.CostEstimate(flops=0, bytes_accessed=32 * rows * total, transcendentals=0),
    )(me, *mine, *other)


def after(v, *others):
    return lax.optimization_barrier((v,) + others)[0]


def all_after(vs, *others):
    return lax.optimization_barrier(tuple(vs) + others)[: len(vs)]


def send_shard(ws, *wait):
    w = after(jnp.concatenate(ws, axis=1) if len(ws) > 1 else ws[0], *wait)
    return w, swap(w, 2), swap(w, 4)


def send_diagonal(got, *wait):
    x, y = all_after(got[1:], *wait)
    half = x.shape[0] // 2
    return swap(x[:half], 4), swap(y[half:], 2)


def send_core(parts, *wait):
    parts = all_after(parts, *wait)
    return parts, tuple(swap(v, 1) for v in parts)


def wgrad_kernel(me_ref, x_ref, keep_in, send_in, *refs):
    keep_ref, send_ref, xt_ref = refs[-3:]

    @pl.when(pl.program_id(0) == 0)
    def _():
        xt_ref[...] = jnp.transpose(x_ref[...])

    rows, n = xt_ref.shape[0], keep_in.shape[1]
    res = dense(xt_ref[...], jnp.concatenate([keep_in[...], send_in[...]], axis=1))
    for t, ref in enumerate((keep_ref, send_ref)):
        for j in range(n // 128):
            ref[0, j * rows : (j + 1) * rows] = res[:, t * n + j * 128 : t * n + (j + 1) * 128].astype(BF)


def wgrad(me, x, dy, into=None, at=0, whole=None):
    tok, rows = x.shape
    n = dy.shape[1] // 8
    stacked = n // 128 * rows
    col = lambda t: lambda i, me_ref: (0, jnp.bitwise_xor(me_ref[0], 2 * i + t))
    out_spec = pl.BlockSpec((1, stacked, 128), lambda i, me_ref: (i, at, 0))
    in_specs = [
        pl.BlockSpec((tok, rows), lambda i, me_ref: (0, 0)),
        pl.BlockSpec((tok, n), col(0)),
        pl.BlockSpec((tok, n), col(1)),
    ]
    extra = () if into is None else tuple(into)
    height = extra[0].shape[1] if extra else whole or stacked
    return pl.pallas_call(
        wgrad_kernel,
        grid_spec=pltpu.PrefetchScalarGridSpec(
            num_scalar_prefetch=1,
            grid=(4,),
            in_specs=in_specs + [pl.BlockSpec(memory_space=pl.ANY)] * len(extra),
            out_specs=[out_spec, out_spec],
            scratch_shapes=[pltpu.VMEM((rows, tok), BF)],
        ),
        out_shape=[jax.ShapeDtypeStruct((4, height, 128), BF)] * 2,
        input_output_aliases={4: 0, 5: 1} if extra else {},
        compiler_params=params(),
        cost_estimate=pl.CostEstimate(
            flops=2 * tok * rows * 8 * n,
            bytes_accessed=2 * (tok * rows + tok * 8 * n + rows * 8 * n),
            transcendentals=0,
        ),
    )(me, x, dy, dy, *extra)


def add(*terms):
    total = terms[0].astype(F32)
    for t in terms[1:]:
        total = total + t.astype(F32)
    return total.astype(BF)


def pick(v, i, half):
    rows = v.shape[1] // 2
    return v[i, half * rows : (half + 1) * rows]


def sum_near(keep, got, *wait):
    keep, got = all_after((keep, got), *wait)
    term = lambda i, h: add(pick(keep, i, h), pick(got, i, h))
    xa = swap(jnp.stack([term(1, 0), term(3, 0)]), 2)
    yb = swap(jnp.stack([term(2, 1), term(3, 1)]), 4)
    return xa, yb


def sum_far(keep, got, near, *wait):
    xa, yb, keep, got = all_after(tuple(near) + (keep, got), *wait)
    ya = swap(add(pick(keep, 2, 0), pick(got, 2, 0), xa[1]), 4)
    xb = swap(add(pick(keep, 1, 1), pick(got, 1, 1), yb[1]), 2)
    return ya, xb


def sum_own(keep, got, near, far):
    halves = [add(pick(keep, 0, h), pick(got, 0, h), near[h][0], far[h]) for h in (0, 1)]
    return jnp.concatenate(halves, axis=0)


def shift(v, n, step, pairs):
    return lax.ppermute(v, "seq", [(a, a + step) for a in pairs if 0 <= a + step < n])


def gather_rows(v, z, n):
    right, left = [v], [v]
    for s in range(n - 1):
        right.append(shift(right[-1], n, 1, range(s, n)))
        left.append(shift(left[-1], n, -1, range(0, n - s)))
    out = []
    for k in range(n):
        val = v
        for d in range(1, n):
            if k + d < n:
                val = jnp.where(z == k + d, right[d], val)
            if k - d >= 0:
                val = jnp.where(z == k - d, left[d], val)
        out.append(val)
    return jnp.concatenate(out, axis=0)


def scatter_rows(v, z, n):
    part = lambda t: lax.dynamic_index_in_dim(v, jnp.clip(t, 0, n - 1), 0, keepdims=False).astype(F32)
    r = l = None
    for p in range(1, n):
        rv, lv = part(n - p + z), part(p - n + z)
        if r is not None:
            rv, lv = rv + r.astype(F32), lv + l.astype(F32)
        r = shift(rv.astype(BF), n, 1, range(0, p))
        l = shift(lv.astype(BF), n, -1, range(n - p, n))
    return part(z) + r.astype(F32) + l.astype(F32)


def local(
    tokens, enc_states, order, lengths, enc_lengths, attn_in, attn_out, cross_q, cross_kv,
    cross_out, ffn_in, ffn_out, proj_bias, gains, ln_bias, ffn_bias, cotangent,
):
    n_dp, n_seq = lax.axis_size("dp"), lax.axis_size("seq")
    z = lax.axis_index("seq")
    dp = lax.axis_index("dp")
    me = dp.astype(jnp.int32).reshape(1)
    fast = n_dp == 8 and n_seq == 4 and attn_out.shape[1] % 128 == 0
    x = tokens[0]
    rows, width = x.shape
    enc_rows = enc_states.shape[1] * n_seq
    group_rows = rows * n_seq
    shard = attn_out.shape[1]

    small = jnp.concatenate([proj_bias, gains, ln_bias, ffn_bias.reshape(-1, shard)], axis=0)
    count = small.shape[0]
    if fast:
        pad_rows = 32
        w = attn_in.shape[1]
        flat = jnp.concatenate([small.reshape(-1), jnp.zeros((pad_rows * w - small.size,), BF)])
        a_near = send_shard([jnp.concatenate([attn_in, flat.reshape(pad_rows, w)], axis=0)])
        x_full = lax.all_gather(x, "seq", axis=0, tiled=True)
        a_far = send_diagonal(a_near)
        b_near = send_shard([cross_kv, attn_out, cross_q, cross_out], *a_near[1:])
        states = lax.all_gather(after(enc_states[0], x_full), "seq", axis=0, tiled=True)
        (first,) = assemble(me, *send_core(a_near + a_far), (w,))
        b_far = send_diagonal(b_near, first)
        w_in = first[:width]
        small_all = first[width:].reshape(pad_rows, n_dp, w).transpose(1, 0, 2).reshape(n_dp, -1)
        small_all = small_all[:, : small.size].reshape(n_dp, count, shard)
    else:
        x_full = gather_rows(x, z, n_seq)
        states = gather_rows(enc_states[0], z, n_seq)
        gather = lambda v: lax.all_gather(v, "dp", axis=1, tiled=True)
        w_in, w_ckv, w_out, w_cq = gather(attn_in), gather(cross_kv), gather(attn_out), gather(cross_q)
        w_cout, w_up, w_down = gather(cross_out), gather(ffn_in), gather(ffn_out)
        small_all = lax.all_gather(small, "dp", axis=0, tiled=False)
    n_bias, n_norm = proj_bias.shape[0], gains.shape[0]
    rows_all = small_all[:, : n_bias + 2 * n_norm].transpose(1, 0, 2).reshape(-1, width).astype(F32)
    bias = rows_all[:n_bias]
    gain = rows_all[n_bias : n_bias + n_norm]
    shift_v = rows_all[n_bias + n_norm :]
    up_bias = small_all[:, n_bias + 2 * n_norm :].reshape(-1).astype(F32)

    place = order[0]
    seg = segment_ids(place, lengths[0])
    seg_enc = segment_ids(jnp.arange(enc_rows, dtype=jnp.int32), enc_lengths[0])
    my_place = lax.dynamic_slice_in_dim(place, z * rows, rows)
    my_seg = lax.dynamic_slice_in_dim(seg, z * rows, rows)
    self_keep = (seg[:, None] == my_seg[None, :]) & (place[:, None] <= my_place[None, :])
    self_bias = jnp.where(self_keep, 0.0, NEG).astype(F32)
    cross_bias = jnp.where(seg_enc[:, None] == my_seg[None, :], 0.0, NEG).astype(F32)
    zero_row = jnp.zeros((width,), F32)

    xf = x_full.astype(F32)
    v1, _, _ = layer_norm(xf, gain[0], shift_v[0])
    a1_full = v1.astype(BF)
    x32 = x.astype(F32)
    v1_own, xh1, rs1 = layer_norm(x32, gain[0], shift_v[0])
    a1 = v1_own.astype(BF)
    kv = (dense(a1_full, w_in[:, width:]) + jnp.concatenate([zero_row, bias[1]])).astype(BF)
    q = (dense(a1, w_in[:, :width]) + bias[0]).astype(BF)
    if fast:
        b_parts, b_other = send_core(b_near + b_far, kv)
        c_near = send_shard([ffn_in], kv)
        q, kv, *_ = all_after((q, kv), *b_far, states)
    half = HEADS // 4
    attn_a, lse_a = attn_fwd(q, kv, self_bias, 0, half)
    if fast:
        q, attn_a, lse_a = all_after((q, attn_a, lse_a), *c_near[1:], *b_other)
        c_far = send_diagonal(c_near, attn_a)
        d_near = send_shard([ffn_out], attn_a)
    attn_b, lse_b = attn_fwd(q, kv, self_bias, half, half)
    attn = jnp.concatenate([attn_a, attn_b], axis=1)
    lse = jnp.concatenate([lse_a, lse_b], axis=0)
    if fast:
        attn, lse = all_after((attn, lse), *c_far)
        widths = tuple(v.shape[1] for v in (cross_kv, attn_out, cross_q, cross_out))
        c_parts, c_other = send_core(c_near + c_far, attn)
        b_parts = all_after(b_parts, attn)
        w_ckv, w_out, w_cq, w_cout = assemble(me, b_parts, b_other, widths)
    h1 = x32 + dense(attn, w_out) + bias[2]
    v2, xh2, rs2 = layer_norm(h1, gain[1], shift_v[1])
    a2 = v2.astype(BF)
    cq = (dense(a2, w_cq) + bias[3]).astype(BF)
    ekv = (dense(states, w_ckv) + jnp.concatenate([zero_row, bias[4]])).astype(BF)
    if fast:
        cq = after(cq, ekv, *c_other, *d_near[1:])
        d_far = send_diagonal(d_near, cq)
    cattn, clse = attn_fwd(cq, ekv, cross_bias)
    if fast:
        cattn = after(cattn, *d_far)
        d_parts, d_other = send_core(d_near + d_far, cattn)
        c_parts = all_after(c_parts, cattn)
        (w_up,) = assemble(me, c_parts, c_other, (ffn_in.shape[1],))
    h2 = h1 + dense(cattn, w_cout) + bias[5]
    v3, xh3, rs3 = layer_norm(h2, gain[2], shift_v[2])
    a3 = v3.astype(BF)
    up = dense(a3, w_up) + up_bias
    gelu, gelu_back = jax.vjp(lambda u: jax.nn.gelu(u, approximate=True), up)
    gelu_h = gelu.astype(BF)
    if fast:
        d_parts = all_after(d_parts, gelu_h)
        (w_down,) = assemble(me, d_parts, d_other, (shard,))
    h3 = h2 + dense(gelu_h, w_down) + bias[6]
    out, xh4, rs4 = layer_norm(h3, gain[3], shift_v[3])

    total = lambda v: jnp.sum(v, axis=0, dtype=F32)
    by_columns = lambda a, b: lax.psum_scatter(dense_left(a, b), "dp", scatter_dimension=1, tiled=True).astype(BF)
    by_chain = lambda v: lax.psum(v, "seq")
    ct = cotangent[0].astype(F32)
    g3, s3 = norm_sums(xh4, ct)
    dh3 = norm_input_grad(xh4, rs4, gain[3], ct)
    dz = dh3.astype(BF)
    if fast:
        d_keep, d_send = wgrad(me, gelu_h, dz)
        dz, d_keep, d_send = all_after((dz, d_keep, d_send))
        d_got = swap(d_send, 1)
    du = gelu_back(dense_t(dz, w_down))[0].astype(BF)
    if fast:
        du, d_got = all_after((du, d_got))
        d_n = sum_near(d_keep, d_got, du)
        c_keep, c_send = wgrad(me, a3, du)
        du, c_send = all_after((du, c_send))
        c_got = swap(c_send, 1)
    c3 = dense_t(du, w_up)
    g2, s2 = norm_sums(xh3, c3)
    dh2 = dh3 + norm_input_grad(xh3, rs3, gain[2], c3)
    dc = dh2.astype(BF)
    if fast:
        dc, c_got = all_after((dc, c_got))
        e_rows = (2 * shard + cross_kv.shape[1]) // 128 * width
        e_grads = wgrad(me, cattn, dc, None, 0, e_rows)
        dc, *e_grads = all_after((dc, *e_grads))
    dcattn = dense_t(dc, w_cout).astype(BF)
    cdelta = attn_delta(cattn, dcattn)
    if fast:
        dcattn, cdelta = all_after((dcattn, cdelta), *d_n)
        d_f = sum_far(d_keep, d_got, d_n, dcattn)
    dcq, dke, dve = attn_bwd(cq, ekv, cross_bias, clse, cdelta, dcattn)
    dekv = jnp.concatenate([dke, dve], axis=1)
    if fast:
        dcq, dekv = all_after((dcq, dekv), *d_f)
        c_n = sum_near(c_keep, c_got, dcq)
        e_grads = wgrad(me, a2, dcq, e_grads, 1)
        e_keep, e_send = wgrad(me, states, dekv, e_grads, 1)
        dcq, dekv, e_keep, e_send = all_after((dcq, dekv, e_keep, e_send))
        e_got = swap(e_send, 1)
        d_all = by_chain(sum_own(d_keep, d_got, d_n, d_f))
        enc_part = dense_t(dekv, w_ckv).astype(BF)
        dcq, enc_part = all_after((dcq, enc_part))
        enc_part = after(enc_part, d_all)
        enc_sum = lax.psum_scatter(enc_part, "seq", scatter_dimension=0, tiled=True)
        enc_grad = enc_sum.astype(F32)
    c2 = dense_t(dcq, w_cq)
    g1, s1 = norm_sums(xh2, c2)
    dh1 = dh2 + norm_input_grad(xh2, rs2, gain[1], c2)
    da = dh1.astype(BF)
    if fast:
        i_rows = (shard + attn_in.shape[1]) // 128 * width
        i_grads = wgrad(me, attn, da, None, attn_in.shape[1] // 128, i_rows)
        da, *i_grads = all_after((da, *i_grads), *c_n, e_got)
        c_f = sum_far(c_keep, c_got, c_n, da)
    dattn = dense_t(da, w_out).astype(BF)
    delta = attn_delta(attn, dattn)
    if fast:
        dattn, delta = all_after((dattn, delta), *c_f, enc_sum)
        e_n = sum_near(e_keep, e_got, dattn)
        c_sum = sum_own(c_keep, c_got, c_n, c_f)
        c_all = by_chain(after(c_sum, enc_sum))
    dq_a, dk_a, dv_a = attn_bwd(q, kv, self_bias, lse, delta, dattn, 0, 5)
    if fast:
        dattn, dq_a, dk_a, dv_a = all_after((dattn, dq_a, dk_a, dv_a), *e_n)
        e_f = sum_far(e_keep, e_got, e_n, dattn)
    dq_b, dk_b, dv_b = attn_bwd(q, kv, self_bias, lse, delta, dattn, 5, 3)
    if fast:
        dq_b, dk_b, dv_b = all_after((dq_b, dk_b, dv_b), *e_f)
        e_sum = sum_own(e_keep, e_got, e_n, e_f)
        e_all = by_chain(after(e_sum, c_all))
    dq, dk, dv = (jnp.concatenate(p, axis=1) for p in ((dq_a, dq_b), (dk_a, dk_b), (dv_a, dv_b)))
    dq_rows = lax.dynamic_update_slice(jnp.zeros((group_rows, width), BF), dq, (z * rows, 0))
    dqkv = jnp.concatenate([dq_rows, dk, dv], axis=1)
    if fast:
        i_keep, i_send = wgrad(me, a1_full, dqkv, i_grads, 0)
        dq, dk, dv, i_keep, i_send = all_after((dq, dk, dv, i_keep, i_send), c_all)
        i_got = swap(i_send, 1)
    c1_part = dense_t(dk, w_in[:, width : 2 * width]) + dense_t(dv, w_in[:, 2 * width :])
    c1_q = dense_t(dq, w_in[:, :width])
    if fast:
        c1_part, i_got = all_after((c1_part, i_got))
        c1_sum = scatter_rows(c1_part.astype(BF).reshape(n_seq, rows, width), z, n_seq)
        i_n = sum_near(i_keep, i_got)
        i_f = sum_far(i_keep, i_got, i_n, e_all)
        i_sum = scatter_rows(sum_own(i_keep, i_got, i_n, i_f).reshape(n_seq, -1, 128), z, n_seq)
        i_all = gather_rows(i_sum.astype(BF), z, n_seq)
        c1 = c1_sum + c1_q
        flat_out = lambda v, r: jnp.concatenate(jnp.split(v, v.shape[0] // r, axis=0), axis=1).astype(F32)
        r_up, r_down = flat_out(c_all, width), d_all.astype(F32)
        r_in, r_out = flat_out(i_all[:-width], width), i_all[-width:].astype(F32)
        r_cout, r_cq, r_ckv = (flat_out(v, width) for v in jnp.split(e_all, [width, 2 * width], axis=0))
    else:
        c1 = lax.psum_scatter(c1_part, "seq", scatter_dimension=0, tiled=True) + c1_q
        enc_grad = lax.psum_scatter(dense_t(dekv, w_ckv), "seq", scatter_dimension=0, tiled=True)
        pairs = [(a1_full, dqkv), (attn, da), (a2, dcq), (states, dekv), (cattn, dc), (a3, du), (gelu_h, dz)]
        grads = [by_chain(by_columns(a, b)).astype(F32) for a, b in pairs]
        r_in, r_out, r_cq, r_ckv, r_cout, r_up, r_down = grads
    tokens_grad = dh1 + norm_input_grad(xh1, rs1, gain[0], c1)
    _, xh1_full, _ = layer_norm(xf, gain[0], shift_v[0])
    g0, s0 = (a + b for a, b in zip(norm_sums(xh1_full, c1_part), norm_sums(xh1, c1_q)))

    bias_rows = [total(dq), total(dv), total(dh1), total(dcq), total(dve), total(dh2), total(dh3)]
    small_rows = jnp.stack(bias_rows + [g0, g1, g2, g3, s0, s1, s2, s3])
    small_rows = small_rows.reshape(-1, n_dp, shard).transpose(1, 0, 2)
    small_rows = jnp.concatenate([small_rows, total(du).reshape(n_dp, -1, shard)], axis=1)
    if fast:
        for bit in (1, 2, 4):
            small_rows = small_rows + swap(small_rows, bit)
        for bit in (1, 2):
            small_rows = small_rows + lax.ppermute(small_rows, "seq", [(i, i ^ bit) for i in range(n_seq)])
    else:
        small_rows = lax.psum(small_rows, ("dp", "seq"))
    small_own = lax.dynamic_index_in_dim(small_rows, dp, 0, keepdims=False)
    return (
        out.astype(BF)[None],
        tokens_grad[None],
        enc_grad[None],
        r_in,
        r_out,
        r_cq,
        r_ckv,
        r_cout,
        r_up,
        r_down,
        small_own[:n_bias],
        small_own[n_bias : n_bias + n_norm],
        small_own[n_bias + n_norm : n_bias + 2 * n_norm],
        small_own[n_bias + 2 * n_norm :].reshape(1, -1),
    )


def solution(mesh):
    rows, cols, per_dp = P("dp", "seq", None), P(None, "dp"), P("dp", None)
    in_specs = (rows, rows, per_dp, per_dp, per_dp) + (cols,) * 11 + (rows,)
    out_specs = (rows,) * 3 + (cols,) * 11
    return jax.shard_map(local, mesh=mesh, in_specs=in_specs, out_specs=out_specs, check_vma=False)
```

time: 1930 us -> 720 us (0.37)
  Pallas kernels: 1200 us -> 194 us
  waiting for transfers between devices: 298 us -> 179 us
  local copies, waits for them, and re-layouts: 78 us -> 35.7 us
  starting transfers between devices: 136 us -> 94 us
    pallas_call x7 -> x4, Pallas kernels: 1030 us -> 31.8 us  [assemble(): pl.pallas_call(functools.partial(assemble_kernel, widths), grid_spec=pltp...]
    ppermute x84 -> x59, waiting for transfers between devices: 142 us -> 61.5 us  [swap(): return lax.ppermute(v, 'dp', [(i, i ^ bit) for i in range(8)])]
    ppermute x24 -> x18, waiting for transfers between devices: 86.5 us -> 39.4 us  [shift(): lax.ppermute(v, 'seq', [(a, a + step) for a in pairs if 0 <= a + step < n])]
    ppermute x84 -> x59, starting transfers between devices: 76.8 us -> 44 us  [swap(): return lax.ppermute(v, 'dp', [(i, i ^ bit) for i in range(8)])]
    unnamed x247 -> x178, local copies, waits for them, and re-layouts: 41.3 us -> 17 us
    ppermute x24 -> x18, starting transfers between devices: 59.3 us -> 42.7 us  [shift(): lax.ppermute(v, 'seq', [(a, a + step) for a in pairs if 0 <= a + step < n])]
    pallas_call x2 -> x3, Pallas kernels: 51.9 us -> 55.1 us  [attn_bwd(): pl.pallas_call(functools.partial(attn_bwd_kernel, head ** (-0.5), chunk),...]
    psum x1 -> x3, waiting for transfers between devices: 70.1 us -> 67.1 us  [local(): by_chain = lambda v: lax.psum(v, 'seq')]
  transfers between devices with their start and end apart: 110 -> 85, of which waited for: 41 -> 32; matrix products, arithmetic and copies ran while one was open for 9% -> 28% of each run, Pallas kernels for 44% -> 22%
where the time goes in v2:
time: 720 us; the launch traced here: 708 us
  Pallas kernels  194 us (27%)
  waiting for transfers between devices  179 us (25%)
  other arithmetic  97.8 us (14%)
  starting transfers between devices  94 us (13%)
  matrix products  91.3 us (13%)
  local copies, waits for them, and re-layouts  35.7 us (5%)
  between operations  16 us (2%)
    psum x3, waiting for transfers between devices, local(): by_chain = lambda v: lax.psum(v, 'seq')  67.1 us
    ppermute x59, waiting for transfers between devices, swap(): return lax.ppermute(v, 'dp', [(i, i ^ bit) for i in range(8)])  61.5 us
    pallas_call x3, Pallas kernels, attn_bwd(): pl.pallas_call(functools.partial(attn_bwd_kernel, head ** (-0.5), chunk),...  55.1 us
    pallas_call x7, Pallas kernels, wgrad(): pl.pallas_call(wgrad_kernel, grid_spec=pltpu.PrefetchScalarGridSpec(num_s...  54 us
    pallas_call x3, Pallas kernels, attn_fwd(): pl.pallas_call(functools.partial(attn_fwd_kernel, head ** (-0.5), chunk),...  52.7 us
    dot_general x9, matrix products, dense_t(): lax.dot_general(a, b, (((1,), (1,)), ((), ())), preferred_element_type=F32)  49.8 us
    ppermute x59, starting transfers between devices, swap(): return lax.ppermute(v, 'dp', [(i, i ^ bit) for i in range(8)])  44 us
    ppermute x18, starting transfers between devices, shift(): lax.ppermute(v, 'seq', [(a, a + step) for a in pairs if 0 <= a + step < n])  42.7 us
  transfers between devices with their start and end apart: 85, of which 32 were waited for; matrix products, arithmetic and copies ran while one was open for 28% of the time, Pallas kernels for 22%

profile of v2, /device:TPU:0, one launch (start us, length us, event | category | flops | bytes accessed | tf_op | source)
XLA Modules:
  0.0 707.6 jit_solution(3554548025967915684)
XLA Ops:
  15.3 16.7 %collective-permute-done.refs_1_ = bf16[1056,384]{1,0:T(8,128)(2,1)} collective-permute-done((bf16[1056,384]{1,0:T(8,128)(2,1)S(1)}, bf16[1056,384]{1,0:T(8,128)(2,1)}, u32[]{:S(2)}, u32[]{:S(2)}) %collective-permute-start) | collective-permute-done | bytes 811040 | tf_op jit(solution)/shard_map/ppermute | solution.py:211
  61.2 18.3 %collective-permute-done.10.refs_2_ = bf16[1024,640]{1,0:T(8,128)(2,1)} collective-permute-done((bf16[1024,640]{1,0:T(8,128)(2,1)S(1)}, bf16[1024,640]{1,0:T(8,128)(2,1)}, u32[]{:S(2)}, u32[]{:S(2)}) %collective-permute-start.10) | collective-permute-done | bytes 1310752 | tf_op jit(solution)/shard_map/ppermute | solution.py:211
  91.4 8.7 %add_convert_fusion.k_ref.v_ref = bf16[1536,2048]{1,0:T(8,128)(2,1)} fusion(bf16[1536,1024]{1,0:T(8,128)(2,1)S(1)} %fusion.5.x_ref, f32[2048]{0:T(1024)S(1)} %concatenate.68, bf16[1056,3072]{1,0:T(8,128)(2,1)S(1)} %copy-done.16), kind=kOutput, calls=%fused_computation | convolution fusion | flops 6448742400 | bytes 13639680 | tf_op jit(solution)/shard_map/dot_general | solution.py:43
  111.4 19.3 %shard_map.273 = (bf16[384,512]{1,0:T(8,128)(2,1)}, f32[4,1,768]{2,1,0:T(1,128)}) custom-call(bf16[384,1024]{1,0:T(8,128)(2,1)} %add_convert_fusion.6.q_ref, bf16[1536,2048]{1,0:T(8,128)(2,1)} %add_convert_fusion.k_ref.v_ref, bf16[1536,2048]{1,0:T(8,128)(2,1)} %add_convert_fusion.k_ref.v_ref, f32[1536,384]{1,0:T(8,128)} %and_select_fusion.bias_ref), custom_call_target="tpu_custom_call" | custom-call | flops 2415919104 | bytes 6291456 | tf_op jit(solution)/shard_map/pallas_call | solution.py:112
  136.3 19.3 %shard_map.274 = (bf16[384,512]{1,0:T(8,128)(2,1)}, f32[4,1,768]{2,1,0:T(1,128)}) custom-call(bf16[384,1024]{1,0:T(8,128)(2,1)} %add_convert_fusion.6.q_ref, bf16[1536,2048]{1,0:T(8,128)(2,1)} %add_convert_fusion.k_ref.v_ref, bf16[1536,2048]{1,0:T(8,128)(2,1)} %add_convert_fusion.k_ref.v_ref, f32[1536,384]{1,0:T(8,128)} %and_select_fusion.bias_ref), custom_call_target="tpu_custom_call" | custom-call | flops 2415919104 | bytes 6291456 | tf_op jit(solution)/shard_map/pallas_call | solution.py:112
  158.9 8.2 %shard_map.275 = (bf16[1024,2048]{1,0:T(8,128)(2,1)}, bf16[1024,1024]{1,0:T(8,128)(2,1)}, bf16[1024,1024]{1,0:T(8,128)(2,1)}, bf16[1024,1024]{1,0:T(8,128)(2,1)}) custom-call(s32[1]{0:T(128)} %bitcast.1.me_ref, bf16[1024,640]{1,0:T(8,128)(2,1)} %copy-done.19, bf16[1024,640]{1,0:T(8,128)(2,1)} %collective-permute-done.9.refs_1_, ...), custom_call_target="tpu_custom_call" | custom-call | bytes 20971520 | tf_op jit(solution)/shard_map/pallas_call | solution.py:246
  182.0 14.1 %shard_map.276 = (bf16[384,1024]{1,0:T(8,128)(2,1)}, f32[8,1,768]{2,1,0:T(1,128)}) custom-call(bf16[384,1024]{1,0:T(8,128)(2,1)} %add_convert_fusion.4.q_ref, bf16[512,2048]{1,0:T(8,128)(2,1)} %add_convert_fusion.1.k_ref.v_ref, bf16[512,2048]{1,0:T(8,128)(2,1)} %add_convert_fusion.1.k_ref.v_ref, f32[512,384]{1,0:T(8,128)} %compare_select_fusion.bias_ref), custom_call_target="tpu_custom_call" | custom-call | flops 1610612736 | bytes 4456448 | tf_op jit(solution)/shard_map/pallas_call | solution.py:112
  207.3 10.8 %multiply_convert_fusion = (bf16[384,4096]{1,0:T(8,128)(2,1)}, f32[384,4096]{1,0:T(8,128)}) fusion(f32[4096]{0:T(1024)S(1)} %bitcast.298, bf16[384,1024]{1,0:T(8,128)(2,1)S(1)} %add_convert_fusion.3.x_ref, bf16[1024,4096]{1,0:T(8,128)(2,1)} %shard_map.277), kind=kOutput, calls=%fused_computation.22 | convolution fusion | flops 3236954112 | bytes 18628608 | tf_op jit(solution)/shard_map/dot_general | solution.py:43
  219.4 10.0 %shard_map.278 = bf16[4096,1024]{1,0:T(8,128)(2,1)} custom-call(s32[1]{0:T(128)} %bitcast.1.me_ref, bf16[4096,128]{1,0:T(8,128)(2,1)} %refs_0_.1, bf16[4096,128]{1,0:T(8,128)(2,1)} %copy-done.34, bf16[4096,128]{1,0:T(8,128)(2,1)} %copy-done.35, bf16[2048,128]{1,0:T(8,128)(2,1)} %collective-permute-done.29.refs_3_, ...), custom_call_target="tpu_custom_call" | custom-call | bytes 16777216 | tf_op jit(solution)/shard_map/pallas_call | solution.py:246
  229.4 7.3 %fusion.101 = (f32[384]{0:T(512)S(1)}, f32[384,1024]{1,0:T(8,128)S(1)}) fusion(f32[1024]{0:T(1024)S(1)} %get-tuple-element.411, f32[384,1024]{1,0:T(8,128)S(1)} %get-tuple-element.430, bf16[384,4096]{1,0:T(8,128)(2,1)} %get-tuple-element.431.x_ref, bf16[4096,1024]{1,0:T(8,128)(2,1)} %shard_map.278), kind=kOutput, calls=%fused_computation.273 | convolution fusion | flops 3222404608 | bytes 14685696 | tf_op jit(solution)/shard_map/dot_general | solution.py:43
  242.3 9.4 %shard_map.279 = (bf16[4,4096,128]{2,1,0:T(8,128)(2,1)}, bf16[4,4096,128]{2,1,0:T(8,128)(2,1)}) custom-call(s32[1]{0:T(128)} %bitcast.1.me_ref, bf16[384,4096]{1,0:T(8,128)(2,1)} %get-tuple-element.431.x_ref, bf16[384,1024]{1,0:T(8,128)(2,1)} %convert_element_type.769.keep_in.send_in, bf16[384,1024]{1,0:T(8,128)(2,1)} %convert_element_type.769.keep_in.send_in), custom_call_target="tpu_custom_call" | custom-call | flops 3221225472 | bytes 12320768 | tf_op jit(solution)/shard_map/pallas_call | solution.py:311
  252.1 13.8 %fusion.14.keep_in.send_in = bf16[384,4096]{1,0:T(8,128)(2,1)} fusion(f32[384,4096]{1,0:T(8,128)} %get-tuple-element.432, bf16[384,1024]{1,0:T(8,128)(2,1)S(1)} %copy-done.48, bf16[4096,1024]{1,0:T(8,128)(2,1)} %shard_map.278), kind=kOutput, calls=%fused_computation.19 | convolution fusion | flops 3252682752 | bytes 18612224 | tf_op jit(solution)/shard_map/dot_general | solution.py:47
  265.9 8.0 %shard_map.280 = (bf16[4,4096,128]{2,1,0:T(8,128)(2,1)}, bf16[4,4096,128]{2,1,0:T(8,128)(2,1)}) custom-call(s32[1]{0:T(128)} %bitcast.1.me_ref, bf16[384,1024]{1,0:T(8,128)(2,1)} %copy-done.47, bf16[384,4096]{1,0:T(8,128)(2,1)} %fusion.14.keep_in.send_in, bf16[384,4096]{1,0:T(8,128)(2,1)} %fusion.14.keep_in.send_in), custom_call_target="tpu_custom_call" | custom-call | flops 3221225472 | bytes 12320768 | tf_op jit(solution)/shard_map/pallas_call | solution.py:311
  309.7 14.6 %shard_map.282 = (bf16[384,1024]{1,0:T(8,128)(2,1)}, bf16[512,1024]{1,0:T(8,128)(2,1)}, bf16[512,1024]{1,0:T(8,128)(2,1)}) custom-call(bf16[384,1024]{1,0:T(8,128)(2,1)} %add_convert_fusion.4.q_ref, bf16[512,2048]{1,0:T(8,128)(2,1)} %add_convert_fusion.1.k_ref.v_ref, bf16[512,2048]{1,0:T(8,128)(2,1)} %add_convert_fusion.1.k_ref.v_ref, ...), custom_call_target="tpu_custom_call" | custom-call | flops 4026531840 | bytes 7340032 | tf_op jit(solution)/shard_map/pallas_call | solution.py:182
  353.2 41.9 %all-reduce.7.cloned.1.call-done = bf16[4096,128]{1,0:T(8,128)(2,1)} async-done(((bf16[4096,128]{1,0:T(8,128)(2,1)}), bf16[4096,128]{1,0:T(8,128)(2,1)}) %all-reduce.7.cloned.1.call-update) | async-done | bytes 1048592 | tf_op jit(solution)/shard_map/psum | solution.py:506
  416.2 8.3 %reduce-scatter.2.cloned.1.call-done = bf16[128,1024]{1,0:T(8,128)(2,1)} async-done(((bf16[512,1024]{1,0:T(8,128)(2,1)}), bf16[128,1024]{1,0:T(8,128)(2,1)}) %reduce-scatter.2.cloned.1.call-update) | async-done | bytes 262160 | tf_op jit(solution)/shard_map/reduce_scatter | solution.py:549
  434.4 24.6 %shard_map.286 = (bf16[384,640]{1,0:T(8,128)(2,1)}, bf16[1536,640]{1,0:T(8,128)(2,1)}, bf16[1536,640]{1,0:T(8,128)(2,1)}) custom-call(bf16[384,1024]{1,0:T(8,128)(2,1)} %add_convert_fusion.6.q_ref, bf16[1536,2048]{1,0:T(8,128)(2,1)} %add_convert_fusion.k_ref.v_ref, bf16[1536,2048]{1,0:T(8,128)(2,1)} %add_convert_fusion.k_ref.v_ref, ...), custom_call_target="tpu_custom_call" | custom-call | flops 7549747200 | bytes 11698176 | tf_op jit(solution)/shard_map/pallas_call | solution.py:182
  463.7 15.9 %shard_map.287 = (bf16[384,384]{1,0:T(8,128)(2,1)}, bf16[1536,384]{1,0:T(8,128)(2,1)}, bf16[1536,384]{1,0:T(8,128)(2,1)}) custom-call(bf16[384,1024]{1,0:T(8,128)(2,1)} %add_convert_fusion.6.q_ref, bf16[1536,2048]{1,0:T(8,128)(2,1)} %add_convert_fusion.k_ref.v_ref, bf16[1536,2048]{1,0:T(8,128)(2,1)} %add_convert_fusion.k_ref.v_ref, ...), custom_call_target="tpu_custom_call" | custom-call | flops 4529848320 | bytes 7962624 | tf_op jit(solution)/shard_map/pallas_call | solution.py:182
  493.3 15.3 %shard_map.288 = (bf16[4,4096,128]{2,1,0:T(8,128)(2,1)}, bf16[4,4096,128]{2,1,0:T(8,128)(2,1)}) custom-call(s32[1]{0:T(128)} %bitcast.1.me_ref, bf16[1536,1024]{1,0:T(8,128)(2,1)} %copy-done.25, bf16[1536,3072]{1,0:T(8,128)(2,1)} %constant_dynamic-update-slice_fusion.2.keep_in.send_in, ...), custom_call_target="tpu_custom_call", output_to_operand_aliasing={{0}: (4, {}), {1}: (5, {})} | custom-call | flops 9663676416 | bytes 18874368 | tf_op jit(solution)/shard_map/pallas_call | solution.py:311
  517.6 7.3 %convolution_add_fusion.1 = f32[1536,1024]{1,0:T(8,128)} fusion(f32[1536,1024]{1,0:T(8,128)S(1)} %fusion.16, bf16[1536,1024]{1,0:T(8,128)(2,1)S(1)} %copy-done.27, bf16[1056,3072]{1,0:T(8,128)(2,1)} %shard_map.272), kind=kOutput, calls=%fused_computation.24 | convolution fusion | flops 3222798336 | bytes 17825792 | tf_op jit(solution)/shard_map/dot_general | solution.py:47
  547.3 25.3 %all-reduce.11.cloned.1.call-done = bf16[4096,128]{1,0:T(8,128)(2,1)} async-done(((bf16[4096,128]{1,0:T(8,128)(2,1)}), bf16[4096,128]{1,0:T(8,128)(2,1)}) %all-reduce.11.cloned.1.call-update) | async-done | bytes 1048592 | tf_op jit(solution)/shard_map/psum | solution.py:506
  599.2 10.4 %collective-permute-done.62 = bf16[1024,128]{1,0:T(8,128)(2,1)S(1)} collective-permute-done((bf16[1024,128]{1,0:T(8,128)(2,1)S(1)}, bf16[1024,128]{1,0:T(8,128)(2,1)S(1)}, u32[]{:S(2)}, u32[]{:S(2)}) %collective-permute-start.62) | collective-permute-done | bytes 262176 | tf_op jit(solution)/shard_map/ppermute | solution.py:364
  632.5 11.4 %collective-permute-done.64 = bf16[1024,128]{1,0:T(8,128)(2,1)S(1)} collective-permute-done((bf16[1024,128]{1,0:T(8,128)(2,1)S(1)}, bf16[1024,128]{1,0:T(8,128)(2,1)S(1)}, u32[]{:S(2)}, u32[]{:S(2)}) %collective-permute-start.64) | collective-permute-done | bytes 262176 | tf_op jit(solution)/shard_map/ppermute | solution.py:364
  658.0 9.8 %collective-permute-done.71 = bf16[1024,128]{1,0:T(8,128)(2,1)S(1)} collective-permute-done((bf16[1024,128]{1,0:T(8,128)(2,1)S(1)}, bf16[1024,128]{1,0:T(8,128)(2,1)S(1)}, u32[]{:S(2)}, u32[]{:S(2)}) %collective-permute-start.71) | collective-permute-done | bytes 262176 | tf_op jit(solution)/shard_map/ppermute | solution.py:364
  (504 shorter events, 342.9 us)
Async XLA Ops:
  7.2 78.4 %all-gather.6.cloned.1.call-start = ((), (), s32[]{:S(2)}) async-start(), calls=%async_computation.6 | async-start | bytes 3932160 | tf_op jit(solution)/shard_map/all_gather | solution.py:418
  7.9 103.5 %all-gather.4.cloned.1.call-start = ((), (), s32[]{:S(2)}) async-start(), calls=%async_computation.1 | async-start | bytes 1310720 | tf_op jit(solution)/shard_map/all_gather | solution.py:421
  48.6 30.9 %collective-permute-start.10 = (bf16[1024,640]{1,0:T(8,128)(2,1)S(1)}, bf16[1024,640]{1,0:T(8,128)(2,1)}, u32[]{:S(2)}, u32[]{:S(2)}) collective-permute-start(bf16[1024,640]{1,0:T(8,128)(2,1)S(1)} %pad_maximum_fusion.3.refs_0_), channel_id=1, source_target_pairs={{0,4},{1,5},{2,6},{3,7},{4,0},{5,1},{6,2},{7,3},{8,12},{9,13},{10,... | collective-permute-start | bytes 3932168 | tf_op jit(solution)/shard_map/ppermute | solution.py:211
  50.3 30.9 %collective-permute-start.9 = (bf16[1024,640]{1,0:T(8,128)(2,1)S(1)}, bf16[1024,640]{1,0:T(8,128)(2,1)}, u32[]{:S(2)}, u32[]{:S(2)}) collective-permute-start(bf16[1024,640]{1,0:T(8,128)(2,1)S(1)} %pad_maximum_fusion.3.refs_0_), channel_id=1, source_target_pairs={{0,2},{1,3},{2,0},{3,1},{4,6},{5,7},{6,4},{7,5},{8,10},{9,11},{10,... | collective-permute-start | bytes 3932168 | tf_op jit(solution)/shard_map/ppermute | solution.py:211
  51.1 344.0 %all-reduce.7.cloned.1.call-start = ((), (), s32[]{:S(2)}) async-start(), calls=%async_computation.2 | async-start | bytes 2097152 | tf_op jit(solution)/shard_map/psum | solution.py:506
  102.2 28.6 %collective-permute-start.15 = (bf16[1024,640]{1,0:T(8,128)(2,1)S(1)}, bf16[1024,640]{1,0:T(8,128)(2,1)}, u32[]{:S(2)}, u32[]{:S(2)}) collective-permute-start(bf16[1024,640]{1,0:T(8,128)(2,1)S(1)} %pad_maximum_fusion.3.refs_0_), channel_id=1, source_target_pairs={{0,1},{1,0},{2,3},{3,2},{4,5},{5,4},{6,7},{7,6},{8,9},{9,8},{10,11... | collective-permute-start | bytes 3932168 | tf_op jit(solution)/shard_map/ppermute | solution.py:211
  102.3 28.5 %collective-permute-start.16 = (bf16[1024,640]{1,0:T(8,128)(2,1)}, bf16[1024,640]{1,0:T(8,128)(2,1)}, u32[]{:S(2)}, u32[]{:S(2)}) collective-permute-start(bf16[1024,640]{1,0:T(8,128)(2,1)} %collective-permute-done.9.refs_1_), channel_id=1, source_target_pairs={{0,1},{1,0},{2,3},{3,2},{4,5},{5,4},{6,7},{7,6},{8,9},{9,8},{10,11... | collective-permute-start | bytes 3932168 | tf_op jit(solution)/shard_map/ppermute | solution.py:211
  133.8 39.5 %collective-permute-start.27 = (bf16[4096,128]{1,0:T(8,128)(2,1)}, bf16[4096,128]{1,0:T(8,128)(2,1)S(1)}, u32[]{:S(2)}, u32[]{:S(2)}) collective-permute-start(bf16[4096,128]{1,0:T(8,128)(2,1)} %refs_0_.1), channel_id=1, source_target_pairs={{0,2},{1,3},{2,0},{3,1},{4,6},{5,7},{6,4},{7,5},{8,10},{9,11},{10,... | collective-permute-start | bytes 3145736 | tf_op jit(solution)/shard_map/ppermute | solution.py:211
  134.8 38.9 %collective-permute-start.28 = (bf16[4096,128]{1,0:T(8,128)(2,1)}, bf16[4096,128]{1,0:T(8,128)(2,1)S(1)}, u32[]{:S(2)}, u32[]{:S(2)}) collective-permute-start(bf16[4096,128]{1,0:T(8,128)(2,1)} %refs_0_.1), channel_id=1, source_target_pairs={{0,4},{1,5},{2,6},{3,7},{4,0},{5,1},{6,2},{7,3},{8,12},{9,13},{10,... | collective-permute-start | bytes 3145736 | tf_op jit(solution)/shard_map/ppermute | solution.py:211
  338.7 68.0 %collective-permute-start.44 = (bf16[4,4096,128]{2,1,0:T(8,128)(2,1)}, bf16[4,4096,128]{2,1,0:T(8,128)(2,1)}, u32[]{:S(2)}, u32[]{:S(2)}) collective-permute-start(bf16[4,4096,128]{2,1,0:T(8,128)(2,1)} %get-tuple-element.278), channel_id=1, source_target_pairs={{0,1},{1,0},{2,3},{3,2},{4,5},{5,4},{6,7},{7,6},{8,9},{9,8},{10,11... | collective-permute-start | bytes 12582920 | tf_op jit(solution)/shard_map/ppermute | solution.py:211
  342.2 82.3 %reduce-scatter.2.cloned.1.call-start = ((), (), s32[]{:S(2)}) async-start(), calls=%async_computation.3 | async-start | bytes 1310720 | tf_op jit(solution)/shard_map/reduce_scatter | solution.py:549
  346.2 60.5 %collective-permute-start.43 = (bf16[2,2048,128]{2,1,0:T(8,128)(2,1)}, bf16[2,2048,128]{2,1,0:T(8,128)(2,1)}, u32[]{:S(2)}, u32[]{:S(2)}) collective-permute-start(bf16[2,2048,128]{2,1,0:T(8,128)(2,1)} %pad_maximum_fusion.7), channel_id=1, source_target_pairs={{0,4},{1,5},{2,6},{3,7},{4,0},{5,1},{6,2},{7,3},{8,12},{9,13},{10,... | collective-permute-start | bytes 3145736 | tf_op jit(solution)/shard_map/ppermute | solution.py:211
  348.8 57.9 %collective-permute-start.42 = (bf16[2,2048,128]{2,1,0:T(8,128)(2,1)}, bf16[2,2048,128]{2,1,0:T(8,128)(2,1)}, u32[]{:S(2)}, u32[]{:S(2)}) collective-permute-start(bf16[2,2048,128]{2,1,0:T(8,128)(2,1)} %pad_maximum_fusion.6), channel_id=1, source_target_pairs={{0,2},{1,3},{2,0},{3,1},{4,6},{5,7},{6,4},{7,5},{8,10},{9,11},{10,... | collective-permute-start | bytes 3145736 | tf_op jit(solution)/shard_map/ppermute | solution.py:211
  395.1 113.4 %all-reduce.9.cloned.1.call-start = ((), (), s32[]{:S(2)}) async-start(), calls=%async_computation.4 | async-start | bytes 2097152 | tf_op jit(solution)/shard_map/psum | solution.py:506
  428.3 30.7 %collective-permute-start.48 = (bf16[2,2048,128]{2,1,0:T(8,128)(2,1)S(1)}, bf16[2,2048,128]{2,1,0:T(8,128)(2,1)S(1)}, u32[]{:S(2)}, u32[]{:S(2)}) collective-permute-start(bf16[2,2048,128]{2,1,0:T(8,128)(2,1)S(1)} %pad_maximum_fusion.10), channel_id=1, source_target_pairs={{0,4},{1,5},{2,6},{3,7},{4,0},{5,1},{6,2},{7,3},{8,12},{9,13},{10,... | collective-permute-start | bytes 3145736 | tf_op jit(solution)/shard_map/ppermute | solution.py:211
  429.0 30.0 %collective-permute-start.47 = (bf16[2,2048,128]{2,1,0:T(8,128)(2,1)S(1)}, bf16[2,2048,128]{2,1,0:T(8,128)(2,1)}, u32[]{:S(2)}, u32[]{:S(2)}) collective-permute-start(bf16[2,2048,128]{2,1,0:T(8,128)(2,1)S(1)} %pad_maximum_fusion.9), channel_id=1, source_target_pairs={{0,2},{1,3},{2,0},{3,1},{4,6},{5,7},{6,4},{7,5},{8,10},{9,11},{10,... | collective-permute-start | bytes 3145736 | tf_op jit(solution)/shard_map/ppermute | solution.py:211
  434.3 138.2 %all-reduce.11.cloned.1.call-start = ((), (), s32[]{:S(2)}) async-start(), calls=%async_computation.5 | async-start | bytes 2097152 | tf_op jit(solution)/shard_map/psum | solution.py:506
  528.1 44.4 %collective-permute-start.59 = (bf16[2,2048,128]{2,1,0:T(8,128)(2,1)}, bf16[2,2048,128]{2,1,0:T(8,128)(2,1)}, u32[]{:S(2)}, u32[]{:S(2)}) collective-permute-start(bf16[2,2048,128]{2,1,0:T(8,128)(2,1)} %pad_maximum_fusion.13), channel_id=1, source_target_pairs={{0,4},{1,5},{2,6},{3,7},{4,0},{5,1},{6,2},{7,3},{8,12},{9,13},{10,... | collective-permute-start | bytes 3145736 | tf_op jit(solution)/shard_map/ppermute | solution.py:211
  529.7 42.9 %collective-permute-start.58 = (bf16[2,2048,128]{2,1,0:T(8,128)(2,1)}, bf16[2,2048,128]{2,1,0:T(8,128)(2,1)}, u32[]{:S(2)}, u32[]{:S(2)}) collective-permute-start(bf16[2,2048,128]{2,1,0:T(8,128)(2,1)} %pad_maximum_fusion.12), channel_id=1, source_target_pairs={{0,2},{1,3},{2,0},{3,1},{4,6},{5,7},{6,4},{7,5},{8,10},{9,11},{10,... | collective-permute-start | bytes 3145736 | tf_op jit(solution)/shard_map/ppermute | solution.py:211
  543.2 38.5 %collective-permute-start.52 = (bf16[384,1024]{1,0:T(8,128)(2,1)}, bf16[384,1024]{1,0:T(8,128)(2,1)}, u32[]{:S(2)}, u32[]{:S(2)}) collective-permute-start(bf16[384,1024]{1,0:T(8,128)(2,1)} %get-tuple-element.387), channel_id=1, source_target_pairs={{0,8},{1,9},{2,10},{3,11},{4,12},{5,13},{6,14},{7,15}} | collective-permute-start | bytes 2359304 | tf_op jit(solution)/shard_map/ppermute | solution.py:364
  580.9 33.3 %collective-permute-start.55 = (bf16[384,1024]{1,0:T(8,128)(2,1)S(1)}, bf16[384,1024]{1,0:T(8,128)(2,1)S(1)}, u32[]{:S(2)}, u32[]{:S(2)}) collective-permute-start(bf16[384,1024]{1,0:T(8,128)(2,1)S(1)} %copy-done.46), channel_id=1, source_target_pairs={{24,16},{25,17},{26,18},{27,19},{28,20},{29,21},{30,22},{31,23}} | collective-permute-start | bytes 2359304 | tf_op jit(solution)/shard_map/ppermute | solution.py:364
  583.6 30.6 %collective-permute-start.53 = (bf16[384,1024]{1,0:T(8,128)(2,1)S(1)}, bf16[384,1024]{1,0:T(8,128)(2,1)S(1)}, u32[]{:S(2)}, u32[]{:S(2)}) collective-permute-start(bf16[384,1024]{1,0:T(8,128)(2,1)S(1)} %fusion.52), channel_id=1, source_target_pairs={{0,8},{8,16},{1,9},{9,17},{2,10},{10,18},{3,11},{11,19},{4,12},{12... | collective-permute-start | bytes 2359304 | tf_op jit(solution)/shard_map/ppermute | solution.py:364
  619.5 49.6 %collective-permute-start.54 = (bf16[384,1024]{1,0:T(8,128)(2,1)S(1)}, bf16[384,1024]{1,0:T(8,128)(2,1)S(1)}, u32[]{:S(2)}, u32[]{:S(2)}) collective-permute-start(bf16[384,1024]{1,0:T(8,128)(2,1)S(1)} %get-tuple-element.385), channel_id=1, source_target_pairs={{0,8},{8,16},{16,24},{1,9},{9,17},{17,25},{2,10},{10,18},{18,26},{... | collective-permute-start | bytes 2359304 | tf_op jit(solution)/shard_map/ppermute | solution.py:364
  631.0 38.1 %collective-permute-start.57 = (bf16[384,1024]{1,0:T(8,128)(2,1)S(1)}, bf16[384,1024]{1,0:T(8,128)(2,1)S(1)}, u32[]{:S(2)}, u32[]{:S(2)}) collective-permute-start(bf16[384,1024]{1,0:T(8,128)(2,1)S(1)} %fusion.51), channel_id=1, source_target_pairs={{8,0},{16,8},{24,16},{9,1},{17,9},{25,17},{10,2},{18,10},{26,18},{... | collective-permute-start | bytes 2359304 | tf_op jit(solution)/shard_map/ppermute | solution.py:364
  (147 other events, 1991.7 us)
Sparse Core Ops, SparseCore 0:
  9.6 66.1 all-gather.5
  77.4 26.4 all-gather.3
  342.3 52.7 all-reduce.6
  397.9 26.5 reduce-scatter.1
  434.5 50.2 all-reduce.8
  512.4 60.0 all-reduce.10

commit v3 on v2

--- a/solution.py
+++ b/solution.py
@@ -13,6 +13,7 @@
 F32 = jnp.float32
 NEG = -1e30
 VMEM_LIMIT = 56 * 1024 * 1024
+SHORT = pl.CostEstimate(flops=0, bytes_accessed=0, transcendentals=0)
 
 
 def params(**kw):
@@ -49,6 +50,14 @@
 
 def dense_left(a, b):
     return lax.dot_general(a, b, (((0,), (0,)), ((), ())), preferred_element_type=F32)
+
+
+def gelu_both(u):
+    c = 0.7978845608028654
+    sq = u * u
+    t = jnp.tanh(c * u * (1.0 + 0.044715 * sq))
+    half = 0.5 * (1.0 + t)
+    return u * half, half + 0.5 * c * u * (1.0 - t * t) * (1.0 + 0.134145 * sq)
 
 
 def segment_ids(positions, lengths):
@@ -79,28 +88,27 @@
     return lax.dot_general(a, b, (((0,), (0,)), ((), ())), preferred_element_type=F32)
 
 
-def attn_fwd_kernel(scale, chunk, q_ref, k_ref, v_ref, bias_ref, o_ref, lse_ref, acc_ref, m_ref, l_ref):
+def attn_fwd_kernel(scale, chunk, q_ref, k_ref, v_ref, bias_ref, o_ref, lse_ref):
     both = split_heads(q_ref[...], scale)
-    acc_ref[...] = jnp.zeros_like(acc_ref)
-    m_ref[...] = jnp.full_like(m_ref, NEG)
-    l_ref[...] = jnp.zeros_like(l_ref)
-
-    @pl.loop(0, k_ref.shape[0] // chunk)
-    def _(c):
-        rows = pl.ds(pl.multiple_of(c * chunk, chunk), chunk)
+    top = jnp.full(lse_ref.shape[1:], NEG, F32)
+    total = jnp.zeros_like(top)
+    acc = None
+    for c in range(k_ref.shape[0] // chunk):
+        rows = slice(c * chunk, (c + 1) * chunk)
         b = bias_ref[rows, :]
         s = nt(k_ref[rows, :], both) + jnp.concatenate([b, b], axis=1)
-        m_old = m_ref[...]
-        m_new = jnp.maximum(m_old, jnp.max(s, axis=0, keepdims=True))
-        alpha = jnp.exp(m_old - m_new)
-        p = jnp.exp(s - m_new)
-        m_ref[...] = m_new
-        l_ref[...] = l_ref[...] * alpha + jnp.sum(p, axis=0, keepdims=True)
-        acc_ref[...] = acc_ref[...] * alpha + tn(v_ref[rows, :], p.astype(BF))
-
-    total = l_ref[...]
-    o_ref[...] = jnp.transpose(join_heads(acc_ref[...] / total)).astype(BF)
-    lse_ref[0] = m_ref[...] + jnp.log(total)
+        new = jnp.maximum(top, jnp.max(s, axis=0, keepdims=True))
+        p = jnp.exp(s - new)
+        part = tn(v_ref[rows, :], p.astype(BF))
+        if acc is None:
+            total, acc = jnp.sum(p, axis=0, keepdims=True), part
+        else:
+            alpha = jnp.exp(top - new)
+            total = total * alpha + jnp.sum(p, axis=0, keepdims=True)
+            acc = acc * alpha + part
+        top = new
+    o_ref[...] = jnp.transpose(join_heads(acc / total)).astype(BF)
+    lse_ref[0] = top + jnp.log(total)
 
 
 def attn_fwd(q, kv, bias, first=0, count=HEADS // 2):
@@ -108,7 +116,7 @@
     nk = kv.shape[0]
     head = width // HEADS
     pairs, pw = HEADS // 2, 2 * head
-    chunk = 256
+    chunk = 512
     return pl.pallas_call(
         functools.partial(attn_fwd_kernel, head**-0.5, chunk),
         grid=(count,),
@@ -126,85 +134,78 @@
             jax.ShapeDtypeStruct((nq, count * pw), BF),
             jax.ShapeDtypeStruct((count, 1, 2 * nq), F32),
         ],
-        scratch_shapes=[
-            pltpu.VMEM((pw, 2 * nq), F32),
-            pltpu.VMEM((1, 2 * nq), F32),
-            pltpu.VMEM((1, 2 * nq), F32),
-        ],
         compiler_params=params(),
-        cost_estimate=pl.CostEstimate(
-            flops=16 * count * nq * nk * head,
-            bytes_accessed=4 * nk * count * pw + 4 * nq * count * pw + 4 * nk * nq,
-            transcendentals=2 * count * nq * nk,
-        ),
+        cost_estimate=SHORT,
     )(q, kv, kv, bias)
 
 
-def attn_bwd_kernel(
-    scale, chunk, q_ref, k_ref, v_ref, do_ref, bias_ref, lse_ref, delta_ref, dq_ref, dk_ref, dv_ref, acc_ref
-):
+def attn_bwd_kernel(scale, chunk, padded, z_ref, q_ref, k_ref, v_ref, do_ref, out_ref, bias_ref, lse_ref, *refs):
+    dq_ref, dkv_ref = refs[-2:]
     both = split_heads(q_ref[...], scale)
     dboth = split_heads(do_ref[...], None)
-    acc_ref[...] = jnp.zeros_like(acc_ref)
     lse = lse_ref[0]
-    delta = delta_ref[0]
-
-    @pl.loop(0, k_ref.shape[0] // chunk)
-    def _(c):
-        rows = pl.ds(pl.multiple_of(c * chunk, chunk), chunk)
+    prod = do_ref[...].astype(F32) * out_ref[...].astype(F32)
+    head = prod.shape[1] // 2
+    lane = lax.broadcasted_iota(jnp.int32, (8, 2 * head), 1)
+    row = lax.broadcasted_iota(jnp.int32, (8, 2 * head), 0)
+    pick_head = jnp.where(lane // head == row, 1.0, 0.0)
+    delta = lax.dot_general(
+        pick_head, prod, (((1,), (1,)), ((), ())), precision=lax.Precision.HIGHEST, preferred_element_type=F32
+    )
+    delta = jnp.concatenate([delta[0:1], delta[1:2]], axis=1)
+    acc = 0.0
+    for c in range(k_ref.shape[0] // chunk):
+        rows = slice(c * chunk, (c + 1) * chunk)
         b = bias_ref[rows, :]
         k = k_ref[rows, :]
         p = jnp.exp(nt(k, both) + jnp.concatenate([b, b], axis=1) - lse)
         ds = (p * (nt(v_ref[rows, :], dboth) - delta)).astype(BF)
-        dk_ref[rows, :] = dense(ds, both).astype(BF)
-        dv_ref[rows, :] = dense(p.astype(BF), dboth).astype(BF)
-        acc_ref[...] += tn(k, ds)
-
-    dq_ref[...] = jnp.transpose(join_heads(acc_ref[...]) * scale).astype(BF)
-
-
-def attn_delta(out, dout):
-    nq, width = out.shape
-    delta = jnp.sum((dout.astype(F32) * out.astype(F32)).reshape(nq, HEADS, width // HEADS), axis=-1)
-    return delta.T.reshape(HEADS // 2, 1, 2 * nq)
-
-
-def attn_bwd(q, kv, bias, lse, delta, dout, first=0, count=HEADS // 2):
+        dkv_ref[padded, rows, :] = dense(ds, both).astype(BF)
+        dkv_ref[padded + 1, rows, :] = dense(p.astype(BF), dboth).astype(BF)
+        acc = acc + tn(k, ds)
+    dq = jnp.transpose(join_heads(acc) * scale).astype(BF)
+    dq_ref[...] = dq
+    if padded:
+        n = dq.shape[0]
+        dkv_ref[0] = jnp.zeros(dkv_ref.shape[1:], BF)
+        dkv_ref[0, pl.ds(pl.multiple_of(z_ref[0] * n, n), n), :] = dq
+
+
+def attn_bwd(z, q, kv, bias, lse, out, dout, padded, first=0, count=HEADS // 2, into=()):
     nq, width = q.shape
     nk = kv.shape[0]
     head = width // HEADS
     pairs, pw = HEADS // 2, 2 * head
-    chunk = 256
-    row_spec = pl.BlockSpec((nq, pw), lambda i: (0, first + i))
-    key_spec = pl.BlockSpec((nk, pw), lambda i: (0, first + i))
-    vec_spec = pl.BlockSpec((1, 1, 2 * nq), lambda i: (first + i, 0, 0))
-    new_spec = lambda n: pl.BlockSpec((n, pw), lambda i: (0, i))
+    chunk = 512
+    row_spec = pl.BlockSpec((nq, pw), lambda i, z_ref: (0, first + i))
+    key_spec = pl.BlockSpec((nk, pw), lambda i, z_ref: (0, first + i))
+    vec_spec = pl.BlockSpec((1, 1, 2 * nq), lambda i, z_ref: (first + i, 0, 0))
+    depth = 3 if padded else 2
     return pl.pallas_call(
-        functools.partial(attn_bwd_kernel, head**-0.5, chunk),
-        grid=(count,),
-        in_specs=[
-            row_spec,
-            key_spec,
-            pl.BlockSpec((nk, pw), lambda i: (0, pairs + first + i)),
-            row_spec,
-            pl.BlockSpec((nk, nq), lambda i: (0, 0)),
-            vec_spec,
-            vec_spec,
+        functools.partial(attn_bwd_kernel, head**-0.5, chunk, depth - 2),
+        grid_spec=pltpu.PrefetchScalarGridSpec(
+            num_scalar_prefetch=1,
+            grid=(count,),
+            in_specs=[
+                row_spec,
+                key_spec,
+                pl.BlockSpec((nk, pw), lambda i, z_ref: (0, pairs + first + i)),
+                row_spec,
+                row_spec,
+                pl.BlockSpec((nk, nq), lambda i, z_ref: (0, 0)),
+                vec_spec,
+            ]
+            + [pl.BlockSpec(memory_space=pl.ANY)] * len(into),
+            out_specs=[row_spec, pl.BlockSpec((depth, nk, pw), lambda i, z_ref: (0, 0, first + i))],
+        ),
+        out_shape=[
+            jax.ShapeDtypeStruct((nq, width), BF),
+            jax.ShapeDtypeStruct((depth, nk, width), BF),
         ],
-        out_specs=[new_spec(nq), new_spec(nk), new_spec(nk)],
-        out_shape=[
-            jax.ShapeDtypeStruct((nq, count * pw), BF),
-            jax.ShapeDtypeStruct((nk, count * pw), BF),
-            jax.ShapeDtypeStruct((nk, count * pw), BF),
-        ],
-        scratch_shapes=[pltpu.VMEM((pw, 2 * nq), F32)],
+        input_output_aliases={8: 0, 9: 1} if into else {},
         compiler_params=params(),
-        cost_estimate=pl.CostEstimate(
-            flops=40 * count * nq * nk * head,
-            bytes_accessed=8 * nk * count * pw + 6 * nq * count * pw + 4 * nk * nq,
-            transcendentals=2 * count * nq * nk,
-        ),
-    )(q, kv, kv, dout, bias, lse, delta)
+        cost_estimate=SHORT,
+    )(z, q, kv, kv, dout, out, bias, lse, *into)
 
 
 def swap(v, bit):
@@ -253,7 +254,7 @@
         ),
         out_shape=[jax.ShapeDtypeStruct((rows, 8 * n), BF) for n in widths],
         compiler_params=params(),
-        cost_estimate=pl.CostEstimate(flops=0, bytes_accessed=32 * rows * total, transcendentals=0),
+        cost_estimate=SHORT,
     )(me, *mine, *other)
 
 
@@ -281,51 +282,130 @@
     return parts, tuple(swap(v, 1) for v in parts)
 
 
-def wgrad_kernel(me_ref, x_ref, keep_in, send_in, *refs):
-    keep_ref, send_ref, xt_ref = refs[-3:]
-
-    @pl.when(pl.program_id(0) == 0)
-    def _():
-        xt_ref[...] = jnp.transpose(x_ref[...])
-
-    rows, n = xt_ref.shape[0], keep_in.shape[1]
-    res = dense(xt_ref[...], jnp.concatenate([keep_in[...], send_in[...]], axis=1))
-    for t, ref in enumerate((keep_ref, send_ref)):
-        for j in range(n // 128):
-            ref[0, j * rows : (j + 1) * rows] = res[:, t * n + j * 128 : t * n + (j + 1) * 128].astype(BF)
-
-
-def wgrad(me, x, dy, into=None, at=0, whole=None):
-    tok, rows = x.shape
-    n = dy.shape[1] // 8
-    stacked = n // 128 * rows
-    col = lambda t: lambda i, me_ref: (0, jnp.bitwise_xor(me_ref[0], 2 * i + t))
-    out_spec = pl.BlockSpec((1, stacked, 128), lambda i, me_ref: (i, at, 0))
-    in_specs = [
-        pl.BlockSpec((tok, rows), lambda i, me_ref: (0, 0)),
-        pl.BlockSpec((tok, n), col(0)),
-        pl.BlockSpec((tok, n), col(1)),
-    ]
-    extra = () if into is None else tuple(into)
-    height = extra[0].shape[1] if extra else whole or stacked
+def wgrad_kernel(counts, me_ref, *refs):
+    keep_ref, send_ref = refs[-2 - len(counts) : -len(counts)]
+    scratch = refs[-len(counts) :]
+    at = first = 0
+    for blocks, xt_ref in zip(counts, scratch):
+        x_ref = refs[at]
+        keep_in = [r[0] for r in refs[at + 1 : at + 1 + blocks]]
+        send_in = [r[0] for r in refs[at + 1 + blocks : at + 1 + 2 * blocks]]
+        at += 1 + 2 * blocks
+
+        @pl.when(pl.program_id(0) == 0)
+        def _():
+            xt_ref[...] = jnp.transpose(x_ref[...])
+
+        rows = xt_ref.shape[0]
+        res = dense(xt_ref[...], jnp.concatenate(keep_in + send_in, axis=1))
+        wide = res.shape[1] // 256
+        for t, ref in enumerate((keep_ref, send_ref)):
+            for j in range(wide):
+                col = (t * wide + j) * 128
+                ref[0, first + j * rows : first + (j + 1) * rows] = res[:, col : col + 128].astype(BF)
+        first += wide * rows
+
+
+def wgrad(me, *products):
+    in_specs, operands, counts, scratch = [], [], [], []
+    height = flops = moved = 0
+    for x, dy in products:
+        tok, rows = x.shape
+        parts, _, cols = dy.shape
+        n = parts * cols // 8
+        width = n if parts == 1 else 128
+        per = cols // width
+        blocks = n // width
+        in_specs.append(pl.BlockSpec((tok, rows), lambda i, me_ref: (0, 0)))
+        operands.append(x)
+        for t in (0, 1):
+            for j in range(blocks):
+
+                def place(i, me_ref, t=t, j=j, blocks=blocks, per=per):
+                    b = jnp.bitwise_xor(me_ref[0], 2 * i + t) * blocks + j
+                    return (b // per, 0, b % per)
+
+                in_specs.append(pl.BlockSpec((1, tok, width), place))
+                operands.append(dy)
+        counts.append(blocks)
+        scratch.append(pltpu.VMEM((rows, tok), BF))
+        height += n // 128 * rows
+        flops += 2 * tok * rows * 8 * n
+        moved += 2 * (tok * rows + tok * 8 * n + rows * 8 * n)
+    out_spec = pl.BlockSpec((1, height, 128), lambda i, me_ref: (i, 0, 0))
     return pl.pallas_call(
-        wgrad_kernel,
+        functools.partial(wgrad_kernel, tuple(counts)),
         grid_spec=pltpu.PrefetchScalarGridSpec(
             num_scalar_prefetch=1,
             grid=(4,),
-            in_specs=in_specs + [pl.BlockSpec(memory_space=pl.ANY)] * len(extra),
+            in_specs=in_specs,
             out_specs=[out_spec, out_spec],
-            scratch_shapes=[pltpu.VMEM((rows, tok), BF)],
+            scratch_shapes=scratch,
         ),
         out_shape=[jax.ShapeDtypeStruct((4, height, 128), BF)] * 2,
-        input_output_aliases={4: 0, 5: 1} if extra else {},
         compiler_params=params(),
-        cost_estimate=pl.CostEstimate(
-            flops=2 * tok * rows * 8 * n,
-            bytes_accessed=2 * (tok * rows + tok * 8 * n + rows * 8 * n),
-            transcendentals=0,
-        ),
-    )(me, x, dy, dy, *extra)
+        cost_estimate=SHORT,
+    )(me, *operands)
+
+
+def gelu_grad_kernel(dz_ref, w_ref, slope_ref, du_ref):
+    du_ref[...] = (nt(dz_ref[...], w_ref[...]) * slope_ref[...].astype(F32)).astype(BF)
+
+
+def gelu_grad(dz, w, slope):
+    rows, width = dz.shape
+    hidden = w.shape[0]
+    block = 512
+    wide = pl.BlockSpec((rows, block), lambda i: (0, i))
+    return pl.pallas_call(
+        gelu_grad_kernel,
+        grid=(hidden // block,),
+        in_specs=[
+            pl.BlockSpec((rows, width), lambda i: (0, 0)),
+            pl.BlockSpec((block, width), lambda i: (i, 0)),
+            wide,
+        ],
+        out_specs=wide,
+        out_shape=jax.ShapeDtypeStruct((rows, hidden), BF),
+        compiler_params=params(),
+        cost_estimate=SHORT,
+    )(dz, w, slope)
+
+
+def kv_grad_kernel(dk_ref, dv_ref, wk_ref, wv_ref, x_ref, part_ref, sums_ref):
+    part = nt(dk_ref[0], wk_ref[...]) + nt(dv_ref[0], wv_ref[...])
+    part_ref[0] = part.astype(BF)
+    _, normed, _ = layer_norm(x_ref[...].astype(F32), 1.0, 0.0)
+
+    @pl.when(pl.program_id(0) == 0)
+    def _():
+        sums_ref[...] = jnp.zeros_like(sums_ref)
+
+    sums_ref[0:1] += jnp.sum(part * normed, axis=0, keepdims=True)
+    sums_ref[1:2] += jnp.sum(part, axis=0, keepdims=True)
+
+
+def kv_grad(dqkv, w, x, n):
+    _, rows, width = dqkv.shape
+    block = rows // n
+    return pl.pallas_call(
+        kv_grad_kernel,
+        grid=(n,),
+        in_specs=[
+            pl.BlockSpec((1, block, width), lambda i: (1, i, 0)),
+            pl.BlockSpec((1, block, width), lambda i: (2, i, 0)),
+            pl.BlockSpec((width, width), lambda i: (0, 1)),
+            pl.BlockSpec((width, width), lambda i: (0, 2)),
+            pl.BlockSpec((block, width), lambda i: (i, 0)),
+        ],
+        out_specs=[
+            pl.BlockSpec((1, block, width), lambda i: (i, 0, 0)),
+            pl.BlockSpec((8, width), lambda i: (0, 0)),
+        ],
+        out_shape=[jax.ShapeDtypeStruct((n, block, width), BF), jax.ShapeDtypeStruct((8, width), F32)],
+        compiler_params=params(),
+        cost_estimate=SHORT,
+    )(dqkv, dqkv, w, w, x)
 
 
 def add(*terms):
@@ -343,16 +423,15 @@
 def sum_near(keep, got, *wait):
     keep, got = all_after((keep, got), *wait)
     term = lambda i, h: add(pick(keep, i, h), pick(got, i, h))
-    xa = swap(jnp.stack([term(1, 0), term(3, 0)]), 2)
-    yb = swap(jnp.stack([term(2, 1), term(3, 1)]), 4)
-    return xa, yb
+    xa, yb = jnp.stack([term(1, 0), term(3, 0)]), jnp.stack([term(2, 1), term(3, 1)])
+    return (swap(xa, 2), swap(yb, 4)), (xa, yb)
 
 
 def sum_far(keep, got, near, *wait):
     xa, yb, keep, got = all_after(tuple(near) + (keep, got), *wait)
-    ya = swap(add(pick(keep, 2, 0), pick(got, 2, 0), xa[1]), 4)
-    xb = swap(add(pick(keep, 1, 1), pick(got, 1, 1), yb[1]), 2)
-    return ya, xb
+    ya = add(pick(keep, 2, 0), pick(got, 2, 0), xa[1])
+    xb = add(pick(keep, 1, 1), pick(got, 1, 1), yb[1])
+    return (swap(ya, 4), swap(xb, 2)), (ya, xb)
 
 
 def sum_own(keep, got, near, far):
@@ -381,16 +460,30 @@
     return jnp.concatenate(out, axis=0)
 
 
-def scatter_rows(v, z, n):
+def scatter_rows(v, z, n, wait=()):
     part = lambda t: lax.dynamic_index_in_dim(v, jnp.clip(t, 0, n - 1), 0, keepdims=False).astype(F32)
     r = l = None
     for p in range(1, n):
         rv, lv = part(n - p + z), part(p - n + z)
         if r is not None:
+            r, l = all_after((r, l), *wait)
             rv, lv = rv + r.astype(F32), lv + l.astype(F32)
         r = shift(rv.astype(BF), n, 1, range(0, p))
         l = shift(lv.astype(BF), n, -1, range(n - p, n))
     return part(z) + r.astype(F32) + l.astype(F32)
+
+
+def twin(v, bit):
+    return lax.ppermute(v, "seq", [(i, i ^ bit) for i in range(4)])
+
+
+def take_part(v, at, count):
+    rows = v.shape[0] // count
+    return lax.dynamic_slice_in_dim(v, at * rows, rows)
+
+
+def in_order(mine, other, bit):
+    return jnp.where(bit == 0, jnp.concatenate([mine, other]), jnp.concatenate([other, mine]))
 
 
 def local(
@@ -493,8 +586,8 @@
     v3, xh3, rs3 = layer_norm(h2, gain[2], shift_v[2])
     a3 = v3.astype(BF)
     up = dense(a3, w_up) + up_bias
-    gelu, gelu_back = jax.vjp(lambda u: jax.nn.gelu(u, approximate=True), up)
-    gelu_h = gelu.astype(BF)
+    gelu, slope = gelu_both(up)
+    gelu_h, slope = gelu.astype(BF), slope.astype(BF)
     if fast:
         d_parts = all_after(d_parts, gelu_h)
         (w_down,) = assemble(me, d_parts, d_other, (shard,))
@@ -503,20 +596,27 @@
 
     total = lambda v: jnp.sum(v, axis=0, dtype=F32)
     by_columns = lambda a, b: lax.psum_scatter(dense_left(a, b), "dp", scatter_dimension=1, tiled=True).astype(BF)
-    by_chain = lambda v: lax.psum(v, "seq")
     ct = cotangent[0].astype(F32)
     g3, s3 = norm_sums(xh4, ct)
     dh3 = norm_input_grad(xh4, rs4, gain[3], ct)
     dz = dh3.astype(BF)
-    if fast:
-        d_keep, d_send = wgrad(me, gelu_h, dz)
+    z_row = z.astype(jnp.int32).reshape(1)
+
+    def by_chain(v, turn=0):
+        listed = [(turn + i) % n_seq for i in range(n_seq)]
+        return lax.psum(v, "seq", axis_index_groups=[listed])
+
+    if fast:
+        dz, gelu_h = all_after((dz, gelu_h))
+        d_keep, d_send = wgrad(me, (gelu_h, dz[None]))
         dz, d_keep, d_send = all_after((dz, d_keep, d_send))
         d_got = swap(d_send, 1)
-    du = gelu_back(dense_t(dz, w_down))[0].astype(BF)
+    du = gelu_grad(dz, w_down, slope)
     if fast:
         du, d_got = all_after((du, d_got))
-        d_n = sum_near(d_keep, d_got, du)
-        c_keep, c_send = wgrad(me, a3, du)
+        d_n, sent = sum_near(d_keep, d_got, du)
+        du, *_ = all_after((du,), *sent)
+        c_keep, c_send = wgrad(me, (a3, du[None]))
         du, c_send = all_after((du, c_send))
         c_got = swap(c_send, 1)
     c3 = dense_t(du, w_up)
@@ -525,96 +625,113 @@
     dc = dh2.astype(BF)
     if fast:
         dc, c_got = all_after((dc, c_got))
-        e_rows = (2 * shard + cross_kv.shape[1]) // 128 * width
-        e_grads = wgrad(me, cattn, dc, None, 0, e_rows)
-        dc, *e_grads = all_after((dc, *e_grads))
     dcattn = dense_t(dc, w_cout).astype(BF)
-    cdelta = attn_delta(cattn, dcattn)
-    if fast:
-        dcattn, cdelta = all_after((dcattn, cdelta), *d_n)
-        d_f = sum_far(d_keep, d_got, d_n, dcattn)
-    dcq, dke, dve = attn_bwd(cq, ekv, cross_bias, clse, cdelta, dcattn)
-    dekv = jnp.concatenate([dke, dve], axis=1)
+    if fast:
+        dcattn, *_ = all_after((dcattn,), *d_n)
+        d_f, sent = sum_far(d_keep, d_got, d_n, dcattn)
+        dcattn = after(dcattn, *sent)
+    dcq, dekv = attn_bwd(z_row, cq, ekv, cross_bias, clse, cattn, dcattn, False)
     if fast:
         dcq, dekv = all_after((dcq, dekv), *d_f)
-        c_n = sum_near(c_keep, c_got, dcq)
-        e_grads = wgrad(me, a2, dcq, e_grads, 1)
-        e_keep, e_send = wgrad(me, states, dekv, e_grads, 1)
-        dcq, dekv, e_keep, e_send = all_after((dcq, dekv, e_keep, e_send))
+        c_n, sent = sum_near(c_keep, c_got, dcq)
+        d_sum = sum_own(d_keep, d_got, d_n, d_f)
+        low, high = z % 2, z // 2
+        d_other = take_part(d_sum, 1 - low, 2)
+        dcq, dekv, *_ = all_after((dcq, dekv), d_other, *sent)
+        d_got_a = twin(d_other, 1)
+        e_keep, e_send = wgrad(me, (cattn, dc[None]), (a2, dcq[None]), (states, dekv))
+        dcq, dekv, e_keep, e_send, d_got_a = all_after((dcq, dekv, e_keep, e_send, d_got_a), *c_n)
+        d_half = add(take_part(d_sum, low, 2), d_got_a)
+        d_other = take_part(d_half, 1 - high, 2)
+        dcq = after(dcq, d_other)
+        d_got_b = twin(d_other, 2)
         e_got = swap(e_send, 1)
-        d_all = by_chain(sum_own(d_keep, d_got, d_n, d_f))
-        enc_part = dense_t(dekv, w_ckv).astype(BF)
-        dcq, enc_part = all_after((dcq, enc_part))
-        enc_part = after(enc_part, d_all)
-        enc_sum = lax.psum_scatter(enc_part, "seq", scatter_dimension=0, tiled=True)
-        enc_grad = enc_sum.astype(F32)
+        c_f, sent = sum_far(c_keep, c_got, c_n, dcq)
+        dcq = after(dcq, *sent)
+    enc_part = dense_t(dekv[0], w_ckv[:, :width]) + dense_t(dekv[1], w_ckv[:, width:])
+    if fast:
+        enc_part = enc_part.astype(BF)
+        dcq = after(dcq, enc_part)
     c2 = dense_t(dcq, w_cq)
     g1, s1 = norm_sums(xh2, c2)
     dh1 = dh2 + norm_input_grad(xh2, rs2, gain[1], c2)
     da = dh1.astype(BF)
     if fast:
-        i_rows = (shard + attn_in.shape[1]) // 128 * width
-        i_grads = wgrad(me, attn, da, None, attn_in.shape[1] // 128, i_rows)
-        da, *i_grads = all_after((da, *i_grads), *c_n, e_got)
-        c_f = sum_far(c_keep, c_got, c_n, da)
+        da, e_got = all_after((da, e_got))
     dattn = dense_t(da, w_out).astype(BF)
-    delta = attn_delta(attn, dattn)
-    if fast:
-        dattn, delta = all_after((dattn, delta), *c_f, enc_sum)
-        e_n = sum_near(e_keep, e_got, dattn)
+    if fast:
+        dattn, d_got_b = all_after((dattn, d_got_b), *c_f)
+        d_quarter = add(take_part(d_half, high, 2), d_got_b)
+        e_n, sent = sum_near(e_keep, e_got, dattn)
         c_sum = sum_own(c_keep, c_got, c_n, c_f)
-        c_all = by_chain(after(c_sum, enc_sum))
-    dq_a, dk_a, dv_a = attn_bwd(q, kv, self_bias, lse, delta, dattn, 0, 5)
-    if fast:
-        dattn, dq_a, dk_a, dv_a = all_after((dattn, dq_a, dk_a, dv_a), *e_n)
-        e_f = sum_far(e_keep, e_got, e_n, dattn)
-    dq_b, dk_b, dv_b = attn_bwd(q, kv, self_bias, lse, delta, dattn, 5, 3)
-    if fast:
-        dq_b, dk_b, dv_b = all_after((dq_b, dk_b, dv_b), *e_f)
+        c_all = by_chain(c_sum, 1)
+        dattn = after(dattn, c_sum, d_quarter, *sent)
+        d_got_c = twin(d_quarter, 2)
+    dq, dqkv = attn_bwd(z_row, q, kv, self_bias, lse, attn, dattn, True, 0, 5)
+    if fast:
+        enc_sum = lax.psum_scatter(enc_part, "seq", scatter_dimension=0, tiled=True)
+        dattn, dq, dqkv, d_got_c = all_after((dattn, dq, dqkv, d_got_c), *e_n, enc_sum)
+        d_half = in_order(d_quarter, d_got_c, high)
+        e_f, sent = sum_far(e_keep, e_got, e_n, dattn)
+        dattn = after(dattn, d_half, *sent)
+        d_got_d = twin(d_half, 1)
+    dq, dqkv = attn_bwd(z_row, q, kv, self_bias, lse, attn, dattn, True, 5, 3, (dq, dqkv))
+    if fast:
+        dq, dqkv, d_got_d = all_after((dq, dqkv, d_got_d), *e_f)
+        d_all = in_order(d_half, d_got_d, low)
         e_sum = sum_own(e_keep, e_got, e_n, e_f)
-        e_all = by_chain(after(e_sum, c_all))
-    dq, dk, dv = (jnp.concatenate(p, axis=1) for p in ((dq_a, dq_b), (dk_a, dk_b), (dv_a, dv_b)))
-    dq_rows = lax.dynamic_update_slice(jnp.zeros((group_rows, width), BF), dq, (z * rows, 0))
-    dqkv = jnp.concatenate([dq_rows, dk, dv], axis=1)
-    if fast:
-        i_keep, i_send = wgrad(me, a1_full, dqkv, i_grads, 0)
-        dq, dk, dv, i_keep, i_send = all_after((dq, dk, dv, i_keep, i_send), c_all)
+        e_all = by_chain(e_sum, 2)
+        dqkv = after(dqkv, e_sum)
+        i_keep, i_send = wgrad(me, (attn, da[None]), (a1_full, dqkv))
+        dq, dqkv, i_keep, i_send = all_after((dq, dqkv, i_keep, i_send), c_all)
         i_got = swap(i_send, 1)
-    c1_part = dense_t(dk, w_in[:, width : 2 * width]) + dense_t(dv, w_in[:, 2 * width :])
-    c1_q = dense_t(dq, w_in[:, :width])
-    if fast:
-        c1_part, i_got = all_after((c1_part, i_got))
-        c1_sum = scatter_rows(c1_part.astype(BF).reshape(n_seq, rows, width), z, n_seq)
-        i_n = sum_near(i_keep, i_got)
-        i_f = sum_far(i_keep, i_got, i_n, e_all)
-        i_sum = scatter_rows(sum_own(i_keep, i_got, i_n, i_f).reshape(n_seq, -1, 128), z, n_seq)
-        i_all = gather_rows(i_sum.astype(BF), z, n_seq)
+    if fast:
+        c1_part, c1_sums = kv_grad(dqkv, first, x_full, n_seq)
+        c1_part, c1_sums, i_got = all_after((c1_part, c1_sums, i_got))
+        i_n, sent = sum_near(i_keep, i_got)
+        c1_part = after(c1_part, *sent)
+        c1_q = dense_t(dq, w_in[:, :width])
+        g0, s0 = (a + b for a, b in zip((c1_sums[0], c1_sums[1]), norm_sums(xh1, c1_q)))
+        c1_q = after(c1_q, g0, s0)
+    else:
+        c1_part = dense_t(dqkv[1], w_in[:, width : 2 * width]) + dense_t(dqkv[2], w_in[:, 2 * width :])
+        c1_q = dense_t(dq, w_in[:, :width])
+        _, xh1_full, _ = layer_norm(xf, gain[0], shift_v[0])
+        g0, s0 = (a + b for a, b in zip(norm_sums(xh1_full, c1_part), norm_sums(xh1, c1_q)))
+
+    bias_rows = [total(dq), total(dqkv[2]), total(dh1), total(dcq), total(dekv[1]), total(dh2), total(dh3)]
+    small_rows = jnp.stack(bias_rows + [g0, g1, g2, g3, s0, s1, s2, s3])
+    small_rows = small_rows.reshape(-1, n_dp, shard).transpose(1, 0, 2)
+    small_rows = jnp.concatenate([small_rows, total(du).reshape(n_dp, -1, shard)], axis=1)
+    dh1, c1_q = all_after((dh1, c1_q), small_rows)
+    if fast:
+        c1_sum = scatter_rows(c1_part, z, n_seq)
+        i_f, _ = sum_far(i_keep, i_got, i_n)
+        i_sum = after(sum_own(i_keep, i_got, i_n, i_f), e_all)
+        i_all = by_chain(i_sum, 3)
+        e_all, c_all, d_all = all_after((e_all, c_all, d_all), i_sum)
+        enc_grad = enc_sum.astype(F32)
         c1 = c1_sum + c1_q
         flat_out = lambda v, r: jnp.concatenate(jnp.split(v, v.shape[0] // r, axis=0), axis=1).astype(F32)
         r_up, r_down = flat_out(c_all, width), d_all.astype(F32)
-        r_in, r_out = flat_out(i_all[:-width], width), i_all[-width:].astype(F32)
+        r_in, r_out = flat_out(i_all[width:], width), i_all[:width].astype(F32)
         r_cout, r_cq, r_ckv = (flat_out(v, width) for v in jnp.split(e_all, [width, 2 * width], axis=0))
     else:
         c1 = lax.psum_scatter(c1_part, "seq", scatter_dimension=0, tiled=True) + c1_q
-        enc_grad = lax.psum_scatter(dense_t(dekv, w_ckv), "seq", scatter_dimension=0, tiled=True)
-        pairs = [(a1_full, dqkv), (attn, da), (a2, dcq), (states, dekv), (cattn, dc), (a3, du), (gelu_h, dz)]
+        enc_grad = lax.psum_scatter(enc_part, "seq", scatter_dimension=0, tiled=True)
+        flat = lambda v: jnp.concatenate(list(v), axis=1)
+        pairs = [(a1_full, flat(dqkv)), (attn, da), (a2, dcq), (states, flat(dekv)), (cattn, dc), (a3, du), (gelu_h, dz)]
         grads = [by_chain(by_columns(a, b)).astype(F32) for a, b in pairs]
         r_in, r_out, r_cq, r_ckv, r_cout, r_up, r_down = grads
-    tokens_grad = dh1 + norm_input_grad(xh1, rs1, gain[0], c1)
-    _, xh1_full, _ = layer_norm(xf, gain[0], shift_v[0])
-    g0, s0 = (a + b for a, b in zip(norm_sums(xh1_full, c1_part), norm_sums(xh1, c1_q)))
-
-    bias_rows = [total(dq), total(dv), total(dh1), total(dcq), total(dve), total(dh2), total(dh3)]
-    small_rows = jnp.stack(bias_rows + [g0, g1, g2, g3, s0, s1, s2, s3])
-    small_rows = small_rows.reshape(-1, n_dp, shard).transpose(1, 0, 2)
-    small_rows = jnp.concatenate([small_rows, total(du).reshape(n_dp, -1, shard)], axis=1)
-    if fast:
+    if fast:
+        small_rows = after(small_rows, i_sum)
         for bit in (1, 2, 4):
             small_rows = small_rows + swap(small_rows, bit)
         for bit in (1, 2):
             small_rows = small_rows + lax.ppermute(small_rows, "seq", [(i, i ^ bit) for i in range(n_seq)])
     else:
         small_rows = lax.psum(small_rows, ("dp", "seq"))
+    tokens_grad = dh1 + norm_input_grad(xh1, rs1, gain[0], c1)
     small_own = lax.dynamic_index_in_dim(small_rows, dp, 0, keepdims=False)
     return (
         out.astype(BF)[None],

time: 720 us -> 644 us (0.89)
  matrix products: 91.3 us -> 63.6 us
  starting transfers between devices: 94 us -> 75.1 us
  waiting for transfers between devices: 179 us -> 165 us
  local copies, waits for them, and re-layouts: 35.7 us -> 27 us
    psum x3, waiting for transfers between devices: 67.1 us -> 25.2 us  [by_chain(): return lax.psum(v, 'seq', axis_index_groups=[listed])]
    dot_general x9 -> x7, matrix products: 49.8 us -> 22.5 us  [dense_t(): lax.dot_general(a, b, (((1,), (1,)), ((), ())), preferred_element_type=F32)]
    ppermute x18 -> x6, starting transfers between devices: 42.7 us -> 18.3 us  [shift(): lax.ppermute(v, 'seq', [(a, a + step) for a in pairs if 0 <= a + step < n])]
    ppermute x2, waiting for transfers between devices: 2 us -> 23.3 us  [local(): lax.ppermute(small_rows, 'seq', [(i, i ^ bit) for i in range(n_seq)])]
    pallas_call x3, Pallas kernels: 52.7 us -> 32.6 us  [attn_fwd(): pl.pallas_call(functools.partial(attn_fwd_kernel, head ** (-0.5), chunk),...]
    all_gather x1, waiting for transfers between devices: 0.01 us -> 18.8 us  [local(): lax.all_gather(after(enc_states[0], x_full), 'seq', axis=0, tiled=True)]
    pallas_call x10 -> x9, Pallas kernels: 109 us -> 125 us  [the longest x4 53.2 us: wgrad(): pl.pallas_call(functools.partial(wgrad_kernel, tuple(counts)), grid_spec=...]
    ppermute x18 -> x6, waiting for transfers between devices: 39.4 us -> 26.7 us  [shift(): lax.ppermute(v, 'seq', [(a, a + step) for a in pairs if 0 <= a + step < n])]
  transfers between devices with their start and end apart: 85 -> 77, of which waited for: 32 -> 23; matrix products, arithmetic and copies ran while one was open for 28% -> 23% of each run, Pallas kernels for 22% -> 25%
where the time goes in v3:
time: 644 us; the launch traced here: 636 us
  Pallas kernels  190 us (30%)
  waiting for transfers between devices  165 us (26%)
  other arithmetic  98.9 us (15%)
  starting transfers between devices  75.1 us (12%)
  matrix products  63.6 us (10%)
  local copies, waits for them, and re-layouts  27 us (4%)
  between operations  16 us (2%)
    ppermute x59, waiting for transfers between devices, swap(): return lax.ppermute(v, 'dp', [(i, i ^ bit) for i in range(8)])  70.2 us
    pallas_call x4, Pallas kernels, wgrad(): pl.pallas_call(functools.partial(wgrad_kernel, tuple(counts)), grid_spec=...  53.2 us
    pallas_call x3, Pallas kernels, attn_bwd(): pl.pallas_call(functools.partial(attn_bwd_kernel, head ** (-0.5), chunk,...  47.6 us
    ppermute x59, starting transfers between devices, swap(): return lax.ppermute(v, 'dp', [(i, i ^ bit) for i in range(8)])  44.4 us
    dot_general x8, matrix products, dense(): return jnp.dot(a, b, preferred_element_type=F32)  41.2 us
    convert_element_type x14, other arithmetic, add(): return total.astype(BF)  33.9 us
    pallas_call x3, Pallas kernels, attn_fwd(): pl.pallas_call(functools.partial(attn_fwd_kernel, head ** (-0.5), chunk),...  32.6 us
    pallas_call x4, Pallas kernels, assemble(): pl.pallas_call(functools.partial(assemble_kernel, widths), grid_spec=pltp...  32.1 us
  transfers between devices with their start and end apart: 77, of which 23 were waited for; matrix products, arithmetic and copies ran while one was open for 23% of the time, Pallas kernels for 25%

profile of v3, /device:TPU:0, one launch (start us, length us, event | category | flops | bytes accessed | tf_op | source)
XLA Modules:
  0.0 635.7 jit_solution(10883923078560218934)
XLA Ops:
  15.3 16.7 %collective-permute-done.refs_1_ = bf16[1056,384]{1,0:T(8,128)(2,1)} collective-permute-done((bf16[1056,384]{1,0:T(8,128)(2,1)S(1)}, bf16[1056,384]{1,0:T(8,128)(2,1)}, u32[]{:S(2)}, u32[]{:S(2)}) %collective-permute-start) | collective-permute-done | bytes 811040 | tf_op jit(solution)/shard_map/ppermute | solution.py:212
  61.2 18.2 %collective-permute-done.9.refs_1_ = bf16[1024,640]{1,0:T(8,128)(2,1)S(1)} collective-permute-done((bf16[1024,640]{1,0:T(8,128)(2,1)S(1)}, bf16[1024,640]{1,0:T(8,128)(2,1)S(1)}, u32[]{:S(2)}, u32[]{:S(2)}) %collective-permute-start.9) | collective-permute-done | bytes 1310752 | tf_op jit(solution)/shard_map/ppermute | solution.py:212
  92.4 8.7 %add_convert_fusion.k_ref.v_ref = bf16[1536,2048]{1,0:T(8,128)(2,1)} fusion(bf16[1536,1024]{1,0:T(8,128)(2,1)S(1)} %fusion.5.refs_3_, f32[2048]{0:T(1024)S(1)} %concatenate.64, bf16[1056,3072]{1,0:T(8,128)(2,1)S(1)} %bitcast.257), kind=kOutput, calls=%fused_computation | convolution fusion | flops 6448742400 | bytes 13639680 | tf_op jit(solution)/shard_map/dot_general | solution.py:44
  112.4 18.8 %all-gather.4.cloned.1.call-done.refs_6_ = bf16[512,1024]{1,0:T(8,128)(2,1)} async-done(((bf16[128,1024]{1,0:T(8,128)(2,1)}), bf16[512,1024]{1,0:T(8,128)(2,1)}) %all-gather.4.cloned.1.call-update) | async-done | bytes 1048592 | tf_op jit(solution)/shard_map/all_gather | solution.py:514
  131.1 11.2 %shard_map.273 = (bf16[384,512]{1,0:T(8,128)(2,1)}, f32[4,1,768]{2,1,0:T(1,128)}) custom-call(bf16[384,1024]{1,0:T(8,128)(2,1)} %add_convert_fusion.8.q_ref, bf16[1536,2048]{1,0:T(8,128)(2,1)} %add_convert_fusion.k_ref.v_ref, bf16[1536,2048]{1,0:T(8,128)(2,1)} %add_convert_fusion.k_ref.v_ref, f32[1536,384]{1,0:T(8,128)} %and_select_fusion.bias_ref), custom_call_target="tpu_custom_call" | custom-call | tf_op jit(solution)/shard_map/pallas_call | solution.py:120
  148.4 11.2 %shard_map.274 = (bf16[384,512]{1,0:T(8,128)(2,1)}, f32[4,1,768]{2,1,0:T(1,128)}) custom-call(bf16[384,1024]{1,0:T(8,128)(2,1)} %add_convert_fusion.8.q_ref, bf16[1536,2048]{1,0:T(8,128)(2,1)} %add_convert_fusion.k_ref.v_ref, bf16[1536,2048]{1,0:T(8,128)(2,1)} %add_convert_fusion.k_ref.v_ref, f32[1536,384]{1,0:T(8,128)} %and_select_fusion.bias_ref), custom_call_target="tpu_custom_call" | custom-call | tf_op jit(solution)/shard_map/pallas_call | solution.py:120
  162.8 8.1 %shard_map.275 = (bf16[1024,2048]{1,0:T(8,128)(2,1)}, bf16[1024,1024]{1,0:T(8,128)(2,1)}, bf16[1024,1024]{1,0:T(8,128)(2,1)}, bf16[1024,1024]{1,0:T(8,128)(2,1)}) custom-call(s32[1]{0:T(128)} %bitcast.1.me_ref, bf16[1024,640]{1,0:T(8,128)(2,1)} %copy-done.19, bf16[1024,640]{1,0:T(8,128)(2,1)} %copy-done.32, ...), custom_call_target="tpu_custom_call" | custom-call | tf_op jit(solution)/shard_map/pallas_call | solution.py:247
  190.3 10.2 %shard_map.276 = (bf16[384,1024]{1,0:T(8,128)(2,1)}, f32[8,1,768]{2,1,0:T(1,128)}) custom-call(bf16[384,1024]{1,0:T(8,128)(2,1)} %add_convert_fusion.6.q_ref, bf16[512,2048]{1,0:T(8,128)(2,1)} %add_convert_fusion.2.k_ref.v_ref, bf16[512,2048]{1,0:T(8,128)(2,1)} %add_convert_fusion.2.k_ref.v_ref, f32[512,384]{1,0:T(8,128)} %compare_select_fusion.bias_ref), custom_call_target="tpu_custom_call" | custom-call | tf_op jit(solution)/shard_map/pallas_call | solution.py:120
  213.1 11.7 %add_convert_fusion.1 = (bf16[384,4096]{1,0:T(8,128)(2,1)}, bf16[384,4096]{1,0:T(8,128)(2,1)S(1)}) fusion(f32[4096]{0:T(1024)S(1)} %bitcast.282, bf16[384,1024]{1,0:T(8,128)(2,1)S(1)} %add_convert_fusion.5.refs_0_, bf16[1024,4096]{1,0:T(8,128)(2,1)} %shard_map.277), kind=kOutput, calls=%fused_computation.11 | convolution fusion | flops 3251109888 | bytes 15482880 | tf_op jit(solution)/shard_map/dot_general | solution.py:44
  225.6 10.4 %shard_map.278.w_ref = bf16[4096,1024]{1,0:T(8,128)(2,1)} custom-call(s32[1]{0:T(128)} %bitcast.1.me_ref, bf16[4096,128]{1,0:T(8,128)(2,1)} %refs_0_.1, bf16[4096,128]{1,0:T(8,128)(2,1)} %collective-permute-done.27.refs_1_, bf16[4096,128]{1,0:T(8,128)(2,1)} %collective-permute-done.28.refs_2_, bf16[2048,128]{1,0:T(8,128)(2,1)} %copy-done.58, ...), custom_call_target="tpu_custom_call" | custom-call | tf_op jit(solution)/shard_map/pallas_call | solution.py:247
  246.4 9.5 %shard_map.279 = (bf16[4,4096,128]{2,1,0:T(8,128)(2,1)}, bf16[4,4096,128]{2,1,0:T(8,128)(2,1)}) custom-call(s32[1]{0:T(128)} %bitcast.1.me_ref, bf16[384,4096]{1,0:T(8,128)(2,1)} %copy-done.29, bf16[1,384,1024]{2,1,0:T(8,128)(2,1)} %bitcast.261, bf16[1,384,1024]{2,1,0:T(8,128)(2,1)} %bitcast.262), custom_call_target="tpu_custom_call" | custom-call | tf_op jit(solution)/shard_map/pallas_call | solution.py:336
  256.4 11.1 %shard_map.280 = bf16[384,4096]{1,0:T(8,128)(2,1)} custom-call(bf16[384,1024]{1,0:T(8,128)(2,1)} %convert_element_type.706.dz_ref, bf16[4096,1024]{1,0:T(8,128)(2,1)} %shard_map.278.w_ref, bf16[384,4096]{1,0:T(8,128)(2,1)} %get-tuple-element.398.slope_ref), custom_call_target="tpu_custom_call" | custom-call | tf_op jit(solution)/shard_map/pallas_call | solution.py:360
  271.7 8.3 %shard_map.281 = (bf16[4,4096,128]{2,1,0:T(8,128)(2,1)}, bf16[4,4096,128]{2,1,0:T(8,128)(2,1)}) custom-call(s32[1]{0:T(128)} %bitcast.1.me_ref, bf16[384,1024]{1,0:T(8,128)(2,1)} %copy-done.31, bf16[1,384,4096]{2,1,0:T(8,128)(2,1)} %bitcast.259, bf16[1,384,4096]{2,1,0:T(8,128)(2,1)} %bitcast.260), custom_call_target="tpu_custom_call" | custom-call | tf_op jit(solution)/shard_map/pallas_call | solution.py:336
  293.8 12.0 %collective-permute-done.38 = bf16[2,2048,128]{2,1,0:T(8,128)(2,1)S(1)} collective-permute-done((bf16[2,2048,128]{2,1,0:T(8,128)(2,1)}, bf16[2,2048,128]{2,1,0:T(8,128)(2,1)S(1)}, u32[]{:S(2)}, u32[]{:S(2)}) %collective-permute-start.38) | collective-permute-done | bytes 1048608 | tf_op jit(solution)/shard_map/ppermute | solution.py:212
  311.5 13.7 %shard_map.282 = (bf16[384,1024]{1,0:T(8,128)(2,1)}, bf16[2,512,1024]{2,1,0:T(8,128)(2,1)}) custom-call(s32[1]{0:T(128)} %bitcast.33.z_ref, bf16[384,1024]{1,0:T(8,128)(2,1)} %add_convert_fusion.6.q_ref, bf16[512,2048]{1,0:T(8,128)(2,1)} %add_convert_fusion.2.k_ref.v_ref, bf16[512,2048]{1,0:T(8,128)(2,1)} %add_convert_fusion.2.k_ref.v_ref, ...), custom_call_target="tpu_custom_call" | custom-call | tf_op jit(solution)/shard_map/pallas_call | solution.py:184
  337.7 13.9 %shard_map.283 = (bf16[4,4096,128]{2,1,0:T(8,128)(2,1)}, bf16[4,4096,128]{2,1,0:T(8,128)(2,1)}) custom-call(s32[1]{0:T(128)} %bitcast.1.me_ref, bf16[384,1024]{1,0:T(8,128)(2,1)} %get-tuple-element.226.out_ref.refs_0_, bf16[1,384,1024]{2,1,0:T(8,128)(2,1)} %bitcast.267, bf16[1,384,1024]{2,1,0:T(8,128)(2,1)} %bitcast.268, bf16[384,1024]{1,0:T(8,128)(2,1)} %copy-done.30, ...), custom_call_target="tpu_custom_call" | custom-call | tf_op jit(solution)/shard_map/pallas_call | solution.py:336
  389.3 20.4 %shard_map.284 = (bf16[384,1024]{1,0:T(8,128)(2,1)}, bf16[3,1536,1024]{2,1,0:T(8,128)(2,1)}) custom-call(s32[1]{0:T(128)} %bitcast.33.z_ref, bf16[384,1024]{1,0:T(8,128)(2,1)} %add_convert_fusion.8.q_ref, bf16[1536,2048]{1,0:T(8,128)(2,1)} %add_convert_fusion.k_ref.v_ref, bf16[1536,2048]{1,0:T(8,128)(2,1)} %add_convert_fusion.k_ref.v_ref, ...), custom_call_target="tpu_custom_call" | custom-call | tf_op jit(solution)/shard_map/pallas_call | solution.py:184
  419.0 13.5 %shard_map.285 = (bf16[384,1024]{1,0:T(8,128)(2,1)}, bf16[3,1536,1024]{2,1,0:T(8,128)(2,1)}) custom-call(s32[1]{0:T(128)} %bitcast.33.z_ref, bf16[384,1024]{1,0:T(8,128)(2,1)} %add_convert_fusion.8.q_ref, bf16[1536,2048]{1,0:T(8,128)(2,1)} %add_convert_fusion.k_ref.v_ref, ...), custom_call_target="tpu_custom_call", output_to_operand_aliasing={{0}: (8, {}), {1}: (9, {})} | custom-call | tf_op jit(solution)/shard_map/pallas_call | solution.py:184
  436.4 21.5 %shard_map.286 = (bf16[4,4096,128]{2,1,0:T(8,128)(2,1)}, bf16[4,4096,128]{2,1,0:T(8,128)(2,1)}) custom-call(s32[1]{0:T(128)} %bitcast.1.me_ref, bf16[384,1024]{1,0:T(8,128)(2,1)} %copy-done.12, bf16[1,384,1024]{2,1,0:T(8,128)(2,1)} %bitcast.263, bf16[1,384,1024]{2,1,0:T(8,128)(2,1)} %bitcast.264, bf16[1536,1024]{1,0:T(8,128)(2,1)} %copy-done.13, ...), custom_call_target="tpu_custom_call" | custom-call | tf_op jit(solution)/shard_map/pallas_call | solution.py:336
  457.8 11.3 %all-reduce.7.cloned.1.call-done = bf16[4096,128]{1,0:T(8,128)(2,1)} async-done(((bf16[4096,128]{1,0:T(8,128)(2,1)}), bf16[4096,128]{1,0:T(8,128)(2,1)}) %all-reduce.7.cloned.1.call-update) | async-done | bytes 1048592 | tf_op jit(solution)/shard_map/psum | solution.py:607
  473.6 13.5 %shard_map.287 = (bf16[4,384,1024]{2,1,0:T(8,128)(2,1)}, f32[8,1024]{1,0:T(8,128)}) custom-call(bf16[3,1536,1024]{2,1,0:T(8,128)(2,1)} %get-tuple-element.317.refs_4_.refs_5_.refs_6_.refs_7_.refs_8_.refs_9_.dk_ref.dv_ref, bf16[3,1536,1024]{2,1,0:T(8,128)(2,1)} %get-tuple-element.317.refs_4_.refs_5_.refs_6_.refs_7_.refs_8_.refs_9_.dk_ref.dv_ref, ...), custom_call_target="tpu_custom_call" | custom-call | tf_op jit(solution)/shard_map/pallas_call | solution.py:391
  501.1 19.2 %collective-permute-done.56 = bf16[384,1024]{1,0:T(8,128)(2,1)S(1)} collective-permute-done((bf16[384,1024]{1,0:T(8,128)(2,1)S(1)}, bf16[384,1024]{1,0:T(8,128)(2,1)S(1)}, u32[]{:S(2)}, u32[]{:S(2)}) %collective-permute-start.56) | collective-permute-done | bytes 786464 | tf_op jit(solution)/shard_map/ppermute | solution.py:443
  576.1 19.7 %collective-permute-done.69 = f32[8,19,128]{2,1,0:T(8,128)S(1)} collective-permute-done((f32[8,19,128]{2,1,0:T(8,128)S(1)}, f32[8,19,128]{2,1,0:T(8,128)S(1)}, u32[]{:S(2)}, u32[]{:S(2)}) %collective-permute-start.69) | collective-permute-done | bytes 77856 | tf_op jit(solution)/shard_map/ppermute | solution.py:731
  611.2 13.9 %all-reduce.11.cloned.1.call-done = bf16[4096,128]{1,0:T(8,128)(2,1)} async-done(((bf16[4096,128]{1,0:T(8,128)(2,1)}), bf16[4096,128]{1,0:T(8,128)(2,1)}) %all-reduce.11.cloned.1.call-update) | async-done | bytes 1048592 | tf_op jit(solution)/shard_map/psum | solution.py:607
  (470 shorter events, 293.0 us)
Async XLA Ops:
  7.2 78.3 %all-gather.6.cloned.1.call-start = ((), (), s32[]{:S(2)}) async-start(), calls=%async_computation.6 | async-start | bytes 3932160 | tf_op jit(solution)/shard_map/all_gather | solution.py:511
  7.9 123.2 %all-gather.4.cloned.1.call-start = ((), (), s32[]{:S(2)}) async-start(), calls=%async_computation.1 | async-start | bytes 1310720 | tf_op jit(solution)/shard_map/all_gather | solution.py:514
  48.6 30.8 %collective-permute-start.9 = (bf16[1024,640]{1,0:T(8,128)(2,1)S(1)}, bf16[1024,640]{1,0:T(8,128)(2,1)S(1)}, u32[]{:S(2)}, u32[]{:S(2)}) collective-permute-start(bf16[1024,640]{1,0:T(8,128)(2,1)S(1)} %pad_maximum_fusion.refs_0_), channel_id=1, source_target_pairs={{0,2},{1,3},{2,0},{3,1},{4,6},{5,7},{6,4},{7,5},{8,10},{9,11},{10,... | collective-permute-start | bytes 3932168 | tf_op jit(solution)/shard_map/ppermute | solution.py:212
  50.3 30.9 %collective-permute-start.10 = (bf16[1024,640]{1,0:T(8,128)(2,1)S(1)}, bf16[1024,640]{1,0:T(8,128)(2,1)}, u32[]{:S(2)}, u32[]{:S(2)}) collective-permute-start(bf16[1024,640]{1,0:T(8,128)(2,1)S(1)} %pad_maximum_fusion.refs_0_), channel_id=1, source_target_pairs={{0,4},{1,5},{2,6},{3,7},{4,0},{5,1},{6,2},{7,3},{8,12},{9,13},{10,... | collective-permute-start | bytes 3932168 | tf_op jit(solution)/shard_map/ppermute | solution.py:212
  101.9 307.8 %reduce-scatter.2.cloned.1.call-start = ((), (), s32[]{:S(2)}) async-start(), calls=%async_computation.2 | async-start | bytes 1310720 | tf_op jit(solution)/shard_map/reduce_scatter | solution.py:672
  102.0 40.4 %collective-permute-start.15 = (bf16[1024,640]{1,0:T(8,128)(2,1)}, bf16[1024,640]{1,0:T(8,128)(2,1)}, u32[]{:S(2)}, u32[]{:S(2)}) collective-permute-start(bf16[1024,640]{1,0:T(8,128)(2,1)} %copy-done.19), channel_id=1, source_target_pairs={{0,1},{1,0},{2,3},{3,2},{4,5},{5,4},{6,7},{7,6},{8,9},{9,8},{10,11... | collective-permute-start | bytes 3932168 | tf_op jit(solution)/shard_map/ppermute | solution.py:212
  102.2 40.3 %collective-permute-start.16 = (bf16[1024,640]{1,0:T(8,128)(2,1)}, bf16[1024,640]{1,0:T(8,128)(2,1)}, u32[]{:S(2)}, u32[]{:S(2)}) collective-permute-start(bf16[1024,640]{1,0:T(8,128)(2,1)} %copy-done.32), channel_id=1, source_target_pairs={{0,1},{1,0},{2,3},{3,2},{4,5},{5,4},{6,7},{7,6},{8,9},{9,8},{10,11... | collective-permute-start | bytes 3932168 | tf_op jit(solution)/shard_map/ppermute | solution.py:212
  102.6 39.9 %collective-permute-start.17 = (bf16[1024,640]{1,0:T(8,128)(2,1)}, bf16[1024,640]{1,0:T(8,128)(2,1)}, u32[]{:S(2)}, u32[]{:S(2)}) collective-permute-start(bf16[1024,640]{1,0:T(8,128)(2,1)} %collective-permute-done.10.refs_2_), channel_id=1, source_target_pairs={{0,1},{1,0},{2,3},{3,2},{4,5},{5,4},{6,7},{7,6},{8,9},{9,8},{10,11... | collective-permute-start | bytes 3932168 | tf_op jit(solution)/shard_map/ppermute | solution.py:212
  103.7 38.7 %collective-permute-start.13 = (bf16[1024,512]{1,0:T(8,128)(2,1)}, bf16[1024,512]{1,0:T(8,128)(2,1)S(1)}, u32[]{:S(2)}, u32[]{:S(2)}) collective-permute-start(bf16[1024,512]{1,0:T(8,128)(2,1)} %refs_0_), channel_id=1, source_target_pairs={{0,2},{1,3},{2,0},{3,1},{4,6},{5,7},{6,4},{7,5},{8,10},{9,11},{10,... | collective-permute-start | bytes 3145736 | tf_op jit(solution)/shard_map/ppermute | solution.py:212
  105.0 37.4 %collective-permute-start.14 = (bf16[1024,512]{1,0:T(8,128)(2,1)}, bf16[1024,512]{1,0:T(8,128)(2,1)S(1)}, u32[]{:S(2)}, u32[]{:S(2)}) collective-permute-start(bf16[1024,512]{1,0:T(8,128)(2,1)} %refs_0_), channel_id=1, source_target_pairs={{0,4},{1,5},{2,6},{3,7},{4,0},{5,1},{6,2},{7,3},{8,12},{9,13},{10,... | collective-permute-start | bytes 3145736 | tf_op jit(solution)/shard_map/ppermute | solution.py:212
  147.2 35.6 %collective-permute-start.27 = (bf16[4096,128]{1,0:T(8,128)(2,1)}, bf16[4096,128]{1,0:T(8,128)(2,1)}, u32[]{:S(2)}, u32[]{:S(2)}) collective-permute-start(bf16[4096,128]{1,0:T(8,128)(2,1)} %refs_0_.1), channel_id=1, source_target_pairs={{0,2},{1,3},{2,0},{3,1},{4,6},{5,7},{6,4},{7,5},{8,10},{9,11},{10,... | collective-permute-start | bytes 3145736 | tf_op jit(solution)/shard_map/ppermute | solution.py:212
  147.9 35.0 %collective-permute-start.28 = (bf16[4096,128]{1,0:T(8,128)(2,1)}, bf16[4096,128]{1,0:T(8,128)(2,1)}, u32[]{:S(2)}, u32[]{:S(2)}) collective-permute-start(bf16[4096,128]{1,0:T(8,128)(2,1)} %refs_0_.1), channel_id=1, source_target_pairs={{0,4},{1,5},{2,6},{3,7},{4,0},{5,1},{6,2},{7,3},{8,12},{9,13},{10,... | collective-permute-start | bytes 3145736 | tf_op jit(solution)/shard_map/ppermute | solution.py:212
  280.1 25.7 %collective-permute-start.38 = (bf16[2,2048,128]{2,1,0:T(8,128)(2,1)}, bf16[2,2048,128]{2,1,0:T(8,128)(2,1)S(1)}, u32[]{:S(2)}, u32[]{:S(2)}) collective-permute-start(bf16[2,2048,128]{2,1,0:T(8,128)(2,1)} %pad_maximum_fusion.1), channel_id=1, source_target_pairs={{0,2},{1,3},{2,0},{3,1},{4,6},{5,7},{6,4},{7,5},{8,10},{9,11},{10,... | collective-permute-start | bytes 3145736 | tf_op jit(solution)/shard_map/ppermute | solution.py:212
  281.5 25.4 %collective-permute-start.39 = (bf16[2,2048,128]{2,1,0:T(8,128)(2,1)}, bf16[2,2048,128]{2,1,0:T(8,128)(2,1)S(1)}, u32[]{:S(2)}, u32[]{:S(2)}) collective-permute-start(bf16[2,2048,128]{2,1,0:T(8,128)(2,1)} %pad_maximum_fusion.2), channel_id=1, source_target_pairs={{0,4},{1,5},{2,6},{3,7},{4,0},{5,1},{6,2},{7,3},{8,12},{9,13},{10,... | collective-permute-start | bytes 3145736 | tf_op jit(solution)/shard_map/ppermute | solution.py:212
  369.0 100.1 %all-reduce.7.cloned.1.call-start = ((), (), s32[]{:S(2)}) async-start(), calls=%async_computation.3 | async-start | bytes 2097152 | tf_op jit(solution)/shard_map/psum | solution.py:607
  381.1 28.7 %collective-permute-start.50 = (bf16[2,2048,128]{2,1,0:T(8,128)(2,1)}, bf16[2,2048,128]{2,1,0:T(8,128)(2,1)}, u32[]{:S(2)}, u32[]{:S(2)}) collective-permute-start(bf16[2,2048,128]{2,1,0:T(8,128)(2,1)} %pad_maximum_fusion.6), channel_id=1, source_target_pairs={{0,2},{1,3},{2,0},{3,1},{4,6},{5,7},{6,4},{7,5},{8,10},{9,11},{10,... | collective-permute-start | bytes 3145736 | tf_op jit(solution)/shard_map/ppermute | solution.py:212
  383.2 26.6 %collective-permute-start.51 = (bf16[2,2048,128]{2,1,0:T(8,128)(2,1)}, bf16[2,2048,128]{2,1,0:T(8,128)(2,1)}, u32[]{:S(2)}, u32[]{:S(2)}) collective-permute-start(bf16[2,2048,128]{2,1,0:T(8,128)(2,1)} %pad_maximum_fusion.7), channel_id=1, source_target_pairs={{0,4},{1,5},{2,6},{3,7},{4,0},{5,1},{6,2},{7,3},{8,12},{9,13},{10,... | collective-permute-start | bytes 3145736 | tf_op jit(solution)/shard_map/ppermute | solution.py:212
  419.0 131.3 %all-reduce.9.cloned.1.call-start = ((), (), s32[]{:S(2)}) async-start(), calls=%async_computation.4 | async-start | bytes 2097152 | tf_op jit(solution)/shard_map/psum | solution.py:607
  473.5 151.6 %all-reduce.11.cloned.1.call-start = ((), (), s32[]{:S(2)}) async-start(), calls=%async_computation.5 | async-start | bytes 2097152 | tf_op jit(solution)/shard_map/psum | solution.py:607
  489.3 39.8 %collective-permute-start.62 = (bf16[2,2048,128]{2,1,0:T(8,128)(2,1)S(1)}, bf16[2,2048,128]{2,1,0:T(8,128)(2,1)S(1)}, u32[]{:S(2)}, u32[]{:S(2)}) collective-permute-start(bf16[2,2048,128]{2,1,0:T(8,128)(2,1)S(1)} %pad_maximum_fusion.9), channel_id=1, source_target_pairs={{0,2},{1,3},{2,0},{3,1},{4,6},{5,7},{6,4},{7,5},{8,10},{9,11},{10,... | collective-permute-start | bytes 3145736 | tf_op jit(solution)/shard_map/ppermute | solution.py:212
  491.0 38.1 %collective-permute-start.63 = (bf16[2,2048,128]{2,1,0:T(8,128)(2,1)S(1)}, bf16[2,2048,128]{2,1,0:T(8,128)(2,1)S(1)}, u32[]{:S(2)}, u32[]{:S(2)}) collective-permute-start(bf16[2,2048,128]{2,1,0:T(8,128)(2,1)S(1)} %pad_maximum_fusion.10), channel_id=1, source_target_pairs={{0,4},{1,5},{2,6},{3,7},{4,0},{5,1},{6,2},{7,3},{8,12},{9,13},{10,... | collective-permute-start | bytes 3145736 | tf_op jit(solution)/shard_map/ppermute | solution.py:212
  492.7 27.7 %collective-permute-start.56 = (bf16[384,1024]{1,0:T(8,128)(2,1)S(1)}, bf16[384,1024]{1,0:T(8,128)(2,1)S(1)}, u32[]{:S(2)}, u32[]{:S(2)}) collective-permute-start(bf16[384,1024]{1,0:T(8,128)(2,1)S(1)} %get-tuple-element.405), channel_id=1, source_target_pairs={{0,8},{1,9},{2,10},{3,11},{4,12},{5,13},{6,14},{7,15}} | collective-permute-start | bytes 2359304 | tf_op jit(solution)/shard_map/ppermute | solution.py:443
  554.0 53.0 %collective-permute-start.61 = (bf16[384,1024]{1,0:T(8,128)(2,1)}, bf16[384,1024]{1,0:T(8,128)(2,1)}, u32[]{:S(2)}, u32[]{:S(2)}) collective-permute-start(bf16[384,1024]{1,0:T(8,128)(2,1)} %get-tuple-element.401), channel_id=1, source_target_pairs={{8,0},{16,8},{24,16},{9,1},{17,9},{25,17},{10,2},{18,10},{26,18},{... | collective-permute-start | bytes 2359304 | tf_op jit(solution)/shard_map/ppermute | solution.py:443
  555.3 51.7 %collective-permute-start.60 = (bf16[384,1024]{1,0:T(8,128)(2,1)}, bf16[384,1024]{1,0:T(8,128)(2,1)}, u32[]{:S(2)}, u32[]{:S(2)}) collective-permute-start(bf16[384,1024]{1,0:T(8,128)(2,1)} %get-tuple-element.400), channel_id=1, source_target_pairs={{0,8},{8,16},{16,24},{1,9},{9,17},{17,25},{2,10},{10,18},{18,26},{... | collective-permute-start | bytes 2359304 | tf_op jit(solution)/shard_map/ppermute | solution.py:443
  (141 other events, 1566.8 us)
Sparse Core Ops, SparseCore 0:
  9.6 66.1 all-gather.5
  102.1 29.0 all-gather.3
  369.2 27.9 reduce-scatter.1
  419.1 49.9 all-reduce.6
  473.7 60.3 all-reduce.8
  561.6 63.4 all-reduce.10

commit v4 on v3

--- a/solution.py
+++ b/solution.py
@@ -258,6 +258,94 @@
     )(me, *mine, *other)
 
 
+def project_kernel(z_ref, x_ref, w_ref, gain_ref, shift_ref, bias_ref, a_ref, q_ref, kv_ref):
+    width = x_ref.shape[1]
+    a = layer_norm(x_ref[...].astype(F32), gain_ref[...], shift_ref[...])[0].astype(BF)
+    a_ref[...] = a
+    kv_ref[...] = (dense(a, w_ref[:, width:]) + bias_ref[:, width:]).astype(BF)
+
+    @pl.when(pl.program_id(0) == z_ref[0])
+    def _():
+        q_ref[...] = (dense(a, w_ref[:, :width]) + bias_ref[:, :width]).astype(BF)
+
+
+def project(z, x, w, gain, shift_row, bias, n):
+    total, width = x.shape
+    rows = total // n
+    whole = lambda v: pl.BlockSpec(v.shape, lambda i, z_ref: (0, 0))
+    block = lambda cols: pl.BlockSpec((rows, cols), lambda i, z_ref: (i, 0))
+    return pl.pallas_call(
+        project_kernel,
+        grid_spec=pltpu.PrefetchScalarGridSpec(
+            num_scalar_prefetch=1,
+            grid=(n,),
+            in_specs=[
+                block(width),
+                pl.BlockSpec((width, 3 * width), lambda i, z_ref: (0, 0)),
+                whole(gain),
+                whole(shift_row),
+                whole(bias),
+            ],
+            out_specs=[block(width), pl.BlockSpec((rows, width), lambda i, z_ref: (0, 0)), block(2 * width)],
+        ),
+        out_shape=[
+            jax.ShapeDtypeStruct((total, width), BF),
+            jax.ShapeDtypeStruct((rows, width), BF),
+            jax.ShapeDtypeStruct((total, 2 * width), BF),
+        ],
+        compiler_params=params(),
+        cost_estimate=SHORT,
+    )(z, x, w, gain, shift_row, bias)
+
+
+def assemble_dot_kernel(gelu, me_ref, *refs):
+    parts, (x_ref, bias_ref) = refs[:10], refs[10:12]
+    w_ref, *outs = refs[12:] if gelu else refs[13:]
+    rows, n = parts[0].shape
+    step = pl.program_id(0)
+    for t in (0, 1):
+        cols = pl.ds(pl.multiple_of(jnp.bitwise_xor(me_ref[0] % 2, t) * n, 128), n)
+        for k in range(3):
+
+            @pl.when(step == k)
+            def _():
+                w_ref[:, cols] = parts[5 * t + k][...]
+
+        @pl.when(step == 3)
+        def _():
+            w_ref[: rows // 2, cols] = parts[5 * t + 3][...]
+            w_ref[rows // 2 :, cols] = parts[5 * t + 4][...]
+
+    value = dense(x_ref[...], w_ref[...]) + bias_ref[...]
+    if gelu:
+        value, slope = gelu_both(value)
+        outs[0][...] = value.astype(BF)
+        outs[1][...] = slope.astype(BF)
+    else:
+        outs[0][...] = refs[12][...] + value
+
+
+def assemble_dot(me, mine, other, x, bias, onto=None):
+    rows, n = mine[0].shape
+    tok = x.shape[0]
+    whole = lambda v: pl.BlockSpec(v.shape, lambda i, me_ref: (0, 0))
+    pair = lambda r: pl.BlockSpec((r, 2 * n), lambda i, me_ref: (0, jnp.bitwise_xor(me_ref[0] // 2, i)))
+    gelu = onto is None
+    outs = [BF, BF] if gelu else [F32]
+    return pl.pallas_call(
+        functools.partial(assemble_dot_kernel, gelu),
+        grid_spec=pltpu.PrefetchScalarGridSpec(
+            num_scalar_prefetch=1,
+            grid=(4,),
+            in_specs=[whole(v) for v in mine + other] + [whole(x), pair(1)] + ([] if gelu else [pair(tok)]),
+            out_specs=[pair(rows)] + [pair(tok)] * len(outs),
+        ),
+        out_shape=[jax.ShapeDtypeStruct((rows, 8 * n), BF)] + [jax.ShapeDtypeStruct((tok, 8 * n), t) for t in outs],
+        compiler_params=params(),
+        cost_estimate=SHORT,
+    )(me, *mine, *other, x, bias, *([] if gelu else [onto]))
+
+
 def after(v, *others):
     return lax.optimization_barrier((v,) + others)[0]
 
@@ -346,6 +434,58 @@
         compiler_params=params(),
         cost_estimate=SHORT,
     )(me, *operands)
+
+
+def up_grad_kernel(me_ref, x_ref, du_ref, w_ref, keep_ref, send_ref, c_ref, xt_ref):
+    step = pl.program_id(0)
+
+    @pl.when(step == 0)
+    def _():
+        xt_ref[...] = jnp.transpose(x_ref[...])
+
+    du = du_ref[...]
+    res = dense(xt_ref[...], du)
+    rows, n = xt_ref.shape[0], du.shape[1] // 2
+    for odd in (0, 1):
+
+        @pl.when(me_ref[0] % 2 == odd)
+        def _():
+            for t, ref in enumerate((keep_ref, send_ref)):
+                for j in range(n // 128):
+                    col = (t ^ odd) * n + j * 128
+                    ref[0, j * rows : (j + 1) * rows] = res[:, col : col + 128].astype(BF)
+
+    part = nt(du, w_ref[...])
+
+    @pl.when(step == 0)
+    def _():
+        c_ref[...] = part
+
+    @pl.when(step > 0)
+    def _():
+        c_ref[...] += part
+
+
+def up_grad(me, x, du, w):
+    tok, rows = x.shape
+    n = du.shape[1] // 8
+    stacked = n // 128 * rows
+    pair = lambda r: pl.BlockSpec((r, 2 * n), lambda i, me_ref: (0, jnp.bitwise_xor(me_ref[0] // 2, i)))
+    whole = pl.BlockSpec((tok, rows), lambda i, me_ref: (0, 0))
+    shards = pl.BlockSpec((1, stacked, 128), lambda i, me_ref: (i, 0, 0))
+    return pl.pallas_call(
+        up_grad_kernel,
+        grid_spec=pltpu.PrefetchScalarGridSpec(
+            num_scalar_prefetch=1,
+            grid=(4,),
+            in_specs=[whole, pair(tok), pair(rows)],
+            out_specs=[shards, shards, whole],
+            scratch_shapes=[pltpu.VMEM((rows, tok), BF)],
+        ),
+        out_shape=[jax.ShapeDtypeStruct((4, stacked, 128), BF)] * 2 + [jax.ShapeDtypeStruct((tok, rows), F32)],
+        compiler_params=params(),
+        cost_estimate=SHORT,
+    )(me, x, du, w)
 
 
 def gelu_grad_kernel(dz_ref, w_ref, slope_ref, du_ref):
@@ -541,57 +681,63 @@
     cross_bias = jnp.where(seg_enc[:, None] == my_seg[None, :], 0.0, NEG).astype(F32)
     zero_row = jnp.zeros((width,), F32)
 
-    xf = x_full.astype(F32)
-    v1, _, _ = layer_norm(xf, gain[0], shift_v[0])
-    a1_full = v1.astype(BF)
     x32 = x.astype(F32)
     v1_own, xh1, rs1 = layer_norm(x32, gain[0], shift_v[0])
-    a1 = v1_own.astype(BF)
-    kv = (dense(a1_full, w_in[:, width:]) + jnp.concatenate([zero_row, bias[1]])).astype(BF)
-    q = (dense(a1, w_in[:, :width]) + bias[0]).astype(BF)
+    z_row = z.astype(jnp.int32).reshape(1)
+    if fast:
+        x_full, self_bias, cross_bias = all_after((x_full, self_bias, cross_bias))
+        qkv_bias = jnp.concatenate([bias[0], zero_row, bias[1]])[None]
+        a1_full, q, kv = project(z_row, x_full, first, gain[:1], shift_v[:1], qkv_bias, n_seq)
+    else:
+        xf = x_full.astype(F32)
+        a1_full = layer_norm(xf, gain[0], shift_v[0])[0].astype(BF)
+        kv = (dense(a1_full, w_in[:, width:]) + jnp.concatenate([zero_row, bias[1]])).astype(BF)
+        q = (dense(v1_own.astype(BF), w_in[:, :width]) + bias[0]).astype(BF)
     if fast:
         b_parts, b_other = send_core(b_near + b_far, kv)
         c_near = send_shard([ffn_in], kv)
-        q, kv, *_ = all_after((q, kv), *b_far, states)
+        q, kv, *_ = all_after((q, kv), *b_far)
     half = HEADS // 4
     attn_a, lse_a = attn_fwd(q, kv, self_bias, 0, half)
     if fast:
-        q, attn_a, lse_a = all_after((q, attn_a, lse_a), *c_near[1:], *b_other)
+        widths = tuple(v.shape[1] for v in (cross_kv, attn_out, cross_q, cross_out))
+        b_parts = all_after(b_parts, attn_a)
+        w_ckv, w_out, w_cq, w_cout = assemble(me, b_parts, b_other, widths)
+        q, attn_a, lse_a, w_out, states = all_after((q, attn_a, lse_a, w_out, states), *c_near[1:])
         c_far = send_diagonal(c_near, attn_a)
-        d_near = send_shard([ffn_out], attn_a)
     attn_b, lse_b = attn_fwd(q, kv, self_bias, half, half)
     attn = jnp.concatenate([attn_a, attn_b], axis=1)
     lse = jnp.concatenate([lse_a, lse_b], axis=0)
     if fast:
         attn, lse = all_after((attn, lse), *c_far)
-        widths = tuple(v.shape[1] for v in (cross_kv, attn_out, cross_q, cross_out))
+        d_near = send_shard([ffn_out], attn)
         c_parts, c_other = send_core(c_near + c_far, attn)
-        b_parts = all_after(b_parts, attn)
-        w_ckv, w_out, w_cq, w_cout = assemble(me, b_parts, b_other, widths)
     h1 = x32 + dense(attn, w_out) + bias[2]
     v2, xh2, rs2 = layer_norm(h1, gain[1], shift_v[1])
     a2 = v2.astype(BF)
     cq = (dense(a2, w_cq) + bias[3]).astype(BF)
     ekv = (dense(states, w_ckv) + jnp.concatenate([zero_row, bias[4]])).astype(BF)
     if fast:
-        cq = after(cq, ekv, *c_other, *d_near[1:])
-        d_far = send_diagonal(d_near, cq)
+        cq = after(cq, ekv, *c_other)
     cattn, clse = attn_fwd(cq, ekv, cross_bias)
     if fast:
-        cattn = after(cattn, *d_far)
-        d_parts, d_other = send_core(d_near + d_far, cattn)
+        cattn = after(cattn, *d_near[1:])
+        d_far = send_diagonal(d_near, cattn)
+        d_parts, d_other = send_core(d_near, cattn)
         c_parts = all_after(c_parts, cattn)
-        (w_up,) = assemble(me, c_parts, c_other, (ffn_in.shape[1],))
     h2 = h1 + dense(cattn, w_cout) + bias[5]
     v3, xh3, rs3 = layer_norm(h2, gain[2], shift_v[2])
     a3 = v3.astype(BF)
-    up = dense(a3, w_up) + up_bias
-    gelu, slope = gelu_both(up)
-    gelu_h, slope = gelu.astype(BF), slope.astype(BF)
-    if fast:
-        d_parts = all_after(d_parts, gelu_h)
-        (w_down,) = assemble(me, d_parts, d_other, (shard,))
-    h3 = h2 + dense(gelu_h, w_down) + bias[6]
+    if fast:
+        w_up, gelu_h, slope = assemble_dot(me, c_parts, c_other, a3, up_bias[None])
+        gelu_h, *d_far = all_after((gelu_h,) + d_far)
+        d_rest, d_other_rest = send_core(d_far, gelu_h)
+        d_parts, d_other = d_parts + d_rest, d_other + d_other_rest
+        w_down, h3 = assemble_dot(me, d_parts, d_other, gelu_h, bias[6:7], h2)
+    else:
+        gelu, slope = gelu_both(dense(a3, w_up) + up_bias)
+        gelu_h, slope = gelu.astype(BF), slope.astype(BF)
+        h3 = h2 + dense(gelu_h, w_down) + bias[6]
     out, xh4, rs4 = layer_norm(h3, gain[3], shift_v[3])
 
     total = lambda v: jnp.sum(v, axis=0, dtype=F32)
@@ -600,7 +746,6 @@
     g3, s3 = norm_sums(xh4, ct)
     dh3 = norm_input_grad(xh4, rs4, gain[3], ct)
     dz = dh3.astype(BF)
-    z_row = z.astype(jnp.int32).reshape(1)
 
     def by_chain(v, turn=0):
         listed = [(turn + i) % n_seq for i in range(n_seq)]
@@ -616,10 +761,11 @@
         du, d_got = all_after((du, d_got))
         d_n, sent = sum_near(d_keep, d_got, du)
         du, *_ = all_after((du,), *sent)
-        c_keep, c_send = wgrad(me, (a3, du[None]))
-        du, c_send = all_after((du, c_send))
+        c_keep, c_send, c3 = up_grad(me, a3, du, w_up)
+        c3, c_send, *d_n = all_after((c3, c_send) + tuple(d_n))
         c_got = swap(c_send, 1)
-    c3 = dense_t(du, w_up)
+    else:
+        c3 = dense_t(du, w_up)
     g2, s2 = norm_sums(xh3, c3)
     dh2 = dh3 + norm_input_grad(xh3, rs3, gain[2], c3)
     dc = dh2.astype(BF)

time: 644 us -> 613 us (0.952)
  matrix products: 63.6 us -> 29.5 us
  Pallas kernels: 190 us -> 219 us
  waiting for transfers between devices: 165 us -> 150 us
    pallas_call x0 -> x4, Pallas kernels: none -> 54.1 us  [the longest x2 23.8 us: assemble_dot(): pl.pallas_call(functools.partial(assemble_dot_kernel, gelu), grid_spec=pl...]
    dot_general x8 -> x4, matrix products: 41.2 us -> 12.3 us  [dense(): return jnp.dot(a, b, preferred_element_type=F32)]
    all_gather x1, waiting for transfers between devices: 18.8 us -> 0.27 us  [local(): lax.all_gather(after(enc_states[0], x_full), 'seq', axis=0, tiled=True)]
    pallas_call x4 -> x2, Pallas kernels: 32.1 us -> 15.3 us  [assemble(): pl.pallas_call(functools.partial(assemble_kernel, widths), grid_spec=pltp...]
    pallas_call x4 -> x3, Pallas kernels: 53.2 us -> 45.1 us  [wgrad(): pl.pallas_call(functools.partial(wgrad_kernel, tuple(counts)), grid_spec=...]
    dot_general x7 -> x6, matrix products: 22.5 us -> 17.2 us  [dense_t(): lax.dot_general(a, b, (((1,), (1,)), ((), ())), preferred_element_type=F32)]
    unnamed x177 -> x169, local copies, waits for them, and re-layouts: 14.3 us -> 12.5 us
  transfers between devices with their start and end apart: 77 -> 77, of which waited for: 23 -> 28; matrix products, arithmetic and copies ran while one was open for 23% -> 18% of each run, Pallas kernels for 25% -> 33%
where the time goes in v4:
time: 613 us; the launch traced here: 606 us
  Pallas kernels  219 us (36%)
  waiting for transfers between devices  150 us (24%)
  other arithmetic  93.3 us (15%)
  starting transfers between devices  75.6 us (12%)
  matrix products  29.5 us (5%)
  local copies, waits for them, and re-layouts  23.4 us (4%)
  between operations  15.6 us (3%)
    ppermute x59, waiting for transfers between devices, swap(): return lax.ppermute(v, 'dp', [(i, i ^ bit) for i in range(8)])  73.3 us
    pallas_call x3, Pallas kernels, attn_bwd(): pl.pallas_call(functools.partial(attn_bwd_kernel, head ** (-0.5), chunk,...  47.4 us
    pallas_call x3, Pallas kernels, wgrad(): pl.pallas_call(functools.partial(wgrad_kernel, tuple(counts)), grid_spec=...  45.1 us
    ppermute x59, starting transfers between devices, swap(): return lax.ppermute(v, 'dp', [(i, i ^ bit) for i in range(8)])  43.5 us
    convert_element_type x14, other arithmetic, add(): return total.astype(BF)  34.2 us
    pallas_call x3, Pallas kernels, attn_fwd(): pl.pallas_call(functools.partial(attn_fwd_kernel, head ** (-0.5), chunk),...  32.6 us
    ppermute x6, waiting for transfers between devices, shift(): lax.ppermute(v, 'seq', [(a, a + step) for a in pairs if 0 <= a + step < n])  25.8 us
    psum x3, waiting for transfers between devices, by_chain(): return lax.psum(v, 'seq', axis_index_groups=[listed])  25.8 us
  transfers between devices with their start and end apart: 77, of which 28 were waited for; matrix products, arithmetic and copies ran while one was open for 18% of the time, Pallas kernels for 33%

profile of v4, /device:TPU:0, one launch (start us, length us, event | category | flops | bytes accessed | tf_op | source)
XLA Modules:
  0.0 606.3 jit_solution(9524616093031156232)
XLA Ops:
  15.3 16.5 %collective-permute-done.refs_1_ = bf16[1056,384]{1,0:T(8,128)(2,1)S(1)} collective-permute-done((bf16[1056,384]{1,0:T(8,128)(2,1)S(1)}, bf16[1056,384]{1,0:T(8,128)(2,1)S(1)}, u32[]{:S(2)}, u32[]{:S(2)}) %collective-permute-start) | collective-permute-done | bytes 811040 | tf_op jit(solution)/shard_map/ppermute | solution.py:212
  38.0 7.8 %collective-permute-done.2.refs_3_ = bf16[528,384]{1,0:T(8,128)(2,1)S(1)} collective-permute-done((bf16[528,384]{1,0:T(8,128)(2,1)S(1)}, bf16[528,384]{1,0:T(8,128)(2,1)S(1)}, u32[]{:S(2)}, u32[]{:S(2)}) %collective-permute-start.2) | collective-permute-done | bytes 405536 | tf_op jit(solution)/shard_map/ppermute | solution.py:212
  61.8 11.3 %collective-permute-done.9.refs_1_ = bf16[1024,640]{1,0:T(8,128)(2,1)} collective-permute-done((bf16[1024,640]{1,0:T(8,128)(2,1)S(1)}, bf16[1024,640]{1,0:T(8,128)(2,1)}, u32[]{:S(2)}, u32[]{:S(2)}) %collective-permute-start.9) | collective-permute-done | bytes 1310752 | tf_op jit(solution)/shard_map/ppermute | solution.py:212
  78.5 14.5 %shard_map.273 = (bf16[1536,1024]{1,0:T(8,128)(2,1)}, bf16[384,1024]{1,0:T(8,128)(2,1)}, bf16[1536,2048]{1,0:T(8,128)(2,1)}) custom-call(s32[1]{0:T(128)} %bitcast.1.z_ref, bf16[1536,1024]{1,0:T(8,128)(2,1)} %bitcast.238, bf16[1056,3072]{1,0:T(8,128)(2,1)} %shard_map.272.w_ref.wk_ref.wv_ref, f32[1,1024]{1,0:T(1,128)} %bitcast.266, f32[1,1024]{1,0:T(1,128)} %bitcast.265, ...), custom_call_target="tpu_custom_call" | custom-call | tf_op jit(solution)/shard_map/pallas_call | solution.py:277
  97.7 11.2 %shard_map.274 = (bf16[384,512]{1,0:T(8,128)(2,1)}, f32[4,1,768]{2,1,0:T(1,128)}) custom-call(bf16[384,1024]{1,0:T(8,128)(2,1)} %get-tuple-element.225.q_ref, bf16[1536,2048]{1,0:T(8,128)(2,1)} %get-tuple-element.207.k_ref.v_ref, bf16[1536,2048]{1,0:T(8,128)(2,1)} %get-tuple-element.207.k_ref.v_ref, f32[1536,384]{1,0:T(8,128)} %and_select_fusion.bias_ref), custom_call_target="tpu_custom_call" | custom-call | tf_op jit(solution)/shard_map/pallas_call | solution.py:120
  111.6 8.1 %shard_map.275 = (bf16[1024,2048]{1,0:T(8,128)(2,1)}, bf16[1024,1024]{1,0:T(8,128)(2,1)}, bf16[1024,1024]{1,0:T(8,128)(2,1)}, bf16[1024,1024]{1,0:T(8,128)(2,1)}) custom-call(s32[1]{0:T(128)} %bitcast.me_ref, bf16[1024,640]{1,0:T(8,128)(2,1)} %copy-done.18, bf16[1024,640]{1,0:T(8,128)(2,1)} %collective-permute-done.9.refs_1_, ...), custom_call_target="tpu_custom_call" | custom-call | tf_op jit(solution)/shard_map/pallas_call | solution.py:247
  127.1 11.3 %shard_map.276 = (bf16[384,512]{1,0:T(8,128)(2,1)}, f32[4,1,768]{2,1,0:T(1,128)}) custom-call(bf16[384,1024]{1,0:T(8,128)(2,1)} %get-tuple-element.225.q_ref, bf16[1536,2048]{1,0:T(8,128)(2,1)} %get-tuple-element.207.k_ref.v_ref, bf16[1536,2048]{1,0:T(8,128)(2,1)} %get-tuple-element.207.k_ref.v_ref, f32[1536,384]{1,0:T(8,128)} %and_select_fusion.bias_ref), custom_call_target="tpu_custom_call" | custom-call | tf_op jit(solution)/shard_map/pallas_call | solution.py:120
  156.5 10.1 %shard_map.277 = (bf16[384,1024]{1,0:T(8,128)(2,1)}, f32[8,1,768]{2,1,0:T(1,128)}) custom-call(bf16[384,1024]{1,0:T(8,128)(2,1)} %add_convert_fusion.4.q_ref, bf16[512,2048]{1,0:T(8,128)(2,1)} %add_convert_fusion.k_ref.v_ref, bf16[512,2048]{1,0:T(8,128)(2,1)} %add_convert_fusion.k_ref.v_ref, f32[512,384]{1,0:T(8,128)} %compare_select_fusion.bias_ref), custom_call_target="tpu_custom_call" | custom-call | tf_op jit(solution)/shard_map/pallas_call | solution.py:120
  182.1 12.7 %shard_map.278 = (bf16[1024,4096]{1,0:T(8,128)(2,1)}, bf16[384,4096]{1,0:T(8,128)(2,1)}, bf16[384,4096]{1,0:T(8,128)(2,1)}) custom-call(s32[1]{0:T(128)} %bitcast.me_ref, bf16[1024,512]{1,0:T(8,128)(2,1)} %refs_0_, bf16[1024,512]{1,0:T(8,128)(2,1)} %copy-done.27, bf16[1024,512]{1,0:T(8,128)(2,1)} %collective-permute-done.19.refs_2_, ...), custom_call_target="tpu_custom_call" | custom-call | tf_op jit(solution)/shard_map/pallas_call | solution.py:335
  198.6 11.1 %shard_map.279 = (bf16[4096,1024]{1,0:T(8,128)(2,1)}, f32[384,1024]{1,0:T(8,128)}) custom-call(s32[1]{0:T(128)} %bitcast.me_ref, bf16[4096,128]{1,0:T(8,128)(2,1)} %refs_0_.1, bf16[4096,128]{1,0:T(8,128)(2,1)} %copy-done.28, bf16[4096,128]{1,0:T(8,128)(2,1)} %copy-done.29, bf16[2048,128]{1,0:T(8,128)(2,1)} %copy-done.60, bf16[2048,128]{1,0:T(8,128)(2,1)} %copy-done.63, ...), custom_call_target="tpu_custom_call" | custom-call | tf_op jit(solution)/shard_map/pallas_call | solution.py:335
  215.1 9.5 %shard_map.280 = (bf16[4,4096,128]{2,1,0:T(8,128)(2,1)}, bf16[4,4096,128]{2,1,0:T(8,128)(2,1)}) custom-call(s32[1]{0:T(128)} %bitcast.me_ref, bf16[384,4096]{1,0:T(8,128)(2,1)} %get-tuple-element.265.refs_10_.refs_0_, bf16[1,384,1024]{2,1,0:T(8,128)(2,1)} %bitcast.240, bf16[1,384,1024]{2,1,0:T(8,128)(2,1)} %bitcast.241), custom_call_target="tpu_custom_call" | custom-call | tf_op jit(solution)/shard_map/pallas_call | solution.py:424
  225.0 10.8 %shard_map.281.du_ref = bf16[384,4096]{1,0:T(8,128)(2,1)} custom-call(bf16[384,1024]{1,0:T(8,128)(2,1)} %convert_element_type.682.dz_ref, bf16[4096,1024]{1,0:T(8,128)(2,1)} %get-tuple-element.269.w_ref, bf16[384,4096]{1,0:T(8,128)(2,1)} %get-tuple-element.270.slope_ref), custom_call_target="tpu_custom_call" | custom-call | tf_op jit(solution)/shard_map/pallas_call | solution.py:500
  240.4 15.7 %shard_map.282 = (bf16[4,4096,128]{2,1,0:T(8,128)(2,1)}, bf16[4,4096,128]{2,1,0:T(8,128)(2,1)}, f32[384,1024]{1,0:T(8,128)}) custom-call(s32[1]{0:T(128)} %bitcast.me_ref, bf16[384,1024]{1,0:T(8,128)(2,1)} %add_convert_fusion.3.refs_10_.x_ref, bf16[384,4096]{1,0:T(8,128)(2,1)} %shard_map.281.du_ref, bf16[1024,4096]{1,0:T(8,128)(2,1)} %get-tuple-element.278.w_ref), custom_call_target="tpu_custom_call" | custom-call | tf_op jit(solution)/shard_map/pallas_call | solution.py:476
  279.5 13.7 %shard_map.283 = (bf16[384,1024]{1,0:T(8,128)(2,1)}, bf16[2,512,1024]{2,1,0:T(8,128)(2,1)}) custom-call(s32[1]{0:T(128)} %bitcast.1.z_ref, bf16[384,1024]{1,0:T(8,128)(2,1)} %add_convert_fusion.4.q_ref, bf16[512,2048]{1,0:T(8,128)(2,1)} %add_convert_fusion.k_ref.v_ref, bf16[512,2048]{1,0:T(8,128)(2,1)} %add_convert_fusion.k_ref.v_ref, ...), custom_call_target="tpu_custom_call" | custom-call | tf_op jit(solution)/shard_map/pallas_call | solution.py:184
  302.6 14.2 %shard_map.284 = (bf16[4,4096,128]{2,1,0:T(8,128)(2,1)}, bf16[4,4096,128]{2,1,0:T(8,128)(2,1)}) custom-call(s32[1]{0:T(128)} %bitcast.me_ref, bf16[384,1024]{1,0:T(8,128)(2,1)} %get-tuple-element.245.out_ref.refs_0_, bf16[1,384,1024]{2,1,0:T(8,128)(2,1)} %bitcast.246, bf16[1,384,1024]{2,1,0:T(8,128)(2,1)} %bitcast.247, bf16[384,1024]{1,0:T(8,128)(2,1)} %copy-done.26, ...), custom_call_target="tpu_custom_call" | custom-call | tf_op jit(solution)/shard_map/pallas_call | solution.py:424
  358.5 20.2 %shard_map.285 = (bf16[384,1024]{1,0:T(8,128)(2,1)}, bf16[3,1536,1024]{2,1,0:T(8,128)(2,1)}) custom-call(s32[1]{0:T(128)} %bitcast.1.z_ref, bf16[384,1024]{1,0:T(8,128)(2,1)} %get-tuple-element.225.q_ref, bf16[1536,2048]{1,0:T(8,128)(2,1)} %get-tuple-element.207.k_ref.v_ref, bf16[1536,2048]{1,0:T(8,128)(2,1)} %get-tuple-element.207.k_ref.v_ref, ...), custom_call_target="tpu_custom_call" | custom-call | tf_op jit(solution)/shard_map/pallas_call | solution.py:184
  387.6 13.5 %shard_map.286 = (bf16[384,1024]{1,0:T(8,128)(2,1)}, bf16[3,1536,1024]{2,1,0:T(8,128)(2,1)}) custom-call(s32[1]{0:T(128)} %bitcast.1.z_ref, bf16[384,1024]{1,0:T(8,128)(2,1)} %get-tuple-element.225.q_ref, bf16[1536,2048]{1,0:T(8,128)(2,1)} %get-tuple-element.207.k_ref.v_ref, ...), custom_call_target="tpu_custom_call", output_to_operand_aliasing={{0}: (8, {}), {1}: (9, {})} | custom-call | tf_op jit(solution)/shard_map/pallas_call | solution.py:184
  404.9 21.4 %shard_map.287 = (bf16[4,4096,128]{2,1,0:T(8,128)(2,1)}, bf16[4,4096,128]{2,1,0:T(8,128)(2,1)}) custom-call(s32[1]{0:T(128)} %bitcast.me_ref, bf16[384,1024]{1,0:T(8,128)(2,1)} %copy-done.11, bf16[1,384,1024]{2,1,0:T(8,128)(2,1)} %bitcast.242, bf16[1,384,1024]{2,1,0:T(8,128)(2,1)} %bitcast.243, bf16[1536,1024]{1,0:T(8,128)(2,1)} %get-tuple-element.341.refs_3_, ...), custom_call_target="tpu_custom_call" | custom-call | tf_op jit(solution)/shard_map/pallas_call | solution.py:424
  426.3 11.9 %all-reduce.6.cloned.1.call-done = bf16[4096,128]{1,0:T(8,128)(2,1)} async-done(((bf16[4096,128]{1,0:T(8,128)(2,1)}), bf16[4096,128]{1,0:T(8,128)(2,1)}) %all-reduce.6.cloned.1.call-update) | async-done | bytes 1048592 | tf_op jit(solution)/shard_map/psum | solution.py:752
  444.8 13.2 %shard_map.288 = (bf16[4,384,1024]{2,1,0:T(8,128)(2,1)}, f32[8,1024]{1,0:T(8,128)}) custom-call(bf16[3,1536,1024]{2,1,0:T(8,128)(2,1)} %get-tuple-element.345.refs_4_.refs_5_.refs_6_.refs_7_.refs_8_.refs_9_.dk_ref.dv_ref, bf16[3,1536,1024]{2,1,0:T(8,128)(2,1)} %get-tuple-element.345.refs_4_.refs_5_.refs_6_.refs_7_.refs_8_.refs_9_.dk_ref.dv_ref, ...), custom_call_target="tpu_custom_call" | custom-call | tf_op jit(solution)/shard_map/pallas_call | solution.py:531
  472.9 18.3 %collective-permute-done.56 = bf16[384,1024]{1,0:T(8,128)(2,1)S(1)} collective-permute-done((bf16[384,1024]{1,0:T(8,128)(2,1)S(1)}, bf16[384,1024]{1,0:T(8,128)(2,1)S(1)}, u32[]{:S(2)}, u32[]{:S(2)}) %collective-permute-start.56) | collective-permute-done | bytes 786464 | tf_op jit(solution)/shard_map/ppermute | solution.py:583
  509.9 7.5 %collective-permute-done.58 = bf16[384,1024]{1,0:T(8,128)(2,1)} collective-permute-done((bf16[384,1024]{1,0:T(8,128)(2,1)}, bf16[384,1024]{1,0:T(8,128)(2,1)}, u32[]{:S(2)}, u32[]{:S(2)}) %collective-permute-start.58) | collective-permute-done | bytes 786464 | tf_op jit(solution)/shard_map/ppermute | solution.py:583
  545.8 20.6 %collective-permute-done.69 = f32[8,19,128]{2,1,0:T(8,128)S(1)} collective-permute-done((f32[8,19,128]{2,1,0:T(8,128)S(1)}, f32[8,19,128]{2,1,0:T(8,128)S(1)}, u32[]{:S(2)}, u32[]{:S(2)}) %collective-permute-start.69) | collective-permute-done | bytes 77856 | tf_op jit(solution)/shard_map/ppermute | solution.py:877
  582.0 13.9 %all-reduce.10.cloned.1.call-done = bf16[4096,128]{1,0:T(8,128)(2,1)} async-done(((bf16[4096,128]{1,0:T(8,128)(2,1)}), bf16[4096,128]{1,0:T(8,128)(2,1)}) %all-reduce.10.cloned.1.call-update) | async-done | bytes 1048592 | tf_op jit(solution)/shard_map/psum | solution.py:752
  (455 shorter events, 271.4 us)
Async XLA Ops:
  7.2 71.3 %all-gather.6.cloned.1.call-start = ((), (), s32[]{:S(2)}) async-start(), calls=%async_computation.6 | async-start | bytes 3932160 | tf_op jit(solution)/shard_map/all_gather | solution.py:651
  7.9 114.4 %all-gather.4.cloned.1.call-start = ((), (), s32[]{:S(2)}) async-start(), calls=%async_computation.1 | async-start | bytes 1310720 | tf_op jit(solution)/shard_map/all_gather | solution.py:654
  35.8 37.2 %collective-permute-start.9 = (bf16[1024,640]{1,0:T(8,128)(2,1)S(1)}, bf16[1024,640]{1,0:T(8,128)(2,1)}, u32[]{:S(2)}, u32[]{:S(2)}) collective-permute-start(bf16[1024,640]{1,0:T(8,128)(2,1)S(1)} %pad_maximum_fusion.refs_0_), channel_id=1, source_target_pairs={{0,2},{1,3},{2,0},{3,1},{4,6},{5,7},{6,4},{7,5},{8,10},{9,11},{10,... | collective-permute-start | bytes 3932168 | tf_op jit(solution)/shard_map/ppermute | solution.py:212
  37.4 35.7 %collective-permute-start.10 = (bf16[1024,640]{1,0:T(8,128)(2,1)S(1)}, bf16[1024,640]{1,0:T(8,128)(2,1)}, u32[]{:S(2)}, u32[]{:S(2)}) collective-permute-start(bf16[1024,640]{1,0:T(8,128)(2,1)S(1)} %pad_maximum_fusion.refs_0_), channel_id=1, source_target_pairs={{0,4},{1,5},{2,6},{3,7},{4,0},{5,1},{6,2},{7,3},{8,12},{9,13},{10,... | collective-permute-start | bytes 3932168 | tf_op jit(solution)/shard_map/ppermute | solution.py:212
  93.7 285.1 %reduce-scatter.2.cloned.1.call-start = ((), (), s32[]{:S(2)}) async-start(), calls=%async_computation.2 | async-start | bytes 1310720 | tf_op jit(solution)/shard_map/reduce_scatter | solution.py:818
  95.4 25.4 %collective-permute-start.18 = (bf16[1024,512]{1,0:T(8,128)(2,1)}, bf16[1024,512]{1,0:T(8,128)(2,1)S(1)}, u32[]{:S(2)}, u32[]{:S(2)}) collective-permute-start(bf16[1024,512]{1,0:T(8,128)(2,1)} %refs_0_), channel_id=1, source_target_pairs={{0,2},{1,3},{2,0},{3,1},{4,6},{5,7},{6,4},{7,5},{8,10},{9,11},{10,... | collective-permute-start | bytes 3145736 | tf_op jit(solution)/shard_map/ppermute | solution.py:212
  96.5 25.5 %collective-permute-start.19 = (bf16[1024,512]{1,0:T(8,128)(2,1)}, bf16[1024,512]{1,0:T(8,128)(2,1)}, u32[]{:S(2)}, u32[]{:S(2)}) collective-permute-start(bf16[1024,512]{1,0:T(8,128)(2,1)} %refs_0_), channel_id=1, source_target_pairs={{0,4},{1,5},{2,6},{3,7},{4,0},{5,1},{6,2},{7,3},{8,12},{9,13},{10,... | collective-permute-start | bytes 3145736 | tf_op jit(solution)/shard_map/ppermute | solution.py:212
  147.5 25.1 %collective-permute-start.22 = (bf16[4096,128]{1,0:T(8,128)(2,1)S(1)}, bf16[4096,128]{1,0:T(8,128)(2,1)S(1)}, u32[]{:S(2)}, u32[]{:S(2)}) collective-permute-start(bf16[4096,128]{1,0:T(8,128)(2,1)S(1)} %copy-done.37), channel_id=1, source_target_pairs={{0,2},{1,3},{2,0},{3,1},{4,6},{5,7},{6,4},{7,5},{8,10},{9,11},{10,... | collective-permute-start | bytes 3145736 | tf_op jit(solution)/shard_map/ppermute | solution.py:212
  148.1 24.9 %collective-permute-start.23 = (bf16[4096,128]{1,0:T(8,128)(2,1)S(1)}, bf16[4096,128]{1,0:T(8,128)(2,1)S(1)}, u32[]{:S(2)}, u32[]{:S(2)}) collective-permute-start(bf16[4096,128]{1,0:T(8,128)(2,1)S(1)} %copy-done.37), channel_id=1, source_target_pairs={{0,4},{1,5},{2,6},{3,7},{4,0},{5,1},{6,2},{7,3},{8,12},{9,13},{10,... | collective-permute-start | bytes 3145736 | tf_op jit(solution)/shard_map/ppermute | solution.py:212
  238.0 25.3 %collective-permute-start.37 = (bf16[2,2048,128]{2,1,0:T(8,128)(2,1)S(1)}, bf16[2,2048,128]{2,1,0:T(8,128)(2,1)S(1)}, u32[]{:S(2)}, u32[]{:S(2)}) collective-permute-start(bf16[2,2048,128]{2,1,0:T(8,128)(2,1)S(1)} %pad_maximum_fusion.1), channel_id=1, source_target_pairs={{0,2},{1,3},{2,0},{3,1},{4,6},{5,7},{6,4},{7,5},{8,10},{9,11},{10,... | collective-permute-start | bytes 3145736 | tf_op jit(solution)/shard_map/ppermute | solution.py:212
  238.8 25.1 %collective-permute-start.38 = (bf16[2,2048,128]{2,1,0:T(8,128)(2,1)S(1)}, bf16[2,2048,128]{2,1,0:T(8,128)(2,1)}, u32[]{:S(2)}, u32[]{:S(2)}) collective-permute-start(bf16[2,2048,128]{2,1,0:T(8,128)(2,1)S(1)} %pad_maximum_fusion.2), channel_id=1, source_target_pairs={{0,4},{1,5},{2,6},{3,7},{4,0},{5,1},{6,2},{7,3},{8,12},{9,13},{10,... | collective-permute-start | bytes 3145736 | tf_op jit(solution)/shard_map/ppermute | solution.py:212
  295.5 24.7 %collective-permute-start.43 = (bf16[2,2048,128]{2,1,0:T(8,128)(2,1)S(1)}, bf16[2,2048,128]{2,1,0:T(8,128)(2,1)S(1)}, u32[]{:S(2)}, u32[]{:S(2)}) collective-permute-start(bf16[2,2048,128]{2,1,0:T(8,128)(2,1)S(1)} %pad_maximum_fusion.3), channel_id=1, source_target_pairs={{0,2},{1,3},{2,0},{3,1},{4,6},{5,7},{6,4},{7,5},{8,10},{9,11},{10,... | collective-permute-start | bytes 3145736 | tf_op jit(solution)/shard_map/ppermute | solution.py:212
  336.7 101.5 %all-reduce.6.cloned.1.call-start = ((), (), s32[]{:S(2)}) async-start(), calls=%async_computation.3 | async-start | bytes 2097152 | tf_op jit(solution)/shard_map/psum | solution.py:752
  348.9 29.9 %collective-permute-start.50 = (bf16[2,2048,128]{2,1,0:T(8,128)(2,1)}, bf16[2,2048,128]{2,1,0:T(8,128)(2,1)}, u32[]{:S(2)}, u32[]{:S(2)}) collective-permute-start(bf16[2,2048,128]{2,1,0:T(8,128)(2,1)} %pad_maximum_fusion.6), channel_id=1, source_target_pairs={{0,2},{1,3},{2,0},{3,1},{4,6},{5,7},{6,4},{7,5},{8,10},{9,11},{10,... | collective-permute-start | bytes 3145736 | tf_op jit(solution)/shard_map/ppermute | solution.py:212
  351.0 27.8 %collective-permute-start.51 = (bf16[2,2048,128]{2,1,0:T(8,128)(2,1)}, bf16[2,2048,128]{2,1,0:T(8,128)(2,1)}, u32[]{:S(2)}, u32[]{:S(2)}) collective-permute-start(bf16[2,2048,128]{2,1,0:T(8,128)(2,1)} %pad_maximum_fusion.7), channel_id=1, source_target_pairs={{0,4},{1,5},{2,6},{3,7},{4,0},{5,1},{6,2},{7,3},{8,12},{9,13},{10,... | collective-permute-start | bytes 3145736 | tf_op jit(solution)/shard_map/ppermute | solution.py:212
  387.3 133.6 %all-reduce.8.cloned.1.call-start = ((), (), s32[]{:S(2)}) async-start(), calls=%async_computation.4 | async-start | bytes 2097152 | tf_op jit(solution)/shard_map/psum | solution.py:752
  444.4 151.4 %all-reduce.10.cloned.1.call-start = ((), (), s32[]{:S(2)}) async-start(), calls=%async_computation.5 | async-start | bytes 2097152 | tf_op jit(solution)/shard_map/psum | solution.py:752
  460.2 39.6 %collective-permute-start.62 = (bf16[2,2048,128]{2,1,0:T(8,128)(2,1)S(1)}, bf16[2,2048,128]{2,1,0:T(8,128)(2,1)S(1)}, u32[]{:S(2)}, u32[]{:S(2)}) collective-permute-start(bf16[2,2048,128]{2,1,0:T(8,128)(2,1)S(1)} %pad_maximum_fusion.9), channel_id=1, source_target_pairs={{0,2},{1,3},{2,0},{3,1},{4,6},{5,7},{6,4},{7,5},{8,10},{9,11},{10,... | collective-permute-start | bytes 3145736 | tf_op jit(solution)/shard_map/ppermute | solution.py:212
  461.9 38.0 %collective-permute-start.63 = (bf16[2,2048,128]{2,1,0:T(8,128)(2,1)S(1)}, bf16[2,2048,128]{2,1,0:T(8,128)(2,1)S(1)}, u32[]{:S(2)}, u32[]{:S(2)}) collective-permute-start(bf16[2,2048,128]{2,1,0:T(8,128)(2,1)S(1)} %pad_maximum_fusion.10), channel_id=1, source_target_pairs={{0,4},{1,5},{2,6},{3,7},{4,0},{5,1},{6,2},{7,3},{8,12},{9,13},{10,... | collective-permute-start | bytes 3145736 | tf_op jit(solution)/shard_map/ppermute | solution.py:212
  463.5 27.6 %collective-permute-start.56 = (bf16[384,1024]{1,0:T(8,128)(2,1)S(1)}, bf16[384,1024]{1,0:T(8,128)(2,1)S(1)}, u32[]{:S(2)}, u32[]{:S(2)}) collective-permute-start(bf16[384,1024]{1,0:T(8,128)(2,1)S(1)} %get-tuple-element.431), channel_id=1, source_target_pairs={{0,8},{1,9},{2,10},{3,11},{4,12},{5,13},{6,14},{7,15}} | collective-permute-start | bytes 2359304 | tf_op jit(solution)/shard_map/ppermute | solution.py:583
  493.0 24.4 %collective-permute-start.58 = (bf16[384,1024]{1,0:T(8,128)(2,1)}, bf16[384,1024]{1,0:T(8,128)(2,1)}, u32[]{:S(2)}, u32[]{:S(2)}) collective-permute-start(bf16[384,1024]{1,0:T(8,128)(2,1)} %get-tuple-element.429), channel_id=1, source_target_pairs={{0,8},{8,16},{1,9},{9,17},{2,10},{10,18},{3,11},{11,19},{4,12},{12... | collective-permute-start | bytes 2359304 | tf_op jit(solution)/shard_map/ppermute | solution.py:583
  524.6 53.1 %collective-permute-start.61 = (bf16[384,1024]{1,0:T(8,128)(2,1)}, bf16[384,1024]{1,0:T(8,128)(2,1)}, u32[]{:S(2)}, u32[]{:S(2)}) collective-permute-start(bf16[384,1024]{1,0:T(8,128)(2,1)} %get-tuple-element.427), channel_id=1, source_target_pairs={{8,0},{16,8},{24,16},{9,1},{17,9},{25,17},{10,2},{18,10},{26,18},{... | collective-permute-start | bytes 2359304 | tf_op jit(solution)/shard_map/ppermute | solution.py:583
  526.0 51.7 %collective-permute-start.60 = (bf16[384,1024]{1,0:T(8,128)(2,1)}, bf16[384,1024]{1,0:T(8,128)(2,1)}, u32[]{:S(2)}, u32[]{:S(2)}) collective-permute-start(bf16[384,1024]{1,0:T(8,128)(2,1)} %get-tuple-element.426), channel_id=1, source_target_pairs={{0,8},{8,16},{16,24},{1,9},{9,17},{17,25},{2,10},{10,18},{18,26},{... | collective-permute-start | bytes 2359304 | tf_op jit(solution)/shard_map/ppermute | solution.py:583
  542.0 24.5 %collective-permute-start.69 = (f32[8,19,128]{2,1,0:T(8,128)S(1)}, f32[8,19,128]{2,1,0:T(8,128)S(1)}, u32[]{:S(2)}, u32[]{:S(2)}) collective-permute-start(f32[8,19,128]{2,1,0:T(8,128)S(1)} %add.570), channel_id=1, source_target_pairs={{0,8},{8,0},{16,24},{24,16},{1,9},{9,1},{17,25},{25,17},{2,10},{10... | collective-permute-start | bytes 233480 | tf_op jit(solution)/shard_map/ppermute | solution.py:877
  (137 other events, 1381.6 us)
Sparse Core Ops, SparseCore 0:
  9.6 66.1 all-gather.5
  93.8 28.4 all-gather.3
  336.8 26.8 reduce-scatter.1
  387.4 50.7 all-reduce.5
  444.6 60.3 all-reduce.7
  532.3 63.5 all-reduce.9

commit v5 on v4

--- a/solution.py
+++ b/solution.py
@@ -176,7 +176,7 @@
     nk = kv.shape[0]
     head = width // HEADS
     pairs, pw = HEADS // 2, 2 * head
-    chunk = 512
+    chunk = min(768, nk)
     row_spec = pl.BlockSpec((nq, pw), lambda i, z_ref: (0, first + i))
     key_spec = pl.BlockSpec((nk, pw), lambda i, z_ref: (0, first + i))
     vec_spec = pl.BlockSpec((1, 1, 2 * nq), lambda i, z_ref: (first + i, 0, 0))
@@ -495,7 +495,7 @@
 def gelu_grad(dz, w, slope):
     rows, width = dz.shape
     hidden = w.shape[0]
-    block = 512
+    block = 1024
     wide = pl.BlockSpec((rows, block), lambda i: (0, i))
     return pl.pallas_call(
         gelu_grad_kernel,
@@ -562,8 +562,9 @@
 
 def sum_near(keep, got, *wait):
     keep, got = all_after((keep, got), *wait)
-    term = lambda i, h: add(pick(keep, i, h), pick(got, i, h))
-    xa, yb = jnp.stack([term(1, 0), term(3, 0)]), jnp.stack([term(2, 1), term(3, 1)])
+    half = keep.shape[1] // 2
+    xa = add(keep[1:4:2, :half], got[1:4:2, :half])
+    yb = add(keep[2:4, half:], got[2:4, half:])
     return (swap(xa, 2), swap(yb, 4)), (xa, yb)
 
 
@@ -769,8 +770,6 @@
     g2, s2 = norm_sums(xh3, c3)
     dh2 = dh3 + norm_input_grad(xh3, rs3, gain[2], c3)
     dc = dh2.astype(BF)
-    if fast:
-        dc, c_got = all_after((dc, c_got))
     dcattn = dense_t(dc, w_cout).astype(BF)
     if fast:
         dcattn, *_ = all_after((dcattn,), *d_n)

time: 613 us -> 610 us (level)
    unnamed x169 -> x163, local copies, waits for them, and re-layouts: 12.5 us -> 13.9 us
  transfers between devices with their start and end apart: 77 -> 77, of which waited for: 28 -> 28; matrix products, arithmetic and copies ran while one was open for 18% -> 19% of each run, Pallas kernels for 33% -> 33%
where the time goes in v5:
time: 610 us; the launch traced here: 603 us
  Pallas kernels  217 us (36%)
  waiting for transfers between devices  145 us (24%)
  other arithmetic  96.4 us (16%)
  starting transfers between devices  77.1 us (13%)
  matrix products  27.4 us (4%)
  local copies, waits for them, and re-layouts  24.9 us (4%)
  between operations  15.5 us (3%)
    ppermute x59, waiting for transfers between devices, swap(): return lax.ppermute(v, 'dp', [(i, i ^ bit) for i in range(8)])  68.3 us
    pallas_call x3, Pallas kernels, attn_bwd(): pl.pallas_call(functools.partial(attn_bwd_kernel, head ** (-0.5), chunk,...  47.2 us
    pallas_call x3, Pallas kernels, wgrad(): pl.pallas_call(functools.partial(wgrad_kernel, tuple(counts)), grid_spec=...  45.2 us
    ppermute x59, starting transfers between devices, swap(): return lax.ppermute(v, 'dp', [(i, i ^ bit) for i in range(8)])  44.3 us
    convert_element_type x14, other arithmetic, add(): return total.astype(BF)  39.2 us
    pallas_call x3, Pallas kernels, attn_fwd(): pl.pallas_call(functools.partial(attn_fwd_kernel, head ** (-0.5), chunk),...  32.6 us
    psum x3, waiting for transfers between devices, by_chain(): return lax.psum(v, 'seq', axis_index_groups=[listed])  26.3 us
    ppermute x6, waiting for transfers between devices, shift(): lax.ppermute(v, 'seq', [(a, a + step) for a in pairs if 0 <= a + step < n])  25.8 us
  transfers between devices with their start and end apart: 77, of which 28 were waited for; matrix products, arithmetic and copies ran while one was open for 19% of the time, Pallas kernels for 33%

profile of v5, /device:TPU:0, one launch (start us, length us, event | category | flops | bytes accessed | tf_op | source)
XLA Modules:
  0.0 603.0 jit_solution(9701510780594031200)
XLA Ops:
  15.3 16.5 %collective-permute-done.refs_1_ = bf16[1056,384]{1,0:T(8,128)(2,1)S(1)} collective-permute-done((bf16[1056,384]{1,0:T(8,128)(2,1)S(1)}, bf16[1056,384]{1,0:T(8,128)(2,1)S(1)}, u32[]{:S(2)}, u32[]{:S(2)}) %collective-permute-start) | collective-permute-done | bytes 811040 | tf_op jit(solution)/shard_map/ppermute | solution.py:212
  38.0 7.8 %collective-permute-done.2.refs_3_ = bf16[528,384]{1,0:T(8,128)(2,1)S(1)} collective-permute-done((bf16[528,384]{1,0:T(8,128)(2,1)S(1)}, bf16[528,384]{1,0:T(8,128)(2,1)S(1)}, u32[]{:S(2)}, u32[]{:S(2)}) %collective-permute-start.2) | collective-permute-done | bytes 405536 | tf_op jit(solution)/shard_map/ppermute | solution.py:212
  61.8 11.3 %collective-permute-done.9.refs_1_ = bf16[1024,640]{1,0:T(8,128)(2,1)} collective-permute-done((bf16[1024,640]{1,0:T(8,128)(2,1)S(1)}, bf16[1024,640]{1,0:T(8,128)(2,1)}, u32[]{:S(2)}, u32[]{:S(2)}) %collective-permute-start.9) | collective-permute-done | bytes 1310752 | tf_op jit(solution)/shard_map/ppermute | solution.py:212
  78.5 14.6 %shard_map.273 = (bf16[1536,1024]{1,0:T(8,128)(2,1)}, bf16[384,1024]{1,0:T(8,128)(2,1)}, bf16[1536,2048]{1,0:T(8,128)(2,1)}) custom-call(s32[1]{0:T(128)} %bitcast.1.z_ref, bf16[1536,1024]{1,0:T(8,128)(2,1)} %bitcast.238, bf16[1056,3072]{1,0:T(8,128)(2,1)} %shard_map.272.w_ref.wk_ref.wv_ref, f32[1,1024]{1,0:T(1,128)} %bitcast.264, f32[1,1024]{1,0:T(1,128)} %bitcast.263, ...), custom_call_target="tpu_custom_call" | custom-call | tf_op jit(solution)/shard_map/pallas_call | solution.py:277
  97.7 11.2 %shard_map.274 = (bf16[384,512]{1,0:T(8,128)(2,1)}, f32[4,1,768]{2,1,0:T(1,128)}) custom-call(bf16[384,1024]{1,0:T(8,128)(2,1)} %get-tuple-element.223.q_ref, bf16[1536,2048]{1,0:T(8,128)(2,1)} %get-tuple-element.205.k_ref.v_ref, bf16[1536,2048]{1,0:T(8,128)(2,1)} %get-tuple-element.205.k_ref.v_ref, f32[1536,384]{1,0:T(8,128)} %and_select_fusion.bias_ref), custom_call_target="tpu_custom_call" | custom-call | tf_op jit(solution)/shard_map/pallas_call | solution.py:120
  111.6 8.1 %shard_map.275 = (bf16[1024,2048]{1,0:T(8,128)(2,1)}, bf16[1024,1024]{1,0:T(8,128)(2,1)}, bf16[1024,1024]{1,0:T(8,128)(2,1)}, bf16[1024,1024]{1,0:T(8,128)(2,1)}) custom-call(s32[1]{0:T(128)} %bitcast.me_ref, bf16[1024,640]{1,0:T(8,128)(2,1)} %copy-done.17, bf16[1024,640]{1,0:T(8,128)(2,1)} %collective-permute-done.9.refs_1_, ...), custom_call_target="tpu_custom_call" | custom-call | tf_op jit(solution)/shard_map/pallas_call | solution.py:247
  127.1 11.3 %shard_map.276 = (bf16[384,512]{1,0:T(8,128)(2,1)}, f32[4,1,768]{2,1,0:T(1,128)}) custom-call(bf16[384,1024]{1,0:T(8,128)(2,1)} %get-tuple-element.223.q_ref, bf16[1536,2048]{1,0:T(8,128)(2,1)} %get-tuple-element.205.k_ref.v_ref, bf16[1536,2048]{1,0:T(8,128)(2,1)} %get-tuple-element.205.k_ref.v_ref, f32[1536,384]{1,0:T(8,128)} %and_select_fusion.bias_ref), custom_call_target="tpu_custom_call" | custom-call | tf_op jit(solution)/shard_map/pallas_call | solution.py:120
  156.7 10.1 %shard_map.277 = (bf16[384,1024]{1,0:T(8,128)(2,1)}, f32[8,1,768]{2,1,0:T(1,128)}) custom-call(bf16[384,1024]{1,0:T(8,128)(2,1)} %add_convert_fusion.12.q_ref, bf16[512,2048]{1,0:T(8,128)(2,1)} %add_convert_fusion.k_ref.v_ref, bf16[512,2048]{1,0:T(8,128)(2,1)} %add_convert_fusion.k_ref.v_ref, f32[512,384]{1,0:T(8,128)} %compare_select_fusion.bias_ref), custom_call_target="tpu_custom_call" | custom-call | tf_op jit(solution)/shard_map/pallas_call | solution.py:120
  182.2 12.8 %shard_map.278 = (bf16[1024,4096]{1,0:T(8,128)(2,1)}, bf16[384,4096]{1,0:T(8,128)(2,1)}, bf16[384,4096]{1,0:T(8,128)(2,1)}) custom-call(s32[1]{0:T(128)} %bitcast.me_ref, bf16[1024,512]{1,0:T(8,128)(2,1)} %refs_0_, bf16[1024,512]{1,0:T(8,128)(2,1)} %copy-done.25, bf16[1024,512]{1,0:T(8,128)(2,1)} %collective-permute-done.19.refs_2_, ...), custom_call_target="tpu_custom_call" | custom-call | tf_op jit(solution)/shard_map/pallas_call | solution.py:335
  198.6 11.1 %shard_map.279 = (bf16[4096,1024]{1,0:T(8,128)(2,1)}, f32[384,1024]{1,0:T(8,128)}) custom-call(s32[1]{0:T(128)} %bitcast.me_ref, bf16[4096,128]{1,0:T(8,128)(2,1)} %refs_0_.1, bf16[4096,128]{1,0:T(8,128)(2,1)} %copy-done.26, bf16[4096,128]{1,0:T(8,128)(2,1)} %copy-done.27, bf16[2048,128]{1,0:T(8,128)(2,1)} %copy-done.58, bf16[2048,128]{1,0:T(8,128)(2,1)} %copy-done.60, ...), custom_call_target="tpu_custom_call" | custom-call | tf_op jit(solution)/shard_map/pallas_call | solution.py:335
  215.2 9.5 %shard_map.280 = (bf16[4,4096,128]{2,1,0:T(8,128)(2,1)}, bf16[4,4096,128]{2,1,0:T(8,128)(2,1)}) custom-call(s32[1]{0:T(128)} %bitcast.me_ref, bf16[384,4096]{1,0:T(8,128)(2,1)} %get-tuple-element.263.refs_10_.refs_0_, bf16[1,384,1024]{2,1,0:T(8,128)(2,1)} %bitcast.240, bf16[1,384,1024]{2,1,0:T(8,128)(2,1)} %bitcast.241), custom_call_target="tpu_custom_call" | custom-call | tf_op jit(solution)/shard_map/pallas_call | solution.py:424
  225.1 9.3 %shard_map.281.du_ref = bf16[384,4096]{1,0:T(8,128)(2,1)} custom-call(bf16[384,1024]{1,0:T(8,128)(2,1)} %convert_element_type.562.dz_ref, bf16[4096,1024]{1,0:T(8,128)(2,1)} %get-tuple-element.267.w_ref, bf16[384,4096]{1,0:T(8,128)(2,1)} %get-tuple-element.268.slope_ref), custom_call_target="tpu_custom_call" | custom-call | tf_op jit(solution)/shard_map/pallas_call | solution.py:500
  239.9 15.7 %shard_map.282 = (bf16[4,4096,128]{2,1,0:T(8,128)(2,1)}, bf16[4,4096,128]{2,1,0:T(8,128)(2,1)}, f32[384,1024]{1,0:T(8,128)}) custom-call(s32[1]{0:T(128)} %bitcast.me_ref, bf16[384,1024]{1,0:T(8,128)(2,1)} %add_convert_fusion.11.refs_10_.x_ref, bf16[384,4096]{1,0:T(8,128)(2,1)} %shard_map.281.du_ref, bf16[1024,4096]{1,0:T(8,128)(2,1)} %get-tuple-element.276.w_ref), custom_call_target="tpu_custom_call" | custom-call | tf_op jit(solution)/shard_map/pallas_call | solution.py:476
  276.1 13.7 %shard_map.283 = (bf16[384,1024]{1,0:T(8,128)(2,1)}, bf16[2,512,1024]{2,1,0:T(8,128)(2,1)}) custom-call(s32[1]{0:T(128)} %bitcast.1.z_ref, bf16[384,1024]{1,0:T(8,128)(2,1)} %add_convert_fusion.12.q_ref, bf16[512,2048]{1,0:T(8,128)(2,1)} %add_convert_fusion.k_ref.v_ref, bf16[512,2048]{1,0:T(8,128)(2,1)} %add_convert_fusion.k_ref.v_ref, ...), custom_call_target="tpu_custom_call" | custom-call | tf_op jit(solution)/shard_map/pallas_call | solution.py:184
  301.6 14.2 %shard_map.284 = (bf16[4,4096,128]{2,1,0:T(8,128)(2,1)}, bf16[4,4096,128]{2,1,0:T(8,128)(2,1)}) custom-call(s32[1]{0:T(128)} %bitcast.me_ref, bf16[384,1024]{1,0:T(8,128)(2,1)} %get-tuple-element.243.out_ref.refs_0_, bf16[1,384,1024]{2,1,0:T(8,128)(2,1)} %convert_bitcast_fusion.2.refs_1_.refs_2_, ...), custom_call_target="tpu_custom_call" | custom-call | tf_op jit(solution)/shard_map/pallas_call | solution.py:424
  355.5 20.1 %shard_map.285 = (bf16[384,1024]{1,0:T(8,128)(2,1)}, bf16[3,1536,1024]{2,1,0:T(8,128)(2,1)}) custom-call(s32[1]{0:T(128)} %bitcast.1.z_ref, bf16[384,1024]{1,0:T(8,128)(2,1)} %get-tuple-element.223.q_ref, bf16[1536,2048]{1,0:T(8,128)(2,1)} %get-tuple-element.205.k_ref.v_ref, bf16[1536,2048]{1,0:T(8,128)(2,1)} %get-tuple-element.205.k_ref.v_ref, ...), custom_call_target="tpu_custom_call" | custom-call | tf_op jit(solution)/shard_map/pallas_call | solution.py:184
  383.8 13.4 %shard_map.286 = (bf16[384,1024]{1,0:T(8,128)(2,1)}, bf16[3,1536,1024]{2,1,0:T(8,128)(2,1)}) custom-call(s32[1]{0:T(128)} %bitcast.1.z_ref, bf16[384,1024]{1,0:T(8,128)(2,1)} %get-tuple-element.223.q_ref, bf16[1536,2048]{1,0:T(8,128)(2,1)} %get-tuple-element.205.k_ref.v_ref, ...), custom_call_target="tpu_custom_call", output_to_operand_aliasing={{0}: (8, {}), {1}: (9, {})} | custom-call | tf_op jit(solution)/shard_map/pallas_call | solution.py:184
  401.0 21.5 %shard_map.287 = (bf16[4,4096,128]{2,1,0:T(8,128)(2,1)}, bf16[4,4096,128]{2,1,0:T(8,128)(2,1)}) custom-call(s32[1]{0:T(128)} %bitcast.me_ref, bf16[384,1024]{1,0:T(8,128)(2,1)} %copy-done.11, bf16[1,384,1024]{2,1,0:T(8,128)(2,1)} %bitcast.242, bf16[1,384,1024]{2,1,0:T(8,128)(2,1)} %bitcast.243, bf16[1536,1024]{1,0:T(8,128)(2,1)} %get-tuple-element.337.refs_3_, ...), custom_call_target="tpu_custom_call" | custom-call | tf_op jit(solution)/shard_map/pallas_call | solution.py:424
  422.5 12.5 %all-reduce.6.cloned.1.call-done = bf16[4096,128]{1,0:T(8,128)(2,1)} async-done(((bf16[4096,128]{1,0:T(8,128)(2,1)}), bf16[4096,128]{1,0:T(8,128)(2,1)}) %all-reduce.6.cloned.1.call-update) | async-done | bytes 1048592 | tf_op jit(solution)/shard_map/psum | solution.py:753
  441.3 13.5 %shard_map.288 = (bf16[4,384,1024]{2,1,0:T(8,128)(2,1)}, f32[8,1024]{1,0:T(8,128)}) custom-call(bf16[3,1536,1024]{2,1,0:T(8,128)(2,1)} %get-tuple-element.341.refs_4_.refs_5_.refs_6_.refs_7_.refs_8_.refs_9_.dk_ref.dv_ref, bf16[3,1536,1024]{2,1,0:T(8,128)(2,1)} %get-tuple-element.341.refs_4_.refs_5_.refs_6_.refs_7_.refs_8_.refs_9_.dk_ref.dv_ref, ...), custom_call_target="tpu_custom_call" | custom-call | tf_op jit(solution)/shard_map/pallas_call | solution.py:531
  469.5 17.3 %collective-permute-done.56 = bf16[384,1024]{1,0:T(8,128)(2,1)S(1)} collective-permute-done((bf16[384,1024]{1,0:T(8,128)(2,1)S(1)}, bf16[384,1024]{1,0:T(8,128)(2,1)S(1)}, u32[]{:S(2)}, u32[]{:S(2)}) %collective-permute-start.56) | collective-permute-done | bytes 786464 | tf_op jit(solution)/shard_map/ppermute | solution.py:584
  505.6 8.5 %collective-permute-done.58 = bf16[384,1024]{1,0:T(8,128)(2,1)} collective-permute-done((bf16[384,1024]{1,0:T(8,128)(2,1)}, bf16[384,1024]{1,0:T(8,128)(2,1)}, u32[]{:S(2)}, u32[]{:S(2)}) %collective-permute-start.58) | collective-permute-done | bytes 786464 | tf_op jit(solution)/shard_map/ppermute | solution.py:584
  542.6 19.5 %collective-permute-done.69 = f32[8,19,128]{2,1,0:T(8,128)S(1)} collective-permute-done((f32[8,19,128]{2,1,0:T(8,128)S(1)}, f32[8,19,128]{2,1,0:T(8,128)S(1)}, u32[]{:S(2)}, u32[]{:S(2)}) %collective-permute-start.69) | collective-permute-done | bytes 77856 | tf_op jit(solution)/shard_map/ppermute | solution.py:876
  578.8 13.8 %all-reduce.10.cloned.1.call-done = bf16[4096,128]{1,0:T(8,128)(2,1)} async-done(((bf16[4096,128]{1,0:T(8,128)(2,1)}), bf16[4096,128]{1,0:T(8,128)(2,1)}) %all-reduce.10.cloned.1.call-update) | async-done | bytes 1048592 | tf_op jit(solution)/shard_map/psum | solution.py:753
  (441 shorter events, 270.3 us)
Async XLA Ops:
  7.2 71.3 %all-gather.6.cloned.1.call-start = ((), (), s32[]{:S(2)}) async-start(), calls=%async_computation.6 | async-start | bytes 3932160 | tf_op jit(solution)/shard_map/all_gather | solution.py:652
  7.9 114.4 %all-gather.4.cloned.1.call-start = ((), (), s32[]{:S(2)}) async-start(), calls=%async_computation.1 | async-start | bytes 1310720 | tf_op jit(solution)/shard_map/all_gather | solution.py:655
  35.8 37.2 %collective-permute-start.9 = (bf16[1024,640]{1,0:T(8,128)(2,1)S(1)}, bf16[1024,640]{1,0:T(8,128)(2,1)}, u32[]{:S(2)}, u32[]{:S(2)}) collective-permute-start(bf16[1024,640]{1,0:T(8,128)(2,1)S(1)} %pad_maximum_fusion.refs_0_), channel_id=1, source_target_pairs={{0,2},{1,3},{2,0},{3,1},{4,6},{5,7},{6,4},{7,5},{8,10},{9,11},{10,... | collective-permute-start | bytes 3932168 | tf_op jit(solution)/shard_map/ppermute | solution.py:212
  37.4 35.7 %collective-permute-start.10 = (bf16[1024,640]{1,0:T(8,128)(2,1)S(1)}, bf16[1024,640]{1,0:T(8,128)(2,1)}, u32[]{:S(2)}, u32[]{:S(2)}) collective-permute-start(bf16[1024,640]{1,0:T(8,128)(2,1)S(1)} %pad_maximum_fusion.refs_0_), channel_id=1, source_target_pairs={{0,4},{1,5},{2,6},{3,7},{4,0},{5,1},{6,2},{7,3},{8,12},{9,13},{10,... | collective-permute-start | bytes 3932168 | tf_op jit(solution)/shard_map/ppermute | solution.py:212
  93.7 282.0 %reduce-scatter.2.cloned.1.call-start = ((), (), s32[]{:S(2)}) async-start(), calls=%async_computation.2 | async-start | bytes 1310720 | tf_op jit(solution)/shard_map/reduce_scatter | solution.py:817
  95.4 25.4 %collective-permute-start.18 = (bf16[1024,512]{1,0:T(8,128)(2,1)}, bf16[1024,512]{1,0:T(8,128)(2,1)S(1)}, u32[]{:S(2)}, u32[]{:S(2)}) collective-permute-start(bf16[1024,512]{1,0:T(8,128)(2,1)} %refs_0_), channel_id=1, source_target_pairs={{0,2},{1,3},{2,0},{3,1},{4,6},{5,7},{6,4},{7,5},{8,10},{9,11},{10,... | collective-permute-start | bytes 3145736 | tf_op jit(solution)/shard_map/ppermute | solution.py:212
  96.6 25.5 %collective-permute-start.19 = (bf16[1024,512]{1,0:T(8,128)(2,1)}, bf16[1024,512]{1,0:T(8,128)(2,1)}, u32[]{:S(2)}, u32[]{:S(2)}) collective-permute-start(bf16[1024,512]{1,0:T(8,128)(2,1)} %refs_0_), channel_id=1, source_target_pairs={{0,4},{1,5},{2,6},{3,7},{4,0},{5,1},{6,2},{7,3},{8,12},{9,13},{10,... | collective-permute-start | bytes 3145736 | tf_op jit(solution)/shard_map/ppermute | solution.py:212
  147.6 25.1 %collective-permute-start.22 = (bf16[4096,128]{1,0:T(8,128)(2,1)S(1)}, bf16[4096,128]{1,0:T(8,128)(2,1)S(1)}, u32[]{:S(2)}, u32[]{:S(2)}) collective-permute-start(bf16[4096,128]{1,0:T(8,128)(2,1)S(1)} %copy-done.37), channel_id=1, source_target_pairs={{0,2},{1,3},{2,0},{3,1},{4,6},{5,7},{6,4},{7,5},{8,10},{9,11},{10,... | collective-permute-start | bytes 3145736 | tf_op jit(solution)/shard_map/ppermute | solution.py:212
  237.8 25.4 %collective-permute-start.37 = (bf16[2,2048,128]{2,1,0:T(8,128)(2,1)}, bf16[2,2048,128]{2,1,0:T(8,128)(2,1)S(1)}, u32[]{:S(2)}, u32[]{:S(2)}) collective-permute-start(bf16[2,2048,128]{2,1,0:T(8,128)(2,1)} %get-tuple-element.413), channel_id=1, source_target_pairs={{0,2},{1,3},{2,0},{3,1},{4,6},{5,7},{6,4},{7,5},{8,10},{9,11},{10,... | collective-permute-start | bytes 3145736 | tf_op jit(solution)/shard_map/ppermute | solution.py:212
  238.4 25.1 %collective-permute-start.38 = (bf16[2,2048,128]{2,1,0:T(8,128)(2,1)}, bf16[2,2048,128]{2,1,0:T(8,128)(2,1)S(1)}, u32[]{:S(2)}, u32[]{:S(2)}) collective-permute-start(bf16[2,2048,128]{2,1,0:T(8,128)(2,1)} %get-tuple-element.412), channel_id=1, source_target_pairs={{0,4},{1,5},{2,6},{3,7},{4,0},{5,1},{6,2},{7,3},{8,12},{9,13},{10,... | collective-permute-start | bytes 3145736 | tf_op jit(solution)/shard_map/ppermute | solution.py:212
  264.5 25.3 %collective-permute-start.41 = (bf16[4,4096,128]{2,1,0:T(8,128)(2,1)}, bf16[4,4096,128]{2,1,0:T(8,128)(2,1)}, u32[]{:S(2)}, u32[]{:S(2)}) collective-permute-start(bf16[4,4096,128]{2,1,0:T(8,128)(2,1)} %get-tuple-element.294), channel_id=1, source_target_pairs={{0,1},{1,0},{2,3},{3,2},{4,5},{5,4},{6,7},{7,6},{8,9},{9,8},{10,11... | collective-permute-start | bytes 12582920 | tf_op jit(solution)/shard_map/ppermute | solution.py:212
  293.7 25.2 %collective-permute-start.43 = (bf16[2,2048,128]{2,1,0:T(8,128)(2,1)}, bf16[2,2048,128]{2,1,0:T(8,128)(2,1)}, u32[]{:S(2)}, u32[]{:S(2)}) collective-permute-start(bf16[2,2048,128]{2,1,0:T(8,128)(2,1)} %get-tuple-element.407), channel_id=1, source_target_pairs={{0,2},{1,3},{2,0},{3,1},{4,6},{5,7},{6,4},{7,5},{8,10},{9,11},{10,... | collective-permute-start | bytes 3145736 | tf_op jit(solution)/shard_map/ppermute | solution.py:212
  294.3 24.9 %collective-permute-start.44 = (bf16[2,2048,128]{2,1,0:T(8,128)(2,1)}, bf16[2,2048,128]{2,1,0:T(8,128)(2,1)}, u32[]{:S(2)}, u32[]{:S(2)}) collective-permute-start(bf16[2,2048,128]{2,1,0:T(8,128)(2,1)} %get-tuple-element.406), channel_id=1, source_target_pairs={{0,4},{1,5},{2,6},{3,7},{4,0},{5,1},{6,2},{7,3},{8,12},{9,13},{10,... | collective-permute-start | bytes 3145736 | tf_op jit(solution)/shard_map/ppermute | solution.py:212
  334.5 100.5 %all-reduce.6.cloned.1.call-start = ((), (), s32[]{:S(2)}) async-start(), calls=%async_computation.3 | async-start | bytes 2097152 | tf_op jit(solution)/shard_map/psum | solution.py:753
  347.2 28.5 %collective-permute-start.50 = (bf16[2,2048,128]{2,1,0:T(8,128)(2,1)}, bf16[2,2048,128]{2,1,0:T(8,128)(2,1)}, u32[]{:S(2)}, u32[]{:S(2)}) collective-permute-start(bf16[2,2048,128]{2,1,0:T(8,128)(2,1)} %get-tuple-element.401), channel_id=1, source_target_pairs={{0,2},{1,3},{2,0},{3,1},{4,6},{5,7},{6,4},{7,5},{8,10},{9,11},{10,... | collective-permute-start | bytes 3145736 | tf_op jit(solution)/shard_map/ppermute | solution.py:212
  348.4 27.3 %collective-permute-start.51 = (bf16[2,2048,128]{2,1,0:T(8,128)(2,1)}, bf16[2,2048,128]{2,1,0:T(8,128)(2,1)}, u32[]{:S(2)}, u32[]{:S(2)}) collective-permute-start(bf16[2,2048,128]{2,1,0:T(8,128)(2,1)} %get-tuple-element.400), channel_id=1, source_target_pairs={{0,4},{1,5},{2,6},{3,7},{4,0},{5,1},{6,2},{7,3},{8,12},{9,13},{10,... | collective-permute-start | bytes 3145736 | tf_op jit(solution)/shard_map/ppermute | solution.py:212
  383.8 133.7 %all-reduce.8.cloned.1.call-start = ((), (), s32[]{:S(2)}) async-start(), calls=%async_computation.4 | async-start | bytes 2097152 | tf_op jit(solution)/shard_map/psum | solution.py:753
  441.3 151.4 %all-reduce.10.cloned.1.call-start = ((), (), s32[]{:S(2)}) async-start(), calls=%async_computation.5 | async-start | bytes 2097152 | tf_op jit(solution)/shard_map/psum | solution.py:753
  457.1 38.4 %collective-permute-start.62 = (bf16[2,2048,128]{2,1,0:T(8,128)(2,1)S(1)}, bf16[2,2048,128]{2,1,0:T(8,128)(2,1)S(1)}, u32[]{:S(2)}, u32[]{:S(2)}) collective-permute-start(bf16[2,2048,128]{2,1,0:T(8,128)(2,1)S(1)} %get-tuple-element.395), channel_id=1, source_target_pairs={{0,2},{1,3},{2,0},{3,1},{4,6},{5,7},{6,4},{7,5},{8,10},{9,11},{10,... | collective-permute-start | bytes 3145736 | tf_op jit(solution)/shard_map/ppermute | solution.py:212
  458.6 36.9 %collective-permute-start.63 = (bf16[2,2048,128]{2,1,0:T(8,128)(2,1)S(1)}, bf16[2,2048,128]{2,1,0:T(8,128)(2,1)S(1)}, u32[]{:S(2)}, u32[]{:S(2)}) collective-permute-start(bf16[2,2048,128]{2,1,0:T(8,128)(2,1)S(1)} %get-tuple-element.394), channel_id=1, source_target_pairs={{0,4},{1,5},{2,6},{3,7},{4,0},{5,1},{6,2},{7,3},{8,12},{9,13},{10,... | collective-permute-start | bytes 3145736 | tf_op jit(solution)/shard_map/ppermute | solution.py:212
  460.2 26.5 %collective-permute-start.56 = (bf16[384,1024]{1,0:T(8,128)(2,1)S(1)}, bf16[384,1024]{1,0:T(8,128)(2,1)S(1)}, u32[]{:S(2)}, u32[]{:S(2)}) collective-permute-start(bf16[384,1024]{1,0:T(8,128)(2,1)S(1)} %get-tuple-element.419), channel_id=1, source_target_pairs={{0,8},{1,9},{2,10},{3,11},{4,12},{5,13},{6,14},{7,15}} | collective-permute-start | bytes 2359304 | tf_op jit(solution)/shard_map/ppermute | solution.py:584
  488.6 25.5 %collective-permute-start.58 = (bf16[384,1024]{1,0:T(8,128)(2,1)}, bf16[384,1024]{1,0:T(8,128)(2,1)}, u32[]{:S(2)}, u32[]{:S(2)}) collective-permute-start(bf16[384,1024]{1,0:T(8,128)(2,1)} %get-tuple-element.417), channel_id=1, source_target_pairs={{0,8},{8,16},{1,9},{9,17},{2,10},{10,18},{3,11},{11,19},{4,12},{12... | collective-permute-start | bytes 2359304 | tf_op jit(solution)/shard_map/ppermute | solution.py:584
  521.2 53.3 %collective-permute-start.61 = (bf16[384,1024]{1,0:T(8,128)(2,1)}, bf16[384,1024]{1,0:T(8,128)(2,1)}, u32[]{:S(2)}, u32[]{:S(2)}) collective-permute-start(bf16[384,1024]{1,0:T(8,128)(2,1)} %get-tuple-element.415), channel_id=1, source_target_pairs={{8,0},{16,8},{24,16},{9,1},{17,9},{25,17},{10,2},{18,10},{26,18},{... | collective-permute-start | bytes 2359304 | tf_op jit(solution)/shard_map/ppermute | solution.py:584
  522.7 51.9 %collective-permute-start.60 = (bf16[384,1024]{1,0:T(8,128)(2,1)}, bf16[384,1024]{1,0:T(8,128)(2,1)}, u32[]{:S(2)}, u32[]{:S(2)}) collective-permute-start(bf16[384,1024]{1,0:T(8,128)(2,1)} %get-tuple-element.414), channel_id=1, source_target_pairs={{0,8},{8,16},{16,24},{1,9},{9,17},{17,25},{2,10},{10,18},{18,26},{... | collective-permute-start | bytes 2359304 | tf_op jit(solution)/shard_map/ppermute | solution.py:584
  (134 other events, 1404.8 us)
Sparse Core Ops, SparseCore 0:
  9.6 66.1 all-gather.5
  93.8 28.4 all-gather.3
  334.6 27.8 reduce-scatter.1
  383.9 51.0 all-reduce.5
  441.4 61.3 all-reduce.7
  529.0 63.6 all-reduce.9

commit v6 on v5

--- a/solution.py
+++ b/solution.py
@@ -116,7 +116,7 @@
     nk = kv.shape[0]
     head = width // HEADS
     pairs, pw = HEADS // 2, 2 * head
-    chunk = 512
+    chunk = min(768, nk)
     return pl.pallas_call(
         functools.partial(attn_fwd_kernel, head**-0.5, chunk),
         grid=(count,),
@@ -495,7 +495,7 @@
 def gelu_grad(dz, w, slope):
     rows, width = dz.shape
     hidden = w.shape[0]
-    block = 1024
+    block = 2048
     wide = pl.BlockSpec((rows, block), lambda i: (0, i))
     return pl.pallas_call(
         gelu_grad_kernel,
@@ -801,8 +801,6 @@
     g1, s1 = norm_sums(xh2, c2)
     dh1 = dh2 + norm_input_grad(xh2, rs2, gain[1], c2)
     da = dh1.astype(BF)
-    if fast:
-        da, e_got = all_after((da, e_got))
     dattn = dense_t(da, w_out).astype(BF)
     if fast:
         dattn, d_got_b = all_after((dattn, d_got_b), *c_f)

time: 610 us -> 609 us (level)
  transfers between devices with their start and end apart: 77 -> 77, of which waited for: 28 -> 29; matrix products, arithmetic and copies ran while one was open for 19% -> 19% of each run, Pallas kernels for 33% -> 32%
where the time goes in v6:
time: 609 us; the launch traced here: 602 us
  Pallas kernels  215 us (35%)
  waiting for transfers between devices  144 us (24%)
  other arithmetic  98.8 us (16%)
  starting transfers between devices  77.5 us (13%)
  matrix products  27.4 us (4%)
  local copies, waits for them, and re-layouts  23.8 us (4%)
  between operations  15.5 us (3%)
    ppermute x59, waiting for transfers between devices, swap(): return lax.ppermute(v, 'dp', [(i, i ^ bit) for i in range(8)])  69.8 us
    pallas_call x3, Pallas kernels, attn_bwd(): pl.pallas_call(functools.partial(attn_bwd_kernel, head ** (-0.5), chunk,...  47.4 us
    pallas_call x3, Pallas kernels, wgrad(): pl.pallas_call(functools.partial(wgrad_kernel, tuple(counts)), grid_spec=...  44.8 us
    ppermute x59, starting transfers between devices, swap(): return lax.ppermute(v, 'dp', [(i, i ^ bit) for i in range(8)])  44.2 us
    convert_element_type x14, other arithmetic, add(): return total.astype(BF)  39.3 us
    pallas_call x3, Pallas kernels, attn_fwd(): pl.pallas_call(functools.partial(attn_fwd_kernel, head ** (-0.5), chunk),...  32.6 us
    ppermute x6, waiting for transfers between devices, shift(): lax.ppermute(v, 'seq', [(a, a + step) for a in pairs if 0 <= a + step < n])  25.9 us
    pallas_call x2, Pallas kernels, assemble_dot(): pl.pallas_call(functools.partial(assemble_dot_kernel, gelu), grid_spec=pl...  23.9 us
  transfers between devices with their start and end apart: 77, of which 29 were waited for; matrix products, arithmetic and copies ran while one was open for 19% of the time, Pallas kernels for 32%

profile of v6, /device:TPU:0, one launch (start us, length us, event | category | flops | bytes accessed | tf_op | source)
XLA Modules:
  0.0 602.1 jit_solution(9433852435145589179)
XLA Ops:
  15.3 16.5 %collective-permute-done.refs_1_ = bf16[1056,384]{1,0:T(8,128)(2,1)S(1)} collective-permute-done((bf16[1056,384]{1,0:T(8,128)(2,1)S(1)}, bf16[1056,384]{1,0:T(8,128)(2,1)S(1)}, u32[]{:S(2)}, u32[]{:S(2)}) %collective-permute-start) | collective-permute-done | bytes 811040 | tf_op jit(solution)/shard_map/ppermute | solution.py:212
  38.0 7.8 %collective-permute-done.2.refs_3_ = bf16[528,384]{1,0:T(8,128)(2,1)S(1)} collective-permute-done((bf16[528,384]{1,0:T(8,128)(2,1)S(1)}, bf16[528,384]{1,0:T(8,128)(2,1)S(1)}, u32[]{:S(2)}, u32[]{:S(2)}) %collective-permute-start.2) | collective-permute-done | bytes 405536 | tf_op jit(solution)/shard_map/ppermute | solution.py:212
  61.8 11.3 %collective-permute-done.9.refs_1_ = bf16[1024,640]{1,0:T(8,128)(2,1)} collective-permute-done((bf16[1024,640]{1,0:T(8,128)(2,1)S(1)}, bf16[1024,640]{1,0:T(8,128)(2,1)}, u32[]{:S(2)}, u32[]{:S(2)}) %collective-permute-start.9) | collective-permute-done | bytes 1310752 | tf_op jit(solution)/shard_map/ppermute | solution.py:212
  78.5 14.6 %shard_map.273 = (bf16[1536,1024]{1,0:T(8,128)(2,1)}, bf16[384,1024]{1,0:T(8,128)(2,1)}, bf16[1536,2048]{1,0:T(8,128)(2,1)}) custom-call(s32[1]{0:T(128)} %bitcast.1.z_ref, bf16[1536,1024]{1,0:T(8,128)(2,1)} %bitcast.238, bf16[1056,3072]{1,0:T(8,128)(2,1)} %shard_map.272.w_ref.wk_ref.wv_ref, f32[1,1024]{1,0:T(1,128)} %bitcast.262, f32[1,1024]{1,0:T(1,128)} %bitcast.261, ...), custom_call_target="tpu_custom_call" | custom-call | tf_op jit(solution)/shard_map/pallas_call | solution.py:277
  97.7 11.2 %shard_map.274 = (bf16[384,512]{1,0:T(8,128)(2,1)}, f32[4,1,768]{2,1,0:T(1,128)}) custom-call(bf16[384,1024]{1,0:T(8,128)(2,1)} %get-tuple-element.221.q_ref, bf16[1536,2048]{1,0:T(8,128)(2,1)} %get-tuple-element.203.k_ref.v_ref, bf16[1536,2048]{1,0:T(8,128)(2,1)} %get-tuple-element.203.k_ref.v_ref, f32[1536,384]{1,0:T(8,128)} %and_select_fusion.bias_ref), custom_call_target="tpu_custom_call" | custom-call | tf_op jit(solution)/shard_map/pallas_call | solution.py:120
  111.6 8.1 %shard_map.275 = (bf16[1024,2048]{1,0:T(8,128)(2,1)}, bf16[1024,1024]{1,0:T(8,128)(2,1)}, bf16[1024,1024]{1,0:T(8,128)(2,1)}, bf16[1024,1024]{1,0:T(8,128)(2,1)}) custom-call(s32[1]{0:T(128)} %bitcast.me_ref, bf16[1024,640]{1,0:T(8,128)(2,1)} %copy-done.16, bf16[1024,640]{1,0:T(8,128)(2,1)} %collective-permute-done.9.refs_1_, ...), custom_call_target="tpu_custom_call" | custom-call | tf_op jit(solution)/shard_map/pallas_call | solution.py:247
  127.1 11.3 %shard_map.276 = (bf16[384,512]{1,0:T(8,128)(2,1)}, f32[4,1,768]{2,1,0:T(1,128)}) custom-call(bf16[384,1024]{1,0:T(8,128)(2,1)} %get-tuple-element.221.q_ref, bf16[1536,2048]{1,0:T(8,128)(2,1)} %get-tuple-element.203.k_ref.v_ref, bf16[1536,2048]{1,0:T(8,128)(2,1)} %get-tuple-element.203.k_ref.v_ref, f32[1536,384]{1,0:T(8,128)} %and_select_fusion.bias_ref), custom_call_target="tpu_custom_call" | custom-call | tf_op jit(solution)/shard_map/pallas_call | solution.py:120
  156.6 10.1 %shard_map.277 = (bf16[384,1024]{1,0:T(8,128)(2,1)}, f32[8,1,768]{2,1,0:T(1,128)}) custom-call(bf16[384,1024]{1,0:T(8,128)(2,1)} %add_convert_fusion.12.q_ref, bf16[512,2048]{1,0:T(8,128)(2,1)} %add_convert_fusion.k_ref.v_ref, bf16[512,2048]{1,0:T(8,128)(2,1)} %add_convert_fusion.k_ref.v_ref, f32[512,384]{1,0:T(8,128)} %compare_select_fusion.bias_ref), custom_call_target="tpu_custom_call" | custom-call | tf_op jit(solution)/shard_map/pallas_call | solution.py:120
  182.1 12.8 %shard_map.278 = (bf16[1024,4096]{1,0:T(8,128)(2,1)}, bf16[384,4096]{1,0:T(8,128)(2,1)}, bf16[384,4096]{1,0:T(8,128)(2,1)}) custom-call(s32[1]{0:T(128)} %bitcast.me_ref, bf16[1024,512]{1,0:T(8,128)(2,1)} %refs_0_, bf16[1024,512]{1,0:T(8,128)(2,1)} %copy-done.24, bf16[1024,512]{1,0:T(8,128)(2,1)} %collective-permute-done.19.refs_2_, ...), custom_call_target="tpu_custom_call" | custom-call | tf_op jit(solution)/shard_map/pallas_call | solution.py:335
  198.6 11.1 %shard_map.279 = (bf16[4096,1024]{1,0:T(8,128)(2,1)}, f32[384,1024]{1,0:T(8,128)}) custom-call(s32[1]{0:T(128)} %bitcast.me_ref, bf16[4096,128]{1,0:T(8,128)(2,1)} %refs_0_.1, bf16[4096,128]{1,0:T(8,128)(2,1)} %copy-done.25, bf16[4096,128]{1,0:T(8,128)(2,1)} %copy-done.26, bf16[2048,128]{1,0:T(8,128)(2,1)} %copy-done.58, bf16[2048,128]{1,0:T(8,128)(2,1)} %copy-done.60, ...), custom_call_target="tpu_custom_call" | custom-call | tf_op jit(solution)/shard_map/pallas_call | solution.py:335
  215.1 9.5 %shard_map.280 = (bf16[4,4096,128]{2,1,0:T(8,128)(2,1)}, bf16[4,4096,128]{2,1,0:T(8,128)(2,1)}) custom-call(s32[1]{0:T(128)} %bitcast.me_ref, bf16[384,4096]{1,0:T(8,128)(2,1)} %get-tuple-element.261.refs_10_.refs_0_, bf16[1,384,1024]{2,1,0:T(8,128)(2,1)} %bitcast.240, bf16[1,384,1024]{2,1,0:T(8,128)(2,1)} %bitcast.241), custom_call_target="tpu_custom_call" | custom-call | tf_op jit(solution)/shard_map/pallas_call | solution.py:424
  225.1 8.1 %shard_map.281.du_ref = bf16[384,4096]{1,0:T(8,128)(2,1)} custom-call(bf16[384,1024]{1,0:T(8,128)(2,1)} %convert_element_type.562.dz_ref, bf16[4096,1024]{1,0:T(8,128)(2,1)} %get-tuple-element.265.w_ref, bf16[384,4096]{1,0:T(8,128)(2,1)} %get-tuple-element.266.slope_ref), custom_call_target="tpu_custom_call" | custom-call | tf_op jit(solution)/shard_map/pallas_call | solution.py:500
  238.6 15.7 %shard_map.282 = (bf16[4,4096,128]{2,1,0:T(8,128)(2,1)}, bf16[4,4096,128]{2,1,0:T(8,128)(2,1)}, f32[384,1024]{1,0:T(8,128)}) custom-call(s32[1]{0:T(128)} %bitcast.me_ref, bf16[384,1024]{1,0:T(8,128)(2,1)} %add_convert_fusion.11.refs_10_.x_ref, bf16[384,4096]{1,0:T(8,128)(2,1)} %shard_map.281.du_ref, bf16[1024,4096]{1,0:T(8,128)(2,1)} %get-tuple-element.274.w_ref), custom_call_target="tpu_custom_call" | custom-call | tf_op jit(solution)/shard_map/pallas_call | solution.py:476
  274.8 14.0 %shard_map.283 = (bf16[384,1024]{1,0:T(8,128)(2,1)}, bf16[2,512,1024]{2,1,0:T(8,128)(2,1)}) custom-call(s32[1]{0:T(128)} %bitcast.1.z_ref, bf16[384,1024]{1,0:T(8,128)(2,1)} %add_convert_fusion.12.q_ref, bf16[512,2048]{1,0:T(8,128)(2,1)} %add_convert_fusion.k_ref.v_ref, bf16[512,2048]{1,0:T(8,128)(2,1)} %add_convert_fusion.k_ref.v_ref, ...), custom_call_target="tpu_custom_call" | custom-call | tf_op jit(solution)/shard_map/pallas_call | solution.py:184
  300.7 13.7 %shard_map.284 = (bf16[4,4096,128]{2,1,0:T(8,128)(2,1)}, bf16[4,4096,128]{2,1,0:T(8,128)(2,1)}) custom-call(s32[1]{0:T(128)} %bitcast.me_ref, bf16[384,1024]{1,0:T(8,128)(2,1)} %get-tuple-element.241.out_ref.refs_0_, bf16[1,384,1024]{2,1,0:T(8,128)(2,1)} %convert_bitcast_fusion.3.refs_1_.refs_2_, ...), custom_call_target="tpu_custom_call" | custom-call | tf_op jit(solution)/shard_map/pallas_call | solution.py:424
  354.7 20.0 %shard_map.285 = (bf16[384,1024]{1,0:T(8,128)(2,1)}, bf16[3,1536,1024]{2,1,0:T(8,128)(2,1)}) custom-call(s32[1]{0:T(128)} %bitcast.1.z_ref, bf16[384,1024]{1,0:T(8,128)(2,1)} %get-tuple-element.221.q_ref, bf16[1536,2048]{1,0:T(8,128)(2,1)} %get-tuple-element.203.k_ref.v_ref, bf16[1536,2048]{1,0:T(8,128)(2,1)} %get-tuple-element.203.k_ref.v_ref, ...), custom_call_target="tpu_custom_call" | custom-call | tf_op jit(solution)/shard_map/pallas_call | solution.py:184
  385.5 13.4 %shard_map.286 = (bf16[384,1024]{1,0:T(8,128)(2,1)}, bf16[3,1536,1024]{2,1,0:T(8,128)(2,1)}) custom-call(s32[1]{0:T(128)} %bitcast.1.z_ref, bf16[384,1024]{1,0:T(8,128)(2,1)} %get-tuple-element.221.q_ref, bf16[1536,2048]{1,0:T(8,128)(2,1)} %get-tuple-element.203.k_ref.v_ref, ...), custom_call_target="tpu_custom_call", output_to_operand_aliasing={{0}: (8, {}), {1}: (9, {})} | custom-call | tf_op jit(solution)/shard_map/pallas_call | solution.py:184
  402.7 21.5 %shard_map.287 = (bf16[4,4096,128]{2,1,0:T(8,128)(2,1)}, bf16[4,4096,128]{2,1,0:T(8,128)(2,1)}) custom-call(s32[1]{0:T(128)} %bitcast.me_ref, bf16[384,1024]{1,0:T(8,128)(2,1)} %copy-done.11, bf16[1,384,1024]{2,1,0:T(8,128)(2,1)} %convert_bitcast_fusion.2.refs_1_.refs_2_, bf16[1,384,1024]{2,1,0:T(8,128)(2,1)} %convert_bitcast_fusion.2.refs_1_.refs_2_, ...), custom_call_target="tpu_custom_call" | custom-call | tf_op jit(solution)/shard_map/pallas_call | solution.py:424
  424.2 9.9 %all-reduce.6.cloned.1.call-done = bf16[4096,128]{1,0:T(8,128)(2,1)} async-done(((bf16[4096,128]{1,0:T(8,128)(2,1)}), bf16[4096,128]{1,0:T(8,128)(2,1)}) %all-reduce.6.cloned.1.call-update) | async-done | bytes 1048592 | tf_op jit(solution)/shard_map/psum | solution.py:753
  440.6 13.2 %shard_map.288 = (bf16[4,384,1024]{2,1,0:T(8,128)(2,1)}, f32[8,1024]{1,0:T(8,128)}) custom-call(bf16[3,1536,1024]{2,1,0:T(8,128)(2,1)} %get-tuple-element.337.refs_4_.refs_5_.refs_6_.refs_7_.refs_8_.refs_9_.dk_ref.dv_ref, bf16[3,1536,1024]{2,1,0:T(8,128)(2,1)} %get-tuple-element.337.refs_4_.refs_5_.refs_6_.refs_7_.refs_8_.refs_9_.dk_ref.dv_ref, ...), custom_call_target="tpu_custom_call" | custom-call | tf_op jit(solution)/shard_map/pallas_call | solution.py:531
  468.6 17.4 %collective-permute-done.56 = bf16[384,1024]{1,0:T(8,128)(2,1)S(1)} collective-permute-done((bf16[384,1024]{1,0:T(8,128)(2,1)S(1)}, bf16[384,1024]{1,0:T(8,128)(2,1)S(1)}, u32[]{:S(2)}, u32[]{:S(2)}) %collective-permute-start.56) | collective-permute-done | bytes 786464 | tf_op jit(solution)/shard_map/ppermute | solution.py:584
  504.7 8.5 %collective-permute-done.58 = bf16[384,1024]{1,0:T(8,128)(2,1)} collective-permute-done((bf16[384,1024]{1,0:T(8,128)(2,1)}, bf16[384,1024]{1,0:T(8,128)(2,1)}, u32[]{:S(2)}, u32[]{:S(2)}) %collective-permute-start.58) | collective-permute-done | bytes 786464 | tf_op jit(solution)/shard_map/ppermute | solution.py:584
  541.7 19.5 %collective-permute-done.69 = f32[8,19,128]{2,1,0:T(8,128)S(1)} collective-permute-done((f32[8,19,128]{2,1,0:T(8,128)S(1)}, f32[8,19,128]{2,1,0:T(8,128)S(1)}, u32[]{:S(2)}, u32[]{:S(2)}) %collective-permute-start.69) | collective-permute-done | bytes 77856 | tf_op jit(solution)/shard_map/ppermute | solution.py:874
  577.9 13.8 %all-reduce.10.cloned.1.call-done = bf16[4096,128]{1,0:T(8,128)(2,1)} async-done(((bf16[4096,128]{1,0:T(8,128)(2,1)}), bf16[4096,128]{1,0:T(8,128)(2,1)}) %all-reduce.10.cloned.1.call-update) | async-done | bytes 1048592 | tf_op jit(solution)/shard_map/psum | solution.py:753
  (441 shorter events, 273.7 us)
Async XLA Ops:
  7.2 71.3 %all-gather.6.cloned.1.call-start = ((), (), s32[]{:S(2)}) async-start(), calls=%async_computation.6 | async-start | bytes 3932160 | tf_op jit(solution)/shard_map/all_gather | solution.py:652
  7.9 114.4 %all-gather.4.cloned.1.call-start = ((), (), s32[]{:S(2)}) async-start(), calls=%async_computation.1 | async-start | bytes 1310720 | tf_op jit(solution)/shard_map/all_gather | solution.py:655
  35.8 37.2 %collective-permute-start.9 = (bf16[1024,640]{1,0:T(8,128)(2,1)S(1)}, bf16[1024,640]{1,0:T(8,128)(2,1)}, u32[]{:S(2)}, u32[]{:S(2)}) collective-permute-start(bf16[1024,640]{1,0:T(8,128)(2,1)S(1)} %pad_maximum_fusion.refs_0_), channel_id=1, source_target_pairs={{0,2},{1,3},{2,0},{3,1},{4,6},{5,7},{6,4},{7,5},{8,10},{9,11},{10,... | collective-permute-start | bytes 3932168 | tf_op jit(solution)/shard_map/ppermute | solution.py:212
  37.4 35.7 %collective-permute-start.10 = (bf16[1024,640]{1,0:T(8,128)(2,1)S(1)}, bf16[1024,640]{1,0:T(8,128)(2,1)}, u32[]{:S(2)}, u32[]{:S(2)}) collective-permute-start(bf16[1024,640]{1,0:T(8,128)(2,1)S(1)} %pad_maximum_fusion.refs_0_), channel_id=1, source_target_pairs={{0,4},{1,5},{2,6},{3,7},{4,0},{5,1},{6,2},{7,3},{8,12},{9,13},{10,... | collective-permute-start | bytes 3932168 | tf_op jit(solution)/shard_map/ppermute | solution.py:212
  93.7 281.1 %reduce-scatter.2.cloned.1.call-start = ((), (), s32[]{:S(2)}) async-start(), calls=%async_computation.2 | async-start | bytes 1310720 | tf_op jit(solution)/shard_map/reduce_scatter | solution.py:815
  95.4 25.4 %collective-permute-start.18 = (bf16[1024,512]{1,0:T(8,128)(2,1)}, bf16[1024,512]{1,0:T(8,128)(2,1)S(1)}, u32[]{:S(2)}, u32[]{:S(2)}) collective-permute-start(bf16[1024,512]{1,0:T(8,128)(2,1)} %refs_0_), channel_id=1, source_target_pairs={{0,2},{1,3},{2,0},{3,1},{4,6},{5,7},{6,4},{7,5},{8,10},{9,11},{10,... | collective-permute-start | bytes 3145736 | tf_op jit(solution)/shard_map/ppermute | solution.py:212
  96.6 25.5 %collective-permute-start.19 = (bf16[1024,512]{1,0:T(8,128)(2,1)}, bf16[1024,512]{1,0:T(8,128)(2,1)}, u32[]{:S(2)}, u32[]{:S(2)}) collective-permute-start(bf16[1024,512]{1,0:T(8,128)(2,1)} %refs_0_), channel_id=1, source_target_pairs={{0,4},{1,5},{2,6},{3,7},{4,0},{5,1},{6,2},{7,3},{8,12},{9,13},{10,... | collective-permute-start | bytes 3145736 | tf_op jit(solution)/shard_map/ppermute | solution.py:212
  147.6 25.1 %collective-permute-start.22 = (bf16[4096,128]{1,0:T(8,128)(2,1)S(1)}, bf16[4096,128]{1,0:T(8,128)(2,1)S(1)}, u32[]{:S(2)}, u32[]{:S(2)}) collective-permute-start(bf16[4096,128]{1,0:T(8,128)(2,1)S(1)} %copy-done.36), channel_id=1, source_target_pairs={{0,2},{1,3},{2,0},{3,1},{4,6},{5,7},{6,4},{7,5},{8,10},{9,11},{10,... | collective-permute-start | bytes 3145736 | tf_op jit(solution)/shard_map/ppermute | solution.py:212
  236.5 25.4 %collective-permute-start.37 = (bf16[2,2048,128]{2,1,0:T(8,128)(2,1)}, bf16[2,2048,128]{2,1,0:T(8,128)(2,1)S(1)}, u32[]{:S(2)}, u32[]{:S(2)}) collective-permute-start(bf16[2,2048,128]{2,1,0:T(8,128)(2,1)} %get-tuple-element.409), channel_id=1, source_target_pairs={{0,2},{1,3},{2,0},{3,1},{4,6},{5,7},{6,4},{7,5},{8,10},{9,11},{10,... | collective-permute-start | bytes 3145736 | tf_op jit(solution)/shard_map/ppermute | solution.py:212
  237.1 25.1 %collective-permute-start.38 = (bf16[2,2048,128]{2,1,0:T(8,128)(2,1)}, bf16[2,2048,128]{2,1,0:T(8,128)(2,1)S(1)}, u32[]{:S(2)}, u32[]{:S(2)}) collective-permute-start(bf16[2,2048,128]{2,1,0:T(8,128)(2,1)} %get-tuple-element.408), channel_id=1, source_target_pairs={{0,4},{1,5},{2,6},{3,7},{4,0},{5,1},{6,2},{7,3},{8,12},{9,13},{10,... | collective-permute-start | bytes 3145736 | tf_op jit(solution)/shard_map/ppermute | solution.py:212
  263.2 25.7 %collective-permute-start.41 = (bf16[4,4096,128]{2,1,0:T(8,128)(2,1)}, bf16[4,4096,128]{2,1,0:T(8,128)(2,1)}, u32[]{:S(2)}, u32[]{:S(2)}) collective-permute-start(bf16[4,4096,128]{2,1,0:T(8,128)(2,1)} %get-tuple-element.292), channel_id=1, source_target_pairs={{0,1},{1,0},{2,3},{3,2},{4,5},{5,4},{6,7},{7,6},{8,9},{9,8},{10,11... | collective-permute-start | bytes 12582920 | tf_op jit(solution)/shard_map/ppermute | solution.py:212
  292.7 25.2 %collective-permute-start.43 = (bf16[2,2048,128]{2,1,0:T(8,128)(2,1)}, bf16[2,2048,128]{2,1,0:T(8,128)(2,1)}, u32[]{:S(2)}, u32[]{:S(2)}) collective-permute-start(bf16[2,2048,128]{2,1,0:T(8,128)(2,1)} %get-tuple-element.403), channel_id=1, source_target_pairs={{0,2},{1,3},{2,0},{3,1},{4,6},{5,7},{6,4},{7,5},{8,10},{9,11},{10,... | collective-permute-start | bytes 3145736 | tf_op jit(solution)/shard_map/ppermute | solution.py:212
  293.4 24.9 %collective-permute-start.44 = (bf16[2,2048,128]{2,1,0:T(8,128)(2,1)}, bf16[2,2048,128]{2,1,0:T(8,128)(2,1)}, u32[]{:S(2)}, u32[]{:S(2)}) collective-permute-start(bf16[2,2048,128]{2,1,0:T(8,128)(2,1)} %get-tuple-element.402), channel_id=1, source_target_pairs={{0,4},{1,5},{2,6},{3,7},{4,0},{5,1},{6,2},{7,3},{8,12},{9,13},{10,... | collective-permute-start | bytes 3145736 | tf_op jit(solution)/shard_map/ppermute | solution.py:212
  333.6 100.5 %all-reduce.6.cloned.1.call-start = ((), (), s32[]{:S(2)}) async-start(), calls=%async_computation.3 | async-start | bytes 2097152 | tf_op jit(solution)/shard_map/psum | solution.py:753
  346.3 28.4 %collective-permute-start.50 = (bf16[2,2048,128]{2,1,0:T(8,128)(2,1)}, bf16[2,2048,128]{2,1,0:T(8,128)(2,1)}, u32[]{:S(2)}, u32[]{:S(2)}) collective-permute-start(bf16[2,2048,128]{2,1,0:T(8,128)(2,1)} %get-tuple-element.397), channel_id=1, source_target_pairs={{0,2},{1,3},{2,0},{3,1},{4,6},{5,7},{6,4},{7,5},{8,10},{9,11},{10,... | collective-permute-start | bytes 3145736 | tf_op jit(solution)/shard_map/ppermute | solution.py:212
  347.5 27.3 %collective-permute-start.51 = (bf16[2,2048,128]{2,1,0:T(8,128)(2,1)}, bf16[2,2048,128]{2,1,0:T(8,128)(2,1)}, u32[]{:S(2)}, u32[]{:S(2)}) collective-permute-start(bf16[2,2048,128]{2,1,0:T(8,128)(2,1)} %get-tuple-element.396), channel_id=1, source_target_pairs={{0,4},{1,5},{2,6},{3,7},{4,0},{5,1},{6,2},{7,3},{8,12},{9,13},{10,... | collective-permute-start | bytes 3145736 | tf_op jit(solution)/shard_map/ppermute | solution.py:212
  382.8 133.8 %all-reduce.8.cloned.1.call-start = ((), (), s32[]{:S(2)}) async-start(), calls=%async_computation.4 | async-start | bytes 2097152 | tf_op jit(solution)/shard_map/psum | solution.py:753
  440.3 151.4 %all-reduce.10.cloned.1.call-start = ((), (), s32[]{:S(2)}) async-start(), calls=%async_computation.5 | async-start | bytes 2097152 | tf_op jit(solution)/shard_map/psum | solution.py:753
  456.2 38.5 %collective-permute-start.62 = (bf16[2,2048,128]{2,1,0:T(8,128)(2,1)S(1)}, bf16[2,2048,128]{2,1,0:T(8,128)(2,1)S(1)}, u32[]{:S(2)}, u32[]{:S(2)}) collective-permute-start(bf16[2,2048,128]{2,1,0:T(8,128)(2,1)S(1)} %get-tuple-element.391), channel_id=1, source_target_pairs={{0,2},{1,3},{2,0},{3,1},{4,6},{5,7},{6,4},{7,5},{8,10},{9,11},{10,... | collective-permute-start | bytes 3145736 | tf_op jit(solution)/shard_map/ppermute | solution.py:212
  457.7 37.0 %collective-permute-start.63 = (bf16[2,2048,128]{2,1,0:T(8,128)(2,1)S(1)}, bf16[2,2048,128]{2,1,0:T(8,128)(2,1)S(1)}, u32[]{:S(2)}, u32[]{:S(2)}) collective-permute-start(bf16[2,2048,128]{2,1,0:T(8,128)(2,1)S(1)} %get-tuple-element.390), channel_id=1, source_target_pairs={{0,4},{1,5},{2,6},{3,7},{4,0},{5,1},{6,2},{7,3},{8,12},{9,13},{10,... | collective-permute-start | bytes 3145736 | tf_op jit(solution)/shard_map/ppermute | solution.py:212
  459.3 26.6 %collective-permute-start.56 = (bf16[384,1024]{1,0:T(8,128)(2,1)S(1)}, bf16[384,1024]{1,0:T(8,128)(2,1)S(1)}, u32[]{:S(2)}, u32[]{:S(2)}) collective-permute-start(bf16[384,1024]{1,0:T(8,128)(2,1)S(1)} %get-tuple-element.415), channel_id=1, source_target_pairs={{0,8},{1,9},{2,10},{3,11},{4,12},{5,13},{6,14},{7,15}} | collective-permute-start | bytes 2359304 | tf_op jit(solution)/shard_map/ppermute | solution.py:584
  487.8 25.4 %collective-permute-start.58 = (bf16[384,1024]{1,0:T(8,128)(2,1)}, bf16[384,1024]{1,0:T(8,128)(2,1)}, u32[]{:S(2)}, u32[]{:S(2)}) collective-permute-start(bf16[384,1024]{1,0:T(8,128)(2,1)} %get-tuple-element.413), channel_id=1, source_target_pairs={{0,8},{8,16},{1,9},{9,17},{2,10},{10,18},{3,11},{11,19},{4,12},{12... | collective-permute-start | bytes 2359304 | tf_op jit(solution)/shard_map/ppermute | solution.py:584
  520.4 53.3 %collective-permute-start.61 = (bf16[384,1024]{1,0:T(8,128)(2,1)}, bf16[384,1024]{1,0:T(8,128)(2,1)}, u32[]{:S(2)}, u32[]{:S(2)}) collective-permute-start(bf16[384,1024]{1,0:T(8,128)(2,1)} %get-tuple-element.411), channel_id=1, source_target_pairs={{8,0},{16,8},{24,16},{9,1},{17,9},{25,17},{10,2},{18,10},{26,18},{... | collective-permute-start | bytes 2359304 | tf_op jit(solution)/shard_map/ppermute | solution.py:584
  521.8 51.9 %collective-permute-start.60 = (bf16[384,1024]{1,0:T(8,128)(2,1)}, bf16[384,1024]{1,0:T(8,128)(2,1)}, u32[]{:S(2)}, u32[]{:S(2)}) collective-permute-start(bf16[384,1024]{1,0:T(8,128)(2,1)} %get-tuple-element.410), channel_id=1, source_target_pairs={{0,8},{8,16},{16,24},{1,9},{9,17},{17,25},{2,10},{10,18},{18,26},{... | collective-permute-start | bytes 2359304 | tf_op jit(solution)/shard_map/ppermute | solution.py:584
  (134 other events, 1398.3 us)
Sparse Core Ops, SparseCore 0:
  9.6 66.1 all-gather.5
  93.8 28.4 all-gather.3
  333.7 30.3 reduce-scatter.1
  382.9 51.0 all-reduce.5
  440.4 61.3 all-reduce.7
  528.0 63.6 all-reduce.9
